TPU v7x, 512 devices: a whole 4x4x16 slice. The times are simulated.
512 devices in a mesh: prefix: 8 (over y, core), branch: 16 (over z), tensor: 4 (over x).
Axes of the slice: x: 4, y: 4, z: 16, core: 2. Of those that a mesh axis runs over, the one named last changes fastest.
Arguments:
- prompt_x: bfloat16 [2048, 16, 4, 128], P('prefix', 'branch', 'tensor'), may hold values from -6 to 6
- prompt_bc: bfloat16 [2048, 4, 256], P('prefix', 'tensor'), may hold values from -6 to 6
- prompt_dt: float32 [16, 4, 2, 2048], P('branch', 'tensor', None, 'prefix'), may hold values from -4 to 4
- branch_x: bfloat16 [16, 1024, 16, 4, 128], P('branch', 'prefix', None, 'tensor'), may hold values from -6 to 6
- branch_bc: bfloat16 [16, 1024, 4, 256], P('branch', 'prefix', 'tensor'), may hold values from -6 to 6
- branch_dt: float32 [16, 16, 4, 2, 1024], P('branch', None, 'tensor', None, 'prefix'), may hold values from -4 to 4
- conv_x: float32 [4, 16, 4, 128], P(None, None, 'tensor'), may hold values from -3 to 3
- conv_bc: float32 [4, 4, 256], P(None, 'tensor'), may hold values from -3 to 3
- a_log: float32 [16, 4, 2], P(None, 'tensor'), may hold values from -4 to 1.5
- dt_bias: float32 [16, 4, 2], P(None, 'tensor'), may hold values from -6 to -2
- d_skip: float32 [16, 4, 2], P(None, 'tensor'), may hold values from 0.5 to 1.5
- lengths: int32 [16], replicated, may hold values from 1 to 1024, 8192 in all
- forks: int32 [16], replicated, may hold values from 1 to 2048
- holder: int32 [16], replicated, may hold values from 0 to 1023, as said below
- prompt_dy: bfloat16 [2048, 16, 4, 128], P('prefix', 'branch', 'tensor'), may hold values from -6 to 6
- branch_dy: bfloat16 [16, 1024, 16, 4, 128], P('branch', 'prefix', None, 'tensor'), may hold values from -6 to 6
Outputs:
- prompt_y: bfloat16 [2048, 16, 4, 128], P('prefix', 'branch', 'tensor')
- branch_y: bfloat16 [16, 1024, 16, 4, 128], P('branch', 'prefix', None, 'tensor')
- prompt_gx: bfloat16 [2048, 16, 4, 128], P('prefix', 'branch', 'tensor')
- branch_gx: bfloat16 [16, 1024, 16, 4, 128], P('branch', 'prefix', None, 'tensor')
- prompt_gbc: bfloat16 [2048, 4, 256], P(('prefix', 'branch'), 'tensor')
Inputs may be any that keep to these rules, and one draw needn't show every extreme that they name: `holder`: the keys are distinct.
All inputs are finite; a program needn't handle non-finite values.
Results may differ from a plain program's by a relative error of at most 0.002.
Values sent between devices are 32-bit elements; how exact they have to be, the bound alone decides.
No kernel may reach another device: no remote copies, remote signals or barrier semaphores. Data moves between devices by JAX's collectives and lax.ppermute only.
A program may use at most 192 MiB of HBM per device.

v0:
```python
import functools

import jax
import jax.numpy as jnp
from jax import lax
from jax.experimental import pallas as pl
from jax.experimental.pallas import tpu as pltpu
from jax.sharding import PartitionSpec as P

HEAD_DIM = 64
STATE = 128
LANES = 128

F32 = jnp.float32
BF16 = jnp.bfloat16

TAIL_X = 0
TAIL_BC = 48
ROW_X = 54
ROW_DY = 102
ROW_BC = 150
ROW_STEP = 160
ROW_LOG = 168
EARLY = 176

VMEM_LIMIT = 56 * 1024 * 1024


def split2(a):
    hi = a.astype(BF16)
    return hi, (a - hi.astype(F32)).astype(BF16)


def split3(a):
    hi = a.astype(BF16)
    rest = a - hi.astype(F32)
    mid = rest.astype(BF16)
    return hi, mid, (rest - mid.astype(F32)).astype(BF16)


def mm(a, b):
    return lax.dot_general(a, b, (((1,), (0,)), ((), ())), preferred_element_type=F32)


def mm_nt(a, b):
    return lax.dot_general(a, b, (((1,), (1,)), ((), ())), preferred_element_type=F32)


def left(a):
    hi, lo = split2(a)
    return jnp.concatenate([hi, hi, lo], axis=1)


def right(b):
    hi, lo = split2(b)
    return jnp.concatenate([hi, lo, hi], axis=0)


def right_nt(b):
    hi, lo = split2(b)
    return jnp.concatenate([hi, lo, hi], axis=1)


def exact(a):
    return jnp.concatenate(split3(a), axis=1)


def iota(shape, dim):
    return lax.broadcasted_iota(jnp.int32, shape, dim)


def picker(base, j):
    one = (iota((LANES, LANES), 0) == base + 2 * j + iota((LANES, LANES), 1) // HEAD_DIM).astype(
        F32
    ).astype(BF16)
    return jnp.concatenate([one, one, one], axis=0)


def running_sum(logs):
    size = logs.shape[1]
    upper = (iota((size, size), 0) <= iota((size, size), 1)).astype(F32).astype(BF16)
    return mm(exact(logs), jnp.concatenate([upper, upper, upper], axis=0))


def block(j):
    return pl.ds(pl.multiple_of(j * LANES, LANES), LANES)


def sigmoid(x):
    return 1.0 / (1.0 + jnp.exp(-x))


def conv_branch(bx, rim, convx, xs, xt, ds):
    js = bx.shape[1]
    for r in range(3):
        xs[(5 + r) * js : (6 + r) * js, :] = rim[r, 0:js, :]

    def fill(c, _):
        xs[pl.ds(pl.multiple_of(8 * js + c * 16 * js, 16 * js), 16 * js), :] = (
            bx[pl.ds(c * 16, 16)].astype(F32).reshape(16 * js, LANES)
        )
        return 0

    lax.fori_loop(0, bx.shape[0] // 16, fill, 0)

    def one(c, _):
        pre = jnp.zeros((16, js, LANES), F32)
        for i in range(4):
            start = pl.multiple_of((5 + i) * js + c * 16 * js, js)
            pre = pre + convx[i][None] * xs[pl.ds(start, 16 * js), :].reshape(16, js, LANES)
        sg = sigmoid(pre)
        at = pl.ds(pl.multiple_of(c * 16 * js, 16 * js), 16 * js)
        xt[at, :] = (pre * sg).reshape(16 * js, LANES)
        if ds is not None:
            ds[at, :] = (sg * (1.0 + pre * (1.0 - sg))).reshape(16 * js, LANES)
        return 0

    lax.fori_loop(0, bx.shape[0] // 16, one, 0)


def conv_rows(raw, halo_rows, taps, scratch):
    n = raw.shape[0]
    scratch[8 : 8 + n, :] = raw.astype(F32)
    for r in range(3):
        scratch[5 + r : 6 + r, :] = halo_rows[r]
    pre = jnp.zeros(raw.shape, F32)
    for i in range(4):
        pre = pre + taps[i] * scratch[5 + i : 5 + i + n, :]
    return pre


def bc_halo(rim, first):
    return [
        jnp.concatenate([rim[r, first : first + 1, :], rim[r, first + 1 : first + 2, :]], axis=1)
        for r in range(3)
    ]


def silu(x):
    return x * sigmoid(x)


def silu_slope(x):
    sg = sigmoid(x)
    return sg * (1.0 + x * (1.0 - sg))


def branch_table(step, run):
    return jnp.concatenate([step, run, jnp.zeros((64, LANES), F32)], axis=0).T


def prompt_table(step, run):
    n = step.shape[1]
    r = iota((LANES, n), 0)
    runs = jnp.where(r % 2 == 0, run[0:1], run[1:2])
    steps = jnp.where(r % 2 == 0, step[0:1], step[1:2])
    return jnp.where((r == 2) | (r == 3), steps, runs).T


def halves(first, second, shape):
    return jnp.where(iota(shape, 1) < HEAD_DIM, first, second)


def local_kernel(
    scal, px, pbc, pstep, plogs, pdy, bx, bbc, bstep, blogs, bdy, rim, convx, convbc,
    out, xs, xt, dys, bcs, pxs, pbcs, wexp, tab,
):
    row, col, length = scal[17], scal[18], scal[16]
    n, js = bx.shape[0], bx.shape[1]
    span = px.shape[0]
    conv_branch(bx, rim, convx, xs, xt, None)

    def fill(c, _):
        pos = row * n + c * 16 + iota((16, js, LANES), 0)
        dead = (pos >= length) | (pos < 3)
        dys[pl.ds(pl.multiple_of(c * 16 * js, 16 * js), 16 * js), :] = jnp.where(
            dead, 0.0, bdy[pl.ds(c * 16, 16)].astype(F32)
        ).reshape(16 * js, LANES)
        return 0

    lax.fori_loop(0, n // 16, fill, 0)
    taps = [convbc[i : i + 1, :] for i in range(4)]
    bc = silu(conv_rows(bbc[...], bc_halo(rim, 19), taps, bcs))
    b_t = left(bc[:, :STATE].T)
    c_t = left(bc[:, STATE:].T)
    table = branch_table(bstep[...], running_sum(blogs[...]))
    parts = exact(table)

    def head_pair(j, _):
        at = pl.ds(j, n, stride=js)
        steps = mm(parts, picker(0, j))
        runs = mm(parts, picker(32, j))
        x_w = xt[at, :] * steps * jnp.exp(runs[n - 1 : n, :] - runs)
        out[:, block(j)] = mm(b_t, right(x_w))
        out[:, block(js + j)] = mm(c_t, right(dys[at, :] * jnp.exp(runs)))
        return 0

    lax.fori_loop(0, js, head_pair, 0)

    own = [convx[i, pl.ds(col, 1), :] for i in range(4)]
    x_p = silu(conv_rows(px[...], [rim[r, 16:17, :] for r in range(3)], own, pxs))
    bc_p = silu(conv_rows(pbc[...], bc_halo(rim, 17), taps, pbcs))
    b_pt = left(bc_p[:, :STATE].T)
    c_pt = left(bc_p[:, STATE:].T)
    ptable = prompt_table(pstep[...], running_sum(plogs[...]))
    tab[...] = ptable
    runs = halves(ptable[:, 0:1], ptable[:, 1:2], (span, LANES))
    steps = halves(ptable[:, 2:3], ptable[:, 3:4], (span, LANES))
    wexp[...] = runs
    x_hat = x_p * steps
    base = 3 * js * LANES
    out[:, base : base + LANES] = mm(b_pt, right(x_hat * jnp.exp(runs[span - 1 : span, :] - runs)))
    out[:, base + LANES : base + 2 * LANES] = mm(
        c_pt, right(pdy[...].astype(F32) * jnp.exp(runs))
    )
    lane = iota((1, LANES), 1)
    pxs[0:span, :] = x_hat

    def fork(g, acc):
        where = scal[g] - 1 - row * span
        inside = (where >= 0) & (where < span)

        @pl.when(inside)
        def _():
            w = wexp[...]
            gap = wexp[pl.ds(where, 1), :] - w
            upto = iota((span, LANES), 0) <= where
            u = jnp.exp(jnp.where(upto, gap, -1e30)) * pxs[0:span, :]
            out[:, block(2 * js + g)] = mm(b_pt, right(u))

        @pl.when(jnp.logical_not(inside))
        def _():
            out[:, block(2 * js + g)] = jnp.zeros((STATE, LANES), F32)

        safe = jnp.clip(where, 0, span - 1)
        return jnp.where(lane // 2 == 32 + g, tab[pl.ds(safe, 1), :], acc)

    marks = lax.fori_loop(0, js, fork, jnp.zeros((1, LANES), F32))
    misc = jnp.where(lane < 2, ptable[span - 1 : span, :], marks)
    misc = jnp.where((lane >= 32) & (lane < 64), table[n - 1 : n, :], misc)
    out[:, base + 2 * LANES : base + 3 * LANES] = jnp.broadcast_to(misc, (STATE, LANES))


def slice_kernel(scal, got, early, convbc, msg, aft, adj, pst, cols, mat, turned):
    row = scal[17]
    count, ns = got.shape[0], got.shape[1]
    js = msg.shape[0]
    span = scal[19]
    for half in range(2):
        seq = [
            jnp.sum(early[:, TAIL_BC + 2 * r + half, :], axis=0, keepdims=True) for r in range(3)
        ] + [early[0, ROW_BC + 2 * s + half : ROW_BC + 2 * s + half + 1, :] for s in range(3)]
        taps = [convbc[i : i + 1, half * STATE : (half + 1) * STATE] for i in range(4)]
        mat[...] = jnp.zeros((LANES, LANES), F32)
        for s in range(3):
            mat[s : s + 1, :] = sum(taps[i] * seq[s + i] for i in range(4))
        for i in range(4):
            mat[8 + i : 9 + i, :] = taps[i]
        turned[half * STATE : (half + 1) * STATE, :] = mat[...].T
    start = pl.multiple_of(row * ns, 16)
    b_col = turned[pl.ds(start, ns), :]
    c_col = turned[pl.ds(STATE + start, ns), :]
    cols[0:ns, :] = b_col
    cols[ns : 2 * ns, :] = c_col
    c_all = silu(c_col)
    misc = got[:, 0, (3 * js + 2) * LANES : (3 * js + 3) * LANES]
    misc_parts = exact(misc)
    log_parts = exact(early[0, ROW_LOG : ROW_LOG + 8, :])
    for j in range(js):
        at = slice(j * LANES, (j + 1) * LANES)
        lead = slice((js + j) * LANES, (js + j + 1) * LANES)
        fall = jnp.exp(mm(misc_parts, picker(32, j)))
        falls = jnp.exp(mm(log_parts, picker(0, j)))
        a = jnp.zeros((ns, LANES), F32)
        for p in reversed(range(count)):
            aft[p, :, at] = a
            a = fall[p : p + 1] * a + got[p, :, lead]
        for s in (2, 1, 0):
            dy = early[0, ROW_DY + s * js + j : ROW_DY + s * js + j + 1, :]
            a = a + dy * c_all[:, s : s + 1]
            adj[s, :, at] = a
            a = falls[s : s + 1] * a
        msg[j, 0:ns, LANES : 2 * LANES] = a
    pfall = jnp.exp(halves(misc[:, 0:1], misc[:, 1:2], (count, LANES)))
    base = 3 * js * LANES
    state = jnp.zeros((ns, LANES), F32)
    for p in range(count):
        pst[p] = state
        state = pfall[p : p + 1] * state + got[p, :, base : base + LANES]
    for g in range(js):
        holder = lax.div(scal[g] - 1, span)
        mark = got[holder, 0:1, base + 2 * LANES : base + 3 * LANES]
        reach = jnp.exp(
            halves(mark[:, 64 + 2 * g : 65 + 2 * g], mark[:, 65 + 2 * g : 66 + 2 * g], (1, LANES))
        )
        at = slice((2 * js + g) * LANES, (2 * js + g + 1) * LANES)
        msg[g, 0:ns, 0:LANES] = got[holder, :, at] + reach * pst[holder]
        msg[g, ns : ns + 8, :] = jnp.zeros((8, 2 * LANES), F32)
        for r in range(3):
            msg[g, ns + r : ns + r + 1, 0:LANES] = jnp.sum(
                early[:, TAIL_X + 3 * g + r, :], axis=0, keepdims=True
            )


def chain_kernel(
    scal, got, early, moved, aft, adj, pst, cols, convx, skip, msg, rows, injected
):
    row = scal[17]
    first = (row == 0).astype(F32)
    count, ns = got.shape[0], got.shape[1]
    js = moved.shape[0]
    span = scal[19]
    b_col, c_col = cols[0:ns, :], cols[ns : 2 * ns, :]
    b_all, c_all = silu(b_col), silu(c_col)
    base = 3 * js * LANES
    misc = got[:, 0, base + 2 * LANES : base + 3 * LANES]
    misc_parts = exact(misc)
    log_parts = exact(early[0, ROW_LOG : ROW_LOG + 8, :])
    step_parts = exact(early[0, ROW_STEP : ROW_STEP + 8, :])
    sum_b = [jnp.zeros((ns, LANES), F32) for _ in range(3)]
    sum_c = [jnp.zeros((ns, LANES), F32) for _ in range(3)]
    for j in range(js):
        at = slice(j * LANES, (j + 1) * LANES)
        fall = jnp.exp(mm(misc_parts, picker(32, j)))
        falls = jnp.exp(mm(log_parts, picker(0, j)))
        steps = mm(step_parts, picker(0, j))
        seq = [moved[j, ns + r : ns + r + 1, 0:LANES] for r in range(3)] + [
            early[0, ROW_X + s * js + j : ROW_X + s * js + j + 1, :] for s in range(3)
        ]
        gain = skip[j : j + 1, :] * first
        state = moved[j, 0:ns, 0:LANES]
        for s in range(3):
            dy = early[0, ROW_DY + s * js + j : ROW_DY + s * js + j + 1, :]
            pre = sum(convx[i, j : j + 1, :] * seq[s + i] for i in range(4))
            sg = sigmoid(pre)
            x_conv = pre * sg
            x_hat = steps[s : s + 1] * x_conv
            state = falls[s : s + 1] * state + x_hat * b_all[:, s : s + 1]
            a = adj[s, :, at]
            rows[j : j + 1, s * LANES : (s + 1) * LANES] = (
                jnp.sum(state * c_all[:, s : s + 1], axis=0, keepdims=True) + gain * x_conv
            )
            grad = steps[s : s + 1] * jnp.sum(a * b_all[:, s : s + 1], axis=0, keepdims=True)
            rows[j : j + 1, (3 + s) * LANES : (4 + s) * LANES] = (
                sg * (1.0 + pre * (1.0 - sg)) * (grad + gain * dy)
            )
            sum_c[s] = sum_c[s] + dy * state
            sum_b[s] = sum_b[s] + x_hat * a
        for p in range(count):
            msg[p, :, at] = state
            state = fall[p : p + 1] * state + got[p, :, at]
            msg[p, :, (js + j) * LANES : (js + j + 1) * LANES] = aft[p, :, at]
    lane = iota((ns, LANES), 1)
    back = jnp.zeros((ns, LANES), F32)
    for which, (total, column) in enumerate(((sum_b, b_col), (sum_c, c_col))):
        grads = [
            jnp.sum(total[s], axis=1, keepdims=True) * silu_slope(column[:, s : s + 1])
            for s in range(3)
        ]
        for m in range(3):
            tail = sum(grads[s] * column[:, 8 + m - s : 9 + m - s] for s in range(m + 1))
            back = jnp.where(lane == 3 * which + m, tail, back)
    pfall = jnp.exp(halves(misc[:, 0:1], misc[:, 1:2], (count, LANES)))
    injected[...] = jnp.zeros(injected.shape, F32)
    for g in range(js):
        holder = lax.div(scal[g] - 1, span)
        mark = got[holder, 0:1, base + 2 * LANES : base + 3 * LANES]
        reach = jnp.exp(
            halves(mark[:, 64 + 2 * g : 65 + 2 * g], mark[:, 65 + 2 * g : 66 + 2 * g], (1, LANES))
        )
        grad = moved[g, 0:ns, LANES : 2 * LANES]
        injected[holder] = injected[holder] + reach * grad
        for p in range(count):
            msg[p, :, (2 * js + g) * LANES : (2 * js + g + 1) * LANES] = grad
    a = jnp.zeros((ns, LANES), F32)
    for p in reversed(range(count)):
        msg[p, :, base + LANES : base + 2 * LANES] = a
        a = pfall[p : p + 1] * a + got[p, :, base + LANES : base + 2 * LANES] + injected[p]
    for p in range(count):
        msg[p, :, base : base + LANES] = pst[p]
        msg[p, :, base + 2 * LANES : base + 8 * LANES] = rows[...]
        msg[p, :, base + 8 * LANES : base + 9 * LANES] = back


def tail_grads(lead, taps):
    return [sum(lead[s] * taps[m - s] for s in range(m + 1)) for m in range(3)]


def final_kernel(
    scal, px, pbc, pstep, plogs, pdy, bx, bbc, bstep, blogs, bdy, rim, convx, convbc, skip, got,
    by, bgx, last, py, pgx, gbc, rims, forks,
    xs, xt, ds, dys, bcs, pxs, pbcs, wexp, wrow, pwrow, ys, rows, dxh, dbs,
):
    row, col, length = scal[17], scal[18], scal[16]
    n, js = bx.shape[0], bx.shape[1]
    span = px.shape[0]
    conv_branch(bx, rim, convx, xs, xt, ds)
    is_first = row == 0

    def fill(c, _):
        pos = row * n + c * 16 + iota((16, js, LANES), 0)
        dead = (pos >= length) | (pos < 3)
        dys[pl.ds(pl.multiple_of(c * 16 * js, 16 * js), 16 * js), :] = jnp.where(
            dead, 0.0, bdy[pl.ds(c * 16, 16)].astype(F32)
        ).reshape(16 * js, LANES)
        return 0

    lax.fori_loop(0, n // 16, fill, 0)
    base = 3 * js * LANES
    sums = got[0:js, base + 2 * LANES : base + 8 * LANES]
    for p in range(1, STATE // js):
        sums = sums + got[p * js : (p + 1) * js, base + 2 * LANES : base + 8 * LANES]
    rows[...] = sums
    taps = [convbc[i : i + 1, :] for i in range(4)]
    bc = silu(conv_rows(bbc[...], bc_halo(rim, 19), taps, bcs))
    b, c = bc[:, :STATE], bc[:, STATE:]
    b_l, c_l = left(b), left(c)
    scores = mm_nt(c_l, right_nt(b))
    scores_t = mm_nt(b_l, right_nt(c))
    run = running_sum(blogs[...])
    wrow[...] = run
    parts = exact(branch_table(bstep[...], run))
    causal = iota((n, n), 0) >= iota((n, n), 1)
    causal_t = iota((n, n), 0) <= iota((n, n), 1)
    low = iota((n, LANES), 1) < HEAD_DIM
    xs[n * js : (n + 8) * js, :] = jnp.zeros((8 * js, LANES), F32)

    def head_pair(j, _):
        at = pl.ds(j, n, stride=js)
        steps = mm(parts, picker(0, j))
        runs = mm(parts, picker(32, j))
        x_conv = xt[at, :]
        dy = dys[at, :]
        gain = skip[pl.ds(j, 1), :]
        x_hat = x_conv * steps
        x_hi, x_lo = split2(x_hat)
        dy_b = dy.astype(BF16)
        zero = jnp.zeros_like(dy_b)
        mix, mix_t = [], []
        for k in range(2):
            down = jnp.broadcast_to(runs[:, k * HEAD_DIM : k * HEAD_DIM + 1], (n, n))
            along = wrow[pl.ds(2 * j + k, 1), :]
            mix.append(split2(jnp.exp(jnp.where(causal, down - along, -1e30)) * scores))
            mix_t.append(split2(jnp.exp(jnp.where(causal_t, along - down, -1e30)) * scores_t))
        x_blk = [jnp.where(low, x_hi, zero), jnp.where(low, zero, x_hi)]
        x_rest = [jnp.where(low, x_lo, zero), jnp.where(low, zero, x_lo)]
        d_blk = [jnp.where(low, dy_b, zero), jnp.where(low, zero, dy_b)]
        y = mm(
            jnp.concatenate([mix[0][0], mix[1][0], mix[0][0], mix[1][0], mix[0][1], mix[1][1]], 1),
            jnp.concatenate(x_blk + x_rest + x_blk, 0),
        )
        y = y + jnp.exp(runs) * mm(c_l, right(got[:, block(j)]))
        ys[at, :] = y + gain * x_conv
        g = mm(
            jnp.concatenate([mix_t[0][0], mix_t[1][0], mix_t[0][1], mix_t[1][1]], 1),
            jnp.concatenate(d_blk + d_blk, 0),
        )
        g = g + jnp.exp(runs[n - 1 : n, :] - runs) * mm(b_l, right(got[:, block(js + j)]))
        xs[at, :] = (steps * g + gain * dy) * ds[at, :]
        return 0

    lax.fori_loop(0, js, head_pair, 0)

    @pl.when(is_first)
    def _():
        for s in range(3):
            ys[s * js : (s + 1) * js, :] = rows[:, s * LANES : (s + 1) * LANES]
            xs[s * js : (s + 1) * js, :] = rows[:, (3 + s) * LANES : (4 + s) * LANES]

    def finish(c, _):
        at = pl.multiple_of(c * 16 * js, 16 * js)
        pos = row * n + c * 16 + iota((16, js, LANES), 0)
        y = ys[pl.ds(at, 16 * js), :].reshape(16, js, LANES)
        by[pl.ds(c * 16, 16)] = jnp.where(pos < length, y, 0.0).astype(BF16)
        g = jnp.zeros((16, js, LANES), F32)
        for i in range(4):
            g = g + convx[i][None] * xs[pl.ds(at + (3 - i) * js, 16 * js), :].reshape(
                16, js, LANES
            )
        bgx[pl.ds(c * 16, 16)] = g.astype(BF16)
        return 0

    lax.fori_loop(0, n // 16, finish, 0)
    for m in range(3):
        at = n - 3 + m
        last[m] = sum(
            convx[i] * xs[(at + 3 - i) * js : (at + 4 - i) * js, :] for i in range(4)
        )
    taps_x = [convx[i] for i in range(4)]
    for m, g in enumerate(tail_grads([xs[s * js : (s + 1) * js, :] for s in range(3)], taps_x)):
        rims[m, 0:js, :] = g
    fork_lead = [rows[:, (3 + s) * LANES : (4 + s) * LANES] for s in range(3)]
    for m, g in enumerate(tail_grads(fork_lead, taps_x)):
        forks[m] = g

    own = [convx[i, pl.ds(col, 1), :] for i in range(4)]
    gain = skip[pl.ds(col, 1), :]
    x_pre = conv_rows(px[...], [rim[r, 16:17, :] for r in range(3)], own, pxs)
    bc_pre = conv_rows(pbc[...], bc_halo(rim, 17), taps, pbcs)
    x_p = silu(x_pre)
    bc_p = silu(bc_pre)
    b_p, c_p = bc_p[:, :STATE], bc_p[:, STATE:]
    b_l, c_l = left(b_p), left(c_p)
    scores = mm_nt(c_l, right_nt(b_p))
    scores_t = mm_nt(b_l, right_nt(c_p))
    prun = running_sum(plogs[...])
    ptable = prompt_table(pstep[...], prun)
    runs = halves(ptable[:, 0:1], ptable[:, 1:2], (span, LANES))
    steps = halves(ptable[:, 2:3], ptable[:, 3:4], (span, LANES))
    wexp[...] = runs
    x_hat = x_p * steps
    x_hi, x_lo = split2(x_hat)
    dy_b = pdy[...]
    dy = dy_b.astype(F32)
    low = iota((span, LANES), 1) < HEAD_DIM
    zero = jnp.zeros_like(x_hi)
    causal = iota((span, span), 0) >= iota((span, span), 1)
    causal_t = iota((span, span), 0) <= iota((span, span), 1)
    y = jnp.exp(runs) * mm(c_l, right(got[:, base : base + LANES])) + gain * x_p
    after = right(got[:, base + LANES : base + 2 * LANES])
    g = jnp.exp(runs[span - 1 : span, :] - runs) * mm(b_l, after)
    d_s = jnp.zeros((span, span), F32)
    d_st = jnp.zeros((span, span), F32)
    for k in range(2):
        keep = low if k == 0 else jnp.logical_not(low)
        xk_hi, xk_lo = jnp.where(keep, x_hi, zero), jnp.where(keep, x_lo, zero)
        dk = jnp.where(keep, dy_b, zero)
        down = jnp.broadcast_to(ptable[:, k : k + 1], (span, span))
        along = prun[k : k + 1, :]
        decay = jnp.exp(jnp.where(causal, down - along, -1e30))
        decay_t = jnp.exp(jnp.where(causal_t, along - down, -1e30))
        m_hi, m_lo = split2(decay * scores)
        t_hi, t_lo = split2(decay_t * scores_t)
        y = y + mm(
            jnp.concatenate([m_hi, m_hi, m_lo], 1), jnp.concatenate([xk_hi, xk_lo, xk_hi], 0)
        )
        g = g + mm(jnp.concatenate([t_hi, t_lo], 1), jnp.concatenate([dk, dk], 0))
        d_two = jnp.concatenate([dk, dk], 1)
        x_two = jnp.concatenate([x_hi, x_lo], 1)
        d_s = d_s + decay * mm_nt(d_two, x_two)
        d_st = d_st + decay_t * mm_nt(x_two, d_two)
    py[...] = y.astype(BF16)
    d_c = mm(left(d_s), right(b_p)) + mm_nt(
        left(jnp.exp(runs) * dy), right_nt(got[:, base : base + LANES])
    )
    d_b = mm(left(d_st), right(c_p)) + mm_nt(
        left(jnp.exp(runs[span - 1 : span, :] - runs) * x_hat),
        right_nt(got[:, base + LANES : base + 2 * LANES]),
    )
    dxh[...] = g
    dbs[...] = d_b
    pxs[0:span, :] = x_hat

    def fork(q, _):
        where = scal[q] - 1 - row * span

        @pl.when((where >= 0) & (where < span))
        def _():
            gap = wexp[pl.ds(where, 1), :] - wexp[...]
            u = jnp.exp(jnp.where(iota((span, LANES), 0) <= where, gap, -1e30))
            grad = got[:, block(2 * js + q)]
            dxh[...] += u * mm(b_l, right(grad))
            dbs[...] += mm_nt(left(u * pxs[0:span, :]), right_nt(grad))

        return 0

    lax.fori_loop(0, js, fork, 0)
    pre_g = (steps * dxh[...] + gain * dy) * silu_slope(x_pre)
    pxs[0:span, :] = pre_g
    pxs[span : span + 8, :] = jnp.zeros((8, LANES), F32)
    pgx[...] = sum(own[i] * pxs[3 - i : 3 - i + span, :] for i in range(4))
    for m, v in enumerate(tail_grads([pxs[s : s + 1, :] for s in range(3)], own)):
        rims[m, 16:17, :] = v
    pbcs[0:span, :] = jnp.concatenate([dbs[...], d_c], axis=1) * silu_slope(bc_pre)
    pbcs[span : span + 8, :] = jnp.zeros((8, 2 * STATE), F32)
    grad = sum(taps[i] * pbcs[3 - i : 3 - i + span, :] for i in range(4))
    for m, v in enumerate(tail_grads([pbcs[s : s + 1, :] for s in range(3)], taps)):
        rims[m, 17:18, :] = v[:, :STATE]
        rims[m, 18:19, :] = v[:, STATE:]
    spot = iota((span, LANES), 0) - (scal[20] - 3 - row * span)
    lane = iota((span, LANES), 1)
    tails = exact(got[:, base + 8 * LANES : base + 9 * LANES])
    into = []
    for half in range(2):
        hit = ((spot >= 0) & (spot < 3) & (lane == spot + 3 * half)).astype(F32).astype(BF16)
        into.append(mm_nt(jnp.concatenate([hit, hit, hit], 1), tails))
    gbc[...] = grad + jnp.concatenate(into, axis=1)


def finish_kernel(scal, pgx, got, out_x, out_bc):
    row = scal[17]
    span = pgx.shape[0]
    peers = got.shape[0]
    width = got.shape[1] - 3
    total = got[0]
    for p in range(1, peers):
        total = total + got[p]
    rows = width // 2
    out_bc[...] = total[0:width].reshape(rows, 2 * STATE).astype(BF16)


def specs(n):
    return [pl.BlockSpec(memory_space=pltpu.SMEM)] + [pl.BlockSpec(memory_space=pltpu.VMEM)] * (
        n - 1
    )


def call(kernel, args, outs, scratch, flops=10**8):
    return pl.pallas_call(
        kernel,
        out_shape=[jax.ShapeDtypeStruct(s, d) for s, d in outs],
        in_specs=specs(len(args)),
        out_specs=[pl.BlockSpec(memory_space=pltpu.VMEM)] * len(outs),
        scratch_shapes=[pltpu.VMEM(s, F32) for s in scratch],
        compiler_params=pltpu.CompilerParams(vmem_limit_bytes=VMEM_LIMIT),
    )(*args)


def shards(
    prompt_x,
    prompt_bc,
    prompt_dt,
    branch_x,
    branch_bc,
    branch_dt,
    conv_x,
    conv_bc,
    a_log,
    dt_bias,
    d_skip,
    lengths,
    forks,
    holder,
    prompt_dy,
    branch_dy,
):
    row = lax.axis_index("prefix")
    col = lax.axis_index("branch")
    count = lax.axis_size("prefix")
    js = lax.axis_size("branch")
    span = prompt_x.shape[0]
    n = branch_x.shape[1]
    heads = 2 * js
    ns = STATE // count

    placed = jnp.sum((holder[None, :] < holder[:, None]).astype(jnp.int32), axis=1)
    owners = (placed[None, :] == jnp.arange(js, dtype=jnp.int32)[:, None]).astype(jnp.int32)
    group_fork = jnp.sum(owners * forks[None, :], axis=1)
    group_length = jnp.sum(owners * lengths[None, :], axis=1)
    mine = (jnp.arange(js, dtype=jnp.int32) == col).astype(jnp.int32)
    own_length = jnp.sum(mine * group_length)
    own_fork = jnp.sum(mine * group_fork)
    scal = jnp.concatenate(
        [
            group_fork,
            jnp.stack(
                [
                    own_length,
                    row.astype(jnp.int32),
                    col.astype(jnp.int32),
                    jnp.int32(span),
                    own_fork,
                ]
            ),
        ]
    )

    px = prompt_x.reshape(span, LANES)
    pbc = prompt_bc.reshape(span, 2 * STATE)
    pdy = prompt_dy.reshape(span, LANES)
    bx = branch_x.reshape(n, js, LANES)
    bbc = branch_bc.reshape(n, 2 * STATE)
    bdy = branch_dy.reshape(n, js, LANES)
    convx = conv_x.reshape(4, js, LANES)
    convbc = conv_bc.reshape(4, 2 * STATE)
    skip = jnp.repeat(d_skip.reshape(js, 2), HEAD_DIM, axis=1)

    rate = jnp.exp(a_log.reshape(heads, 1))
    step = jax.nn.softplus(branch_dt.reshape(heads, n) + dt_bias.reshape(heads, 1))
    logs = -rate * step
    null = (row == 0) & (jnp.arange(n) < 3)[None, :]
    bstep = jnp.where(null, 0.0, step)
    blogs = jnp.where(null, 0.0, logs)
    rate_own = jnp.exp(lax.dynamic_slice_in_dim(a_log.reshape(js, 2), col, 1, 0)).reshape(2, 1)
    bias_own = lax.dynamic_slice_in_dim(dt_bias.reshape(js, 2), col, 1, 0).reshape(2, 1)
    pstep = jax.nn.softplus(prompt_dt.reshape(2, span) + bias_own)
    plogs = -rate_own * pstep

    def wide(a):
        return a.astype(F32).reshape(3, -1, LANES)

    packed = jnp.concatenate(
        [wide(bx[-3:]), wide(px[-3:]), wide(pbc[-3:]), wide(bbc[-3:])], axis=1
    )
    rim = lax.ppermute(packed, "prefix", [(i, i + 1) for i in range(count - 1)])

    tail_pos = (
        group_fork[:, None] - 3 + jnp.arange(3, dtype=jnp.int32)[None, :] - row * span
    ).reshape(-1)
    pick = (tail_pos[:, None] == jnp.arange(span, dtype=jnp.int32)[None, :]).astype(BF16)
    own_pos = own_fork - 3 + jnp.arange(3, dtype=jnp.int32) - row * span
    own_pick = (own_pos[:, None] == jnp.arange(span, dtype=jnp.int32)[None, :]).astype(BF16)
    tail_x = jnp.dot(pick, px, preferred_element_type=F32)
    tail_bc = jnp.dot(own_pick, pbc, preferred_element_type=F32).reshape(6, LANES)
    live3 = (jnp.arange(3) < own_length).astype(F32)[:, None, None]
    early = jnp.concatenate(
        [
            tail_x,
            tail_bc,
            bx[:3].astype(F32).reshape(3 * js, LANES),
            (bdy[:3].astype(F32) * live3).reshape(3 * js, LANES),
            bbc[:3].astype(F32).reshape(6, LANES),
            jnp.zeros((4, LANES), F32),
            jnp.pad(step[:, :3].T, ((0, 5), (0, LANES - heads))),
            jnp.pad(logs[:, :3].T, ((0, 5), (0, LANES - heads))),
        ],
        axis=0,
    )
    early = lax.all_gather(early, "prefix")

    locals_in = [scal, px, pbc, pstep, plogs, pdy, bx, bbc, bstep, blogs, bdy, rim, convx, convbc]
    big = (n * js, LANES)
    with jax.named_scope("local"):
        (sent,) = call(
            local_kernel,
            locals_in,
            [((STATE, (3 * js + 3) * LANES), F32)],
            [
                ((n + 8) * js, LANES), big, big, (n + 8, 2 * STATE), (span + 8, LANES),
                (span + 8, 2 * STATE), (span, LANES), (span, LANES),
            ],
        )
    got = lax.all_to_all(sent.reshape(count, ns, -1), "prefix", 0, 0, tiled=True)
    with jax.named_scope("slices"):
        msg, aft, adj, pst, cols = call(
            slice_kernel,
            [scal, got, early, convbc],
            [
                ((js, ns + 8, 2 * LANES), F32),
                ((count, ns, js * LANES), F32),
                ((3, ns, js * LANES), F32),
                ((count, ns, LANES), F32),
                ((2 * ns, LANES), F32),
            ],
            [(LANES, LANES), (2 * STATE, LANES)],
        )
    moved = lax.all_to_all(msg, "branch", 0, 0, tiled=True)
    with jax.named_scope("chains"):
        (msg3,) = call(
            chain_kernel,
            [scal, got, early, moved, aft, adj, pst, cols, convx, skip],
            [((count, ns, (3 * js + 9) * LANES), F32)],
            [(js, 6 * LANES), (count, ns, LANES)],
        )
    got3 = lax.all_to_all(msg3, "prefix", 0, 0, tiled=True).reshape(STATE, -1)
    with jax.named_scope("final"):
        by, bgx, last, py, pgx, gbc, rims, fork_grads = call(
            final_kernel,
            locals_in + [skip, got3],
            [
                ((n, js, LANES), BF16),
                ((n, js, LANES), BF16),
                ((3, js, LANES), F32),
                ((span, LANES), BF16),
                ((span, LANES), F32),
                ((span, 2 * STATE), F32),
                ((3, js + 3, LANES), F32),
                ((3, js, LANES), F32),
            ],
            [
                ((n + 8) * js, LANES), big, big, big, (n + 8, 2 * STATE), (span + 8, LANES),
                (span + 8, 2 * STATE), (span, LANES), (heads, n), (8, LANES), big,
                (js, 6 * LANES), (span, LANES), (span, STATE),
            ],
        )
    back = lax.ppermute(rims, "prefix", [(i, i - 1) for i in range(1, count)])
    bgx = bgx.at[-3:].set((last + back[:, :js]).astype(BF16))
    pgx = pgx.at[-3:].add(back[:, js])
    gbc = gbc.at[-3:].add(back[:, js + 1 : js + 3].reshape(3, 2 * STATE))
    rows = span // js
    out_msg = jnp.concatenate(
        [gbc.reshape(js, 2 * rows, LANES), jnp.moveaxis(fork_grads, 1, 0)], axis=1
    )
    end = lax.all_to_all(out_msg, "branch", 0, 0, tiled=True)
    prompt_gbc = jnp.sum(end[:, : 2 * rows], axis=0).reshape(rows, 1, 2 * STATE).astype(BF16)
    tails = end[:, 2 * rows :].reshape(3 * js, LANES)
    into = jnp.dot(pick.T.astype(F32), tails, precision=lax.Precision.HIGHEST)
    prompt_gx = (pgx + into).astype(BF16)
    return (
        py.reshape(prompt_x.shape),
        by.reshape(branch_x.shape),
        prompt_gx.reshape(prompt_x.shape),
        bgx.reshape(branch_x.shape),
        prompt_gbc,
    )


def solution(mesh):
    return jax.shard_map(
        shards,
        mesh=mesh,
        in_specs=(
            P("prefix", "branch", "tensor", None),
            P("prefix", "tensor", None),
            P("branch", "tensor", None, "prefix"),
            P("branch", "prefix", None, "tensor", None),
            P("branch", "prefix", "tensor", None),
            P("branch", None, "tensor", None, "prefix"),
            P(None, None, "tensor", None),
            P(None, "tensor", None),
            P(None, "tensor", None),
            P(None, "tensor", None),
            P(None, "tensor", None),
            P(),
            P(),
            P(),
            P("prefix", "branch", "tensor", None),
            P("branch", "prefix", None, "tensor", None),
        ),
        out_specs=(
            P("prefix", "branch", "tensor", None),
            P("branch", "prefix", None, "tensor", None),
            P("prefix", "branch", "tensor", None),
            P("branch", "prefix", None, "tensor", None),
            P(("prefix", "branch"), "tensor", None),
        ),
        check_vma=False,
    )
```

profile of v0, /device:TPU:1, one launch (start us, length us, event | category | flops | bytes accessed | tf_op | source)
XLA Modules:
  0.0 244.8 jit_solution(3524828664536065318)
XLA Ops:
  2.0 1.3 slice_convert_fusion
  4.1 4.6 %collective-permute-start = (f32[3,21,128]{2,1,0:T(8,128)S(1)}, f32[3,21,128]{2,1,0:T(8,128)S(1)}, u32[]{:S(2)}, u32[]{:S(2)}) collective-permute-start(f32[3,21,128]{2,1,0:T(8,128)S(1)} %maximum_convert_fusion), channel_id=1, source_target_pairs={{0,64},{64,128},{128,192},{192,256},{256,320},{320,384},{384,448},... | collective-permute-start | bytes 96776 | tf_op jit(solution)/shard_map/ppermute | solution.py:695
  11.1 0.9 negate_reduce_fusion
  12.2 1.4 broadcast_select_fusion
  15.1 1.4 broadcast_multiply_fusion.1
  16.4 1.1 broadcast_add_fusion
  17.6 1.3 copy.58
  18.8 1.8 concatenate.21.scal
  21.3 12.6 %local.1 = f32[128,6528]{1,0:T(8,128)} custom-call(s32[21]{0:T(128)} %concatenate.21.scal, bf16[256,128]{1,0:T(8,128)(2,1)} %bitcast.89, bf16[256,256]{1,0:T(8,128)(2,1)} %bitcast.82, f32[2,256]{1,0:T(2,128)} %get-tuple-element.88.pstep, f32[2,256]{1,0:T(2,128)} %get-tuple-element.87.plogs, bf16[256,128]{1,0:T(8,128)(2,1)} %bitcast.91, ...), custom_call_target="tpu_custom_call" | custom-call | tf_op jit(solution)/shard_map/local/pallas_call | solution.py:609
  33.9 7.3 %all-to-all-start = ((f32[8,16,6528]{2,1,0:T(8,128)}), f32[8,16,6528]{2,1,0:T(8,128)S(1)}, u32[]{:S(2)}, u32[]{:S(2)}) async-start(f32[8,16,6528]{2,1,0:T(8,128)} %bitcast.74), calls=%async_computation | async-start | bytes 6684672 | tf_op jit(solution)/shard_map/all_to_all | solution.py:733
  41.2 1.3 slice.114
  42.5 1.3 slice.113
  45.7 1.2 mul.67
  51.5 1.4 convert_multiply_fusion
  53.7 1.7 concatenate.24
  55.4 35.4 %all-gather = f32[1408,128]{1,0:T(8,128)} all-gather(f32[176,128]{1,0:T(8,128)S(1)} %concatenate.24), channel_id=2, replica_groups=mesh['prefix'=8,'branch'=16,'tensor'=4] {'prefix'}, dimensions={0}, use_global_device_ids=true | all-gather | bytes 811008 | tf_op jit(solution)/shard_map/all_gather | solution.py:719
  90.8 1.7 copy-done
  92.5 4.1 %slices.1 = (f32[16,24,256]{2,1,0:T(8,128)}, f32[8,16,2048]{2,1,0:T(8,128)}, f32[3,16,2048]{2,1,0:T(8,128)}, f32[8,16,128]{2,1,0:T(8,128)}, f32[32,128]{1,0:T(8,128)}) custom-call(s32[21]{0:T(128)} %concatenate.21.scal, f32[8,16,6528]{2,1,0:T(8,128)} %copy-done, f32[8,176,128]{2,1,0:T(8,128)} %bitcast.75, f32[4,256]{1,0:T(4,128)} %bitcast.94), custom_call_target="tpu_custom_call" | custom-call | tf_op jit(solution)/shard_map/slices/pallas_call | solution.py:609
  96.6 12.5 %all-to-all-start.1 = ((f32[16,24,256]{2,1,0:T(8,128)}), f32[16,24,256]{2,1,0:T(8,128)S(1)}, u32[]{:S(2)}, u32[]{:S(2)}) async-start(f32[16,24,256]{2,1,0:T(8,128)} %get-tuple-element.54), calls=%async_computation.1 | async-start | bytes 786432 | tf_op jit(solution)/shard_map/all_to_all | solution.py:747
  109.9 18.2 %all-to-all-done.1.moved = f32[16,24,256]{2,1,0:T(8,128)S(1)} async-done(((f32[16,24,256]{2,1,0:T(8,128)}), f32[16,24,256]{2,1,0:T(8,128)S(1)}, u32[]{:S(2)}, u32[]{:S(2)}) %all-to-all-start.1) | async-done | bytes 393248 | tf_op jit(solution)/shard_map/all_to_all | solution.py:747
  128.9 5.7 %chains.1 = f32[8,16,7296]{2,1,0:T(8,128)} custom-call(s32[21]{0:T(128)} %concatenate.21.scal, f32[8,16,6528]{2,1,0:T(8,128)} %copy-done, f32[8,176,128]{2,1,0:T(8,128)} %bitcast.76, f32[16,24,256]{2,1,0:T(8,128)} %copy-done.1, f32[8,16,2048]{2,1,0:T(8,128)} %get-tuple-element.55.aft, f32[3,16,2048]{2,1,0:T(8,128)} %get-tuple-element.56.adj, ...), custom_call_target="tpu_custom_call" | custom-call | tf_op jit(solution)/shard_map/chains/pallas_call | solution.py:609
  134.6 55.1 %all_to_all.20 = f32[8,16,7296]{2,1,0:T(8,128)} all-to-all(f32[8,16,7296]{2,1,0:T(8,128)} %chains.1), channel_id=1, replica_groups=mesh['prefix'=8,'branch'=16,'tensor'=4] {'prefix'}, dimensions={0} | all-to-all | bytes 7471104 | tf_op jit(solution)/shard_map/all_to_all | solution.py:755
  189.7 17.1 %final.1 = (bf16[128,16,128]{2,1,0:T(8,128)(2,1)}, bf16[128,16,128]{2,1,0:T(8,128)(2,1)}, f32[3,16,128]{2,1,0:T(8,128)}, bf16[256,128]{1,0:T(8,128)(2,1)}, f32[2...) custom-call(s32[21]{0:T(128)} %concatenate.21.scal, ...), custom_call_target="tpu_custom_call" | custom-call | tf_op jit(solution)/shard_map/final/pallas_call | solution.py:609
  206.8 2.6 %collective-permute-start.1 = (f32[3,19,128]{2,1,0:T(8,128)}, f32[3,19,128]{2,1,0:T(8,128)S(1)}, u32[]{:S(2)}, u32[]{:S(2)}) collective-permute-start(f32[3,19,128]{2,1,0:T(8,128)} %get-tuple-element.62), channel_id=1, source_target_pairs={{64,0},{128,64},{192,128},{256,192},{320,256},{384,320},{448,384},... | collective-permute-start | bytes 87560 | tf_op jit(solution)/shard_map/ppermute | solution.py:776
  210.3 2.1 collective-permute-done.1
  213.0 1.3 scatter-add.9
  214.3 1.0 reshape.314
  216.1 5.3 %all-to-all-start.3 = ((f32[16,35,128]{2,1,0:T(8,128)}), f32[16,35,128]{2,1,0:T(8,128)S(1)}, u32[]{:S(2)}, u32[]{:S(2)}) async-start(f32[16,35,128]{2,1,0:T(8,128)} %pad_maximum_fusion), calls=%async_computation.3 | async-start | bytes 655360 | tf_op jit(solution)/shard_map/all_to_all | solution.py:784
  222.1 1.3 scatter-add.6
  223.4 1.3 fusion.7
  224.7 17.5 %all-to-all-done.3 = f32[16,35,128]{2,1,0:T(8,128)S(1)} async-done(((f32[16,35,128]{2,1,0:T(8,128)}), f32[16,35,128]{2,1,0:T(8,128)S(1)}, u32[]{:S(2)}, u32[]{:S(2)}) %all-to-all-start.3) | async-done | bytes 286752 | tf_op jit(solution)/shard_map/all_to_all | solution.py:784
  242.9 1.9 fusion.1
  (62 shorter events, 18.5 us)
Async XLA Ops:
  4.1 16.6 %collective-permute-start = (f32[3,21,128]{2,1,0:T(8,128)S(1)}, f32[3,21,128]{2,1,0:T(8,128)S(1)}, u32[]{:S(2)}, u32[]{:S(2)}) collective-permute-start(f32[3,21,128]{2,1,0:T(8,128)S(1)} %maximum_convert_fusion), channel_id=1, source_target_pairs={{0,64},{64,128},{128,192},{192,256},{256,320},{320,384},{384,448},... | collective-permute-start | bytes 96776 | tf_op jit(solution)/shard_map/ppermute | solution.py:695
  20.7 0.6 copy-start.4
  33.9 13.0 %copy-start.2 = (bf16[256,1,256]{2,0,1:T(8,128)(2,1)S(1)}, bf16[256,1,256]{2,0,1:T(8,128)(2,1)}, u32[]{:S(2)}) copy-start(bf16[256,1,256]{2,0,1:T(8,128)(2,1)} %param.23) | copy-start | bytes 393220
  33.9 19.0 %copy-start.3 = (bf16[256,1,1,128]{3,0,2,1:T(8,128)(2,1)S(1)}, bf16[256,1,1,128]{3,0,2,1:T(8,128)(2,1)}, u32[]{:S(2)}) copy-start(bf16[256,1,1,128]{3,0,2,1:T(8,128)(2,1)} %param.22) | copy-start | bytes 196612
  33.9 56.9 %all-to-all-start = ((f32[8,16,6528]{2,1,0:T(8,128)}), f32[8,16,6528]{2,1,0:T(8,128)S(1)}, u32[]{:S(2)}, u32[]{:S(2)}) async-start(f32[8,16,6528]{2,1,0:T(8,128)} %bitcast.74), calls=%async_computation | async-start | bytes 6684672 | tf_op jit(solution)/shard_map/all_to_all | solution.py:733
  49.9 3.8 %copy-start.5 = (s32[48]{0:T(128)}, s32[48]{0:T(128)S(1)}, u32[]{:S(2)}) copy-start(s32[48]{0:T(128)S(1)} %sub.32) | copy-start | bytes 580
  50.6 58.5 %copy-start.7 = (f32[16,1,2]{0,2,1:T(2,128)S(1)}, f32[16,1,2]{0,2,1:T(2,128)}, u32[]{:S(2)}) copy-start(f32[16,1,2]{0,2,1:T(2,128)} %param.32) | copy-start | bytes 388
  90.8 1.7 copy-start
  96.6 31.6 %all-to-all-start.1 = ((f32[16,24,256]{2,1,0:T(8,128)}), f32[16,24,256]{2,1,0:T(8,128)S(1)}, u32[]{:S(2)}, u32[]{:S(2)}) async-start(f32[16,24,256]{2,1,0:T(8,128)} %get-tuple-element.54), calls=%async_computation.1 | async-start | bytes 786432 | tf_op jit(solution)/shard_map/all_to_all | solution.py:747
  128.2 0.7 copy-start.1
  189.7 53.2 %copy-start.6 = (s32[48]{0:T(128)S(1)}, s32[48]{0:T(128)}, u32[]{:S(2)}) copy-start(s32[48]{0:T(128)} %copy-done.5) | copy-start | bytes 580
  206.8 5.5 %collective-permute-start.1 = (f32[3,19,128]{2,1,0:T(8,128)}, f32[3,19,128]{2,1,0:T(8,128)S(1)}, u32[]{:S(2)}, u32[]{:S(2)}) collective-permute-start(f32[3,19,128]{2,1,0:T(8,128)} %get-tuple-element.62), channel_id=1, source_target_pairs={{64,0},{128,64},{192,128},{256,192},{320,256},{384,320},{448,384},... | collective-permute-start | bytes 87560 | tf_op jit(solution)/shard_map/ppermute | solution.py:776
  216.1 26.2 %all-to-all-start.3 = ((f32[16,35,128]{2,1,0:T(8,128)}), f32[16,35,128]{2,1,0:T(8,128)S(1)}, u32[]{:S(2)}, u32[]{:S(2)}) async-start(f32[16,35,128]{2,1,0:T(8,128)} %pad_maximum_fusion), calls=%async_computation.3 | async-start | bytes 655360 | tf_op jit(solution)/shard_map/all_to_all | solution.py:784
where the time goes:
time: 246 us; the launch traced here: 245 us
  blocking collectives  90.4 us (37%)
  Pallas kernels  39.6 us (16%)
  waiting for transfers between devices  37.8 us (15%)
  starting transfers between devices  32.3 us (13%)
  local copies, waits for them, and re-layouts  23.8 us (10%)
  other arithmetic  16 us (7%)
  matrix products  3.47 us (1%)
    all_to_all x1, blocking collectives, shards(): got3 = lax.all_to_all(msg3, 'prefix', 0, 0, tiled=True).reshape(STATE, -1)  55.1 us
    pallas_call x4, Pallas kernels, call(): pl.pallas_call(kernel, out_shape=[jax.ShapeDtypeStruct(s, d) for s, d in...  39.6 us
    all_gather x1, blocking collectives, shards(): early = lax.all_gather(early, 'prefix')  35.4 us
    all_to_all x1, waiting for transfers between devices, shards(): moved = lax.all_to_all(msg, 'branch', 0, 0, tiled=True)  18.2 us
    all_to_all x1, waiting for transfers between devices, shards(): end = lax.all_to_all(out_msg, 'branch', 0, 0, tiled=True)  17.5 us
    all_to_all x1, starting transfers between devices, shards(): moved = lax.all_to_all(msg, 'branch', 0, 0, tiled=True)  12.5 us
    all_to_all x1, starting transfers between devices, shards(): lax.all_to_all(sent.reshape(count, ns, -1), 'prefix', 0, 0, tiled=True)  7.28 us
    all_to_all x1, starting transfers between devices, shards(): end = lax.all_to_all(out_msg, 'branch', 0, 0, tiled=True)  5.3 us
  transfers between devices with their start and end apart: 5, of which 3 were waited for; matrix products, arithmetic and copies ran while one was open for 12% of the time, Pallas kernels for 0%

commit v1 on v0

v1 whole, which is shorter than its diff:
```python
import functools

import jax
import jax.numpy as jnp
from jax import lax
from jax.experimental import pallas as pl
from jax.experimental.pallas import tpu as pltpu
from jax.sharding import PartitionSpec as P

HEAD_DIM = 64
STATE = 128
LANES = 128

F32 = jnp.float32
BF16 = jnp.bfloat16

TAIL_X = 0
ROW_X = 3
ROW_DY = 6
ROW_BC = 9
ROW_STEP = 10
EARLY = 11

VMEM_LIMIT = 56 * 1024 * 1024


def split2(a):
    hi = a.astype(BF16)
    return hi, (a - hi.astype(F32)).astype(BF16)


def split3(a):
    hi = a.astype(BF16)
    rest = a - hi.astype(F32)
    mid = rest.astype(BF16)
    return hi, mid, (rest - mid.astype(F32)).astype(BF16)


def mm(a, b):
    return lax.dot_general(a, b, (((1,), (0,)), ((), ())), preferred_element_type=F32)


def mm_nt(a, b):
    return lax.dot_general(a, b, (((1,), (1,)), ((), ())), preferred_element_type=F32)


def left(a):
    hi, lo = split2(a)
    return jnp.concatenate([hi, hi, lo], axis=1)


def right(b):
    hi, lo = split2(b)
    return jnp.concatenate([hi, lo, hi], axis=0)


def right_nt(b):
    hi, lo = split2(b)
    return jnp.concatenate([hi, lo, hi], axis=1)


def exact(a):
    return jnp.concatenate(split3(a), axis=1)


def iota(shape, dim):
    return lax.broadcasted_iota(jnp.int32, shape, dim)


def picker(base, j):
    one = (iota((LANES, LANES), 0) == base + 2 * j + iota((LANES, LANES), 1) // HEAD_DIM).astype(
        F32
    ).astype(BF16)
    return jnp.concatenate([one, one, one], axis=0)


def running_sum(logs):
    size = logs.shape[1]
    upper = (iota((size, size), 0) <= iota((size, size), 1)).astype(F32).astype(BF16)
    return mm(exact(logs), jnp.concatenate([upper, upper, upper], axis=0))


def block(j):
    return pl.ds(pl.multiple_of(j * LANES, LANES), LANES)


def sigmoid(x):
    return 1.0 / (1.0 + jnp.exp(-x))


def head_column(pair, heads):
    shape = (heads, heads // 2)
    r = iota(shape, 0)
    both = jnp.where(r % 2 == 0, pair[0:1], pair[1:2])
    return jnp.sum(jnp.where(iota(shape, 1) == r // 2, both, 0.0), axis=1, keepdims=True)


def softplus(x):
    return jnp.maximum(x, 0.0) + jnp.log1p(jnp.exp(-jnp.abs(x)))


def setup_kernel(
    forks, lengths, holder, bx, px, pbc, bbc, alog, bias, gain, bdt, pdt,
    scal, rim, step, logs, pstep, plogs, skip,
):
    row, col = lax.axis_index("prefix"), lax.axis_index("branch")
    js = bx.shape[1]

    def place(b, _):
        group = lax.fori_loop(
            0, js, lambda c, t: t + (holder[c] < holder[b]).astype(jnp.int32), jnp.int32(0),
            unroll=16,
        )
        scal[group] = forks[b]

        @pl.when(group == col)
        def _():
            scal[16] = lengths[b]
            scal[20] = forks[b]

        return 0

    lax.fori_loop(0, js, place, 0)
    scal[17] = row
    scal[18] = col
    scal[19] = pdt.shape[1]
    last = bx.shape[0] - 3
    xl = px[...].astype(F32)
    bcl = pbc[...].astype(F32)
    bbl = bbc[...].astype(F32)
    for r in range(3):
        rim[r, 0:js, :] = bx[last + r].astype(F32)
        at = slice(last + r, last + r + 1)
        rim[r, js : js + 1, :] = xl[at]
        rim[r, js + 1 : js + 2, :] = bcl[at, :STATE]
        rim[r, js + 2 : js + 3, :] = bcl[at, STATE:]
        rim[r, js + 3 : js + 4, :] = bbl[at, :STATE]
        rim[r, js + 4 : js + 5, :] = bbl[at, STATE:]
    heads = bdt.shape[0]
    s = softplus(bdt[...] + head_column(bias[...], heads))
    step[...] = s
    logs[...] = -jnp.exp(head_column(alog[...], heads)) * s
    own = iota((2, js), 1) == col
    own_bias = jnp.sum(jnp.where(own, bias[...], 0.0), axis=1, keepdims=True)
    own_rate = jnp.exp(jnp.sum(jnp.where(own, alog[...], 0.0), axis=1, keepdims=True))
    s = softplus(pdt[...] + own_bias)
    pstep[...] = s
    plogs[...] = -own_rate * s
    diag = iota((js, js), 0) == iota((js, js), 1)
    first = jnp.sum(jnp.where(diag, gain[0:1], 0.0), axis=1, keepdims=True)
    second = jnp.sum(jnp.where(diag, gain[1:2], 0.0), axis=1, keepdims=True)
    skip[...] = halves(first, second, (js, LANES))


def conv_branch(bx, rim, convx, xs, xt, ds):
    js = bx.shape[1]
    for r in range(3):
        xs[(5 + r) * js : (6 + r) * js, :] = rim[r, 0:js, :]

    def fill(c, _):
        xs[pl.ds(pl.multiple_of(8 * js + c * 16 * js, 16 * js), 16 * js), :] = (
            bx[pl.ds(c * 16, 16)].astype(F32).reshape(16 * js, LANES)
        )
        return 0

    lax.fori_loop(0, bx.shape[0] // 16, fill, 0)

    def one(c, _):
        pre = jnp.zeros((16, js, LANES), F32)
        for i in range(4):
            start = pl.multiple_of((5 + i) * js + c * 16 * js, js)
            pre = pre + convx[i][None] * xs[pl.ds(start, 16 * js), :].reshape(16, js, LANES)
        sg = sigmoid(pre)
        at = pl.ds(pl.multiple_of(c * 16 * js, 16 * js), 16 * js)
        xt[at, :] = (pre * sg).reshape(16 * js, LANES)
        if ds is not None:
            ds[at, :] = (sg * (1.0 + pre * (1.0 - sg))).reshape(16 * js, LANES)
        return 0

    lax.fori_loop(0, bx.shape[0] // 16, one, 0)


def conv_rows(raw, halo_rows, taps, scratch):
    n = raw.shape[0]
    scratch[8 : 8 + n, :] = raw.astype(F32)
    for r in range(3):
        scratch[5 + r : 6 + r, :] = halo_rows[r]
    pre = jnp.zeros(raw.shape, F32)
    for i in range(4):
        pre = pre + taps[i] * scratch[5 + i : 5 + i + n, :]
    return pre


def bc_halo(rim, first):
    return [
        jnp.concatenate([rim[r, first : first + 1, :], rim[r, first + 1 : first + 2, :]], axis=1)
        for r in range(3)
    ]


def silu(x):
    return x * sigmoid(x)


def silu_slope(x):
    sg = sigmoid(x)
    return sg * (1.0 + x * (1.0 - sg))


def without_first(row, values):
    return jnp.where((row == 0) & (iota(values.shape, 1) < 3), 0.0, values)


def branch_table(step, run):
    return jnp.concatenate([step, run, jnp.zeros((64, LANES), F32)], axis=0).T


def prompt_table(step, run):
    n = step.shape[1]
    r = iota((LANES, n), 0)
    runs = jnp.where(r % 2 == 0, run[0:1], run[1:2])
    steps = jnp.where(r % 2 == 0, step[0:1], step[1:2])
    return jnp.where((r == 2) | (r == 3), steps, runs).T


def halves(first, second, shape):
    return jnp.where(iota(shape, 1) < HEAD_DIM, first, second)


def part(h, row):
    half = STATE // 2
    core = lax.rem(row, 2)
    return pl.ds(pl.multiple_of((core if h == 0 else 1 - core) * half, half), half)


def live_dy(row, length, bdy, dys):
    n, js = bdy.shape[0], bdy.shape[1]

    def fill(c, _):
        pos = row * n + c * 16 + iota((16, js, LANES), 0)
        dead = (pos >= length) | (pos < 3)
        dys[pl.ds(pl.multiple_of(c * 16 * js, 16 * js), 16 * js), :] = jnp.where(
            dead, 0.0, bdy[pl.ds(c * 16, 16)].astype(F32)
        ).reshape(16 * js, LANES)
        return 0

    lax.fori_loop(0, n // 16, fill, 0)


def lead_kernel(
    scal, px, pbc, pstep, plogs, pdy, bx, bbc, bstep, blogs, bdy, rim, convx, convbc,
    mine, other, dys, bcs, pxs, pbcs, wexp, tab, early, out,
):
    row, col, length = scal[17], scal[18], scal[16]
    n, js = bdy.shape[0], bdy.shape[1]
    span = px.shape[0]
    live_dy(row, length, bdy, dys)
    taps = [convbc[i : i + 1, :] for i in range(4)]
    bc = silu(conv_rows(bbc[...], bc_halo(rim, 19), taps, bcs))
    c_t = left(bc[:, STATE:].T)
    step, log = without_first(row, bstep[...]), without_first(row, blogs[...])
    table = branch_table(step, running_sum(log))
    parts = exact(table)

    def head_pair(j, _):
        at = pl.ds(j, n, stride=js)
        runs = mm(parts, picker(32, j))
        out[:, block(j)] = mm(c_t, right(dys[at, :] * jnp.exp(runs)))
        return 0

    lax.fori_loop(0, js, head_pair, 0, unroll=4)

    own = [convx[i, pl.ds(col, 1), :] for i in range(4)]
    x_p = silu(conv_rows(px[...], [rim[r, 16:17, :] for r in range(3)], own, pxs))
    bc_p = silu(conv_rows(pbc[...], bc_halo(rim, 17), taps, pbcs))
    b_pt = left(bc_p[:, :STATE].T)
    c_pt = left(bc_p[:, STATE:].T)
    ptable = prompt_table(pstep[...], running_sum(plogs[...]))
    tab[...] = ptable
    runs = halves(ptable[:, 0:1], ptable[:, 1:2], (span, LANES))
    steps = halves(ptable[:, 2:3], ptable[:, 3:4], (span, LANES))
    wexp[...] = runs
    x_hat = x_p * steps
    base = 2 * js * LANES
    out[:, base : base + LANES] = mm(b_pt, right(x_hat * jnp.exp(runs[span - 1 : span, :] - runs)))
    out[:, base + LANES : base + 2 * LANES] = mm(
        c_pt, right(pdy[...].astype(F32) * jnp.exp(runs))
    )
    lane = iota((1, LANES), 1)
    pxs[0:span, :] = x_hat

    def fork(g, acc):
        where = scal[g] - 1 - row * span
        inside = (where >= 0) & (where < span)

        @pl.when(inside)
        def _():
            w = wexp[...]
            gap = wexp[pl.ds(where, 1), :] - w
            upto = iota((span, LANES), 0) <= where
            u = jnp.exp(jnp.where(upto, gap, -1e30)) * pxs[0:span, :]
            out[:, block(js + g)] = mm(b_pt, right(u))

        @pl.when(jnp.logical_not(inside))
        def _():
            out[:, block(js + g)] = jnp.zeros((STATE, LANES), F32)

        safe = jnp.clip(where, 0, span - 1)
        return jnp.where(lane // 2 == 32 + g, tab[pl.ds(safe, 1), :], acc)

    marks = lax.fori_loop(0, js, fork, jnp.zeros((1, LANES), F32))
    misc = jnp.where(lane < 2, ptable[span - 1 : span, :], marks)
    misc = jnp.where((lane >= 32) & (lane < 64), table[n - 1 : n, :], misc)
    out[:, base + 2 * LANES : base + 3 * LANES] = jnp.broadcast_to(misc, (STATE, LANES))

    first = (row == 0).astype(F32)
    lane2 = iota((js, span), 1)
    spot = jnp.zeros((js, span), jnp.int32)
    for g in range(js):
        spot = jnp.where(iota((js, span), 0) == g, scal[g] - 3 - row * span, spot)
    hits = jnp.concatenate([(lane2 == spot + r).astype(F32).astype(BF16) for r in range(3)], 0)
    tails = mm(hits, px[...])
    own_spot = scal[20] - 3 - row * span + iota((js, span), 0)
    hit = ((lane2 == own_spot) & (iota((js, span), 0) < 3)).astype(F32).astype(BF16)
    tail_bc = mm(hit, pbc[...])
    raw_bc = bbc[0:16].astype(F32) * first
    raw = jnp.concatenate([bstep[...], blogs[...], jnp.zeros((64, LANES), F32)], axis=0).T
    early[...] = jnp.zeros(early.shape, F32)
    for r in range(3):
        early[:, (TAIL_X + r) * LANES : (TAIL_X + r + 1) * LANES] = tails[r * js : (r + 1) * js]
        early[:, (ROW_X + r) * LANES : (ROW_X + r + 1) * LANES] = bx[r].astype(F32) * first
        early[:, (ROW_DY + r) * LANES : (ROW_DY + r + 1) * LANES] = bdy[r].astype(F32) * (
            first * (r < length).astype(F32)
        )
        for half in range(2):
            at = slice(half * STATE, (half + 1) * STATE)
            early[2 * r + half : 2 * r + half + 1, ROW_BC * LANES : (ROW_BC + 1) * LANES] = (
                tail_bc[r : r + 1, at]
            )
            early[6 + 2 * r + half : 7 + 2 * r + half, ROW_BC * LANES : (ROW_BC + 1) * LANES] = (
                raw_bc[r : r + 1, at]
            )
    early[0:8, ROW_STEP * LANES : (ROW_STEP + 1) * LANES] = raw[0:8] * first
    for h, half_out in enumerate((mine, other)):
        half_out[:, : base + 3 * LANES] = out[part(h, row), :]
        for q in range(half_out.shape[0] // js):
            half_out[q * js : (q + 1) * js, base + 3 * LANES :] = early[...]


def pair_falls(even, odd, column):
    both = jnp.concatenate([even[0:1, column], odd[0:1, column], jnp.zeros((6, LANES), F32)], 0)
    return both, exact(both)


def in_odd(scal, g, span):
    where = scal[g] - 1 - lax.div(scal[17], 2) * (2 * span)
    return (where >= span) & (where < 2 * span)


def reach_of(mark, g):
    return jnp.exp(
        halves(mark[:, 64 + 2 * g : 65 + 2 * g], mark[:, 65 + 2 * g : 66 + 2 * g], (1, LANES))
    )


def by_core(row, run):
    core = lax.rem(row, 2)
    pl.when(core == 0)(functools.partial(run, True))
    pl.when(core == 1)(functools.partial(run, False))


def chip_kernel(scal, mine, theirs, out):
    row, span = scal[17], scal[19]
    half = theirs.shape[0]
    js = 16
    base = 2 * js * LANES
    column = slice(base + 2 * LANES, base + 3 * LANES)

    def join(is_even):
        even, odd = (mine, theirs) if is_even else (theirs, mine)
        both, parts = pair_falls(even, odd, column)
        for j in range(js):
            fall = jnp.exp(mm(parts, picker(32, j)))
            at = slice(j * LANES, (j + 1) * LANES)
            out[:, at] = even[:, at] + fall[0:1] * odd[:, at]
        fall = jnp.exp(halves(both[:, 0:1], both[:, 1:2], (8, LANES)))
        state = even[:, base : base + LANES]
        at = slice(base, base + LANES)
        out[:, at] = fall[1:2] * state + odd[:, at]
        at = slice(base + LANES, base + 2 * LANES)
        out[:, at] = even[:, at] + fall[0:1] * odd[:, at]
        lane = iota((1, LANES), 1)
        late = lane < 0
        for g in range(js):
            at = slice((js + g) * LANES, (js + g + 1) * LANES)
            is_odd = in_odd(scal, g, span)
            gain = is_odd.astype(F32) * reach_of(both[1:2], g)
            out[:, at] = even[:, at] + odd[:, at] + gain * state
            late = late | ((lane // 2 == 32 + g) & is_odd)
        before = jnp.where(lane % 2 == 0, both[0:1, 0:1], both[0:1, 1:2])
        marks = jnp.where(late, before + both[1:2], both[0:1])
        misc = jnp.where(lane < 64, both[0:1] + both[1:2], marks)
        out[:, column] = jnp.broadcast_to(misc, (half, LANES))
        out[:, base + 3 * LANES :] = even[:, base + 3 * LANES :] + odd[:, base + 3 * LANES :]

    by_core(row, join)


def spread_prompt_kernel(scal, got, mine, theirs, to_mine, to_other):
    row, span = scal[17], scal[19]
    js = 16
    base = 2 * js * LANES
    at0 = js * LANES
    column = slice(base + 2 * LANES, base + 3 * LANES)

    def split(is_even):
        even, odd = (mine, theirs) if is_even else (theirs, mine)
        to_even, to_odd = (to_mine, to_other) if is_even else (to_other, to_mine)
        both, _ = pair_falls(even, odd, column)
        fall = jnp.exp(halves(both[:, 0:1], both[:, 1:2], (8, LANES)))
        start = got[:, at0 : at0 + LANES]
        to_even[:, at0 : at0 + LANES] = start
        to_odd[:, at0 : at0 + LANES] = even[:, base : base + LANES] + fall[0:1] * start
        after = got[:, at0 + LANES : at0 + 2 * LANES]
        end = odd[:, base + LANES : base + 2 * LANES] + fall[1:2] * after
        for g in range(js):
            gain = in_odd(scal, g, span).astype(F32) * reach_of(both[1:2], g)
            grad = got[:, g * LANES : (g + 1) * LANES]
            end = end + gain * grad
        to_even[:, at0 + LANES : at0 + 2 * LANES] = end
        to_odd[:, at0 + LANES : at0 + 2 * LANES] = after
        for dst in (to_even, to_odd):
            dst[:, :at0] = got[:, :at0]
            dst[:, at0 + 2 * LANES :] = got[:, at0 + 2 * LANES : at0 + 9 * LANES]

    by_core(row, split)


def by_chip(row, pieces):
    chips = len(pieces)
    chip = lax.div(row, 2)
    for d, piece in enumerate(pieces):
        ns = piece.shape[0]
        yield piece, pl.multiple_of(lax.rem(chip - d + chips, chips) * ns, ns)


def spread_branch_kernel(
    scal, got, p0, p1, p2, p3, mine, theirs, smine, stheirs, to_mine, to_other, after
):
    row = scal[17]
    js = 16
    column = slice((2 * js + 2) * LANES, (2 * js + 3) * LANES)
    for piece, first in by_chip(row, (p0, p1, p2, p3)):
        after[pl.ds(first, piece.shape[0]), :] = piece[:, : js * LANES]

    def split(is_even):
        even, odd = (mine, theirs) if is_even else (theirs, mine)
        state = smine if is_even else stheirs
        to_even, to_odd = (to_mine, to_other) if is_even else (to_other, to_mine)
        _, parts = pair_falls(even, odd, column)
        for j in range(js):
            fall = jnp.exp(mm(parts, picker(32, j)))
            at = slice(j * LANES, (j + 1) * LANES)
            start = got[:, (js + 9 + j) * LANES : (js + 10 + j) * LANES]
            to_even[:, at] = start
            to_odd[:, at] = state[:, at] + fall[0:1] * start
            end = after[:, at]
            at2 = slice((js + j) * LANES, (js + j + 1) * LANES)
            to_even[:, at2] = odd[:, at] + fall[1:2] * end
            to_odd[:, at2] = end

    by_core(row, split)


def join_states_kernel(scal, mine, theirs, smine, stheirs, out):
    row = scal[17]
    js = 16
    column = slice((2 * js + 2) * LANES, (2 * js + 3) * LANES)

    def join(is_even):
        even, odd = (mine, theirs) if is_even else (theirs, mine)
        first, second = (smine, stheirs) if is_even else (stheirs, smine)
        _, parts = pair_falls(even, odd, column)
        for j in range(js):
            fall = jnp.exp(mm(parts, picker(32, j)))
            at = slice(j * LANES, (j + 1) * LANES)
            out[:, at] = fall[1:2] * first[:, at] + second[:, at]

    by_core(row, join)


def slice_kernel(
    scal, got, convbc, joined, msg, adj, pst, cols, early, q0, q1, q2, q3, mat, turned, aft
):
    row = scal[17]
    count, ns = got.shape[0], got.shape[1]
    js = msg.shape[0]
    span = 2 * scal[19]
    base = 2 * js * LANES
    total = got[0, :, base + 3 * LANES :]
    for p in range(1, count):
        total = total + got[p, :, base + 3 * LANES :]
    early[...] = total
    for half in range(2):
        seq = [
            early[2 * r + half : 2 * r + half + 1, ROW_BC * LANES : (ROW_BC + 1) * LANES]
            for r in range(6)
        ]
        taps = [convbc[i : i + 1, half * STATE : (half + 1) * STATE] for i in range(4)]
        mat[...] = jnp.zeros((LANES, LANES), F32)
        for s in range(3):
            mat[s : s + 1, :] = sum(taps[i] * seq[s + i] for i in range(4))
        for i in range(4):
            mat[8 + i : 9 + i, :] = taps[i]
        turned[half * STATE : (half + 1) * STATE, :] = mat[...].T
    start = pl.multiple_of((lax.rem(row, 2) * count + lax.div(row, 2)) * ns, 16)
    b_col = turned[pl.ds(start, ns), :]
    c_col = turned[pl.ds(STATE + start, ns), :]
    cols[0:ns, :] = b_col
    cols[ns : 2 * ns, :] = c_col
    c_all = silu(c_col)
    misc = got[:, 0, base + 2 * LANES : base + 3 * LANES]
    misc_parts = exact(misc)
    log_parts = exact(early[0:8, ROW_STEP * LANES : (ROW_STEP + 1) * LANES])
    for j in range(js):
        at = slice(j * LANES, (j + 1) * LANES)
        fall = jnp.exp(mm(misc_parts, picker(32, j)))
        falls = jnp.exp(mm(log_parts, picker(32, j)))
        a = jnp.zeros((ns, LANES), F32)
        for p in reversed(range(count)):
            aft[p, :, at] = a
            a = fall[p : p + 1] * a + got[p, :, at]
        for s in (2, 1, 0):
            dy = early[j : j + 1, (ROW_DY + s) * LANES : (ROW_DY + s + 1) * LANES]
            a = a + dy * c_all[:, s : s + 1]
            adj[s, :, at] = a
            a = falls[s : s + 1] * a
        msg[j, ns : 2 * ns, :] = a
    pfall = jnp.exp(halves(misc[:, 0:1], misc[:, 1:2], (count, LANES)))
    state = jnp.zeros((ns, LANES), F32)
    for p in range(count):
        pst[p] = state
        state = pfall[p : p + 1] * state + got[p, :, base : base + LANES]
    for g in range(js):
        holder = lax.div(scal[g] - 1, span)
        mark = got[holder, 0:1, base + 2 * LANES : base + 3 * LANES]
        reach = reach_of(mark, g)
        at = slice((js + g) * LANES, (js + g + 1) * LANES)
        msg[g, 0:ns, :] = got[holder, :, at] + reach * pst[holder]
        for r in range(3):
            msg[g, 2 * ns + r : 2 * ns + r + 1, :] = early[
                g : g + 1, (TAIL_X + r) * LANES : (TAIL_X + r + 1) * LANES
            ]
        msg[g, 2 * ns + 3 : 2 * ns + 8, :] = jnp.zeros((5, LANES), F32)
    chip = lax.div(row, 2)
    for d, q in enumerate((q0, q1, q2, q3)):
        to = lax.rem(chip + d, count)
        q[:, : js * LANES] = aft[to]
        q[:, js * LANES :] = joined[pl.ds(pl.multiple_of(to * ns, ns), ns), :]


def chain_kernel(
    scal, got, moved, s0, s1, s2, s3, adj, pst, cols, early, convx, skip,
    msg, rows, injected, states,
):
    row = scal[17]
    first = (row == 0).astype(F32)
    count, ns = got.shape[0], got.shape[1]
    js = moved.shape[0]
    span = 2 * scal[19]
    b_col, c_col = cols[0:ns, :], cols[ns : 2 * ns, :]
    b_all, c_all = silu(b_col), silu(c_col)
    base = 2 * js * LANES
    wide = js * LANES
    for piece, first_row in by_chip(row, (s0, s1, s2, s3)):
        states[pl.ds(first_row, ns), :] = piece[:, js * LANES :]
    misc = got[:, 0, base + 2 * LANES : base + 3 * LANES]
    misc_parts = exact(misc)
    log_parts = exact(early[0:8, ROW_STEP * LANES : (ROW_STEP + 1) * LANES])
    sum_b = [jnp.zeros((ns, LANES), F32) for _ in range(3)]
    sum_c = [jnp.zeros((ns, LANES), F32) for _ in range(3)]
    for j in range(js):
        at = slice(j * LANES, (j + 1) * LANES)
        fall = jnp.exp(mm(misc_parts, picker(32, j)))
        falls = jnp.exp(mm(log_parts, picker(32, j)))
        steps = mm(log_parts, picker(0, j))
        seq = [moved[j, 2 * ns + r : 2 * ns + r + 1, :] for r in range(3)] + [
            early[j : j + 1, (ROW_X + s) * LANES : (ROW_X + s + 1) * LANES] for s in range(3)
        ]
        gain = skip[j : j + 1, :] * first
        state = moved[j, 0:ns, :]
        for s in range(3):
            dy = early[j : j + 1, (ROW_DY + s) * LANES : (ROW_DY + s + 1) * LANES]
            pre = sum(convx[i, j : j + 1, :] * seq[s + i] for i in range(4))
            sg = sigmoid(pre)
            x_conv = pre * sg
            x_hat = steps[s : s + 1] * x_conv
            state = falls[s : s + 1] * state + x_hat * b_all[:, s : s + 1]
            a = adj[s, :, at]
            rows[j : j + 1, s * LANES : (s + 1) * LANES] = (
                jnp.sum(state * c_all[:, s : s + 1], axis=0, keepdims=True) + gain * x_conv
            )
            grad = steps[s : s + 1] * jnp.sum(a * b_all[:, s : s + 1], axis=0, keepdims=True)
            rows[j : j + 1, (3 + s) * LANES : (4 + s) * LANES] = (
                sg * (1.0 + pre * (1.0 - sg)) * (grad + gain * dy)
            )
            sum_c[s] = sum_c[s] + dy * state
            sum_b[s] = sum_b[s] + x_hat * a
        for p in range(count):
            msg[p, :, (js + 9 + j) * LANES : (js + 10 + j) * LANES] = state
            state = fall[p : p + 1] * state + states[p * ns : (p + 1) * ns, at]
    lane = iota((ns, LANES), 1)
    back = jnp.zeros((ns, LANES), F32)
    for which, (total, column) in enumerate(((sum_b, b_col), (sum_c, c_col))):
        grads = [
            jnp.sum(total[s], axis=1, keepdims=True) * silu_slope(column[:, s : s + 1])
            for s in range(3)
        ]
        for m in range(3):
            tail = sum(grads[s] * column[:, 8 + m - s : 9 + m - s] for s in range(m + 1))
            back = jnp.where(lane == 3 * which + m, tail, back)
    pfall = jnp.exp(halves(misc[:, 0:1], misc[:, 1:2], (count, LANES)))
    injected[...] = jnp.zeros(injected.shape, F32)
    for g in range(js):
        holder = lax.div(scal[g] - 1, span)
        mark = got[holder, 0:1, base + 2 * LANES : base + 3 * LANES]
        reach = reach_of(mark, g)
        grad = moved[g, ns : 2 * ns, :]
        injected[holder] = injected[holder] + reach * grad
        for p in range(count):
            msg[p, :, g * LANES : (g + 1) * LANES] = grad
    a = jnp.zeros((ns, LANES), F32)
    for p in reversed(range(count)):
        msg[p, :, wide + LANES : wide + 2 * LANES] = a
        a = pfall[p : p + 1] * a + got[p, :, base + LANES : base + 2 * LANES] + injected[p]
    for p in range(count):
        msg[p, :, wide : wide + LANES] = pst[p]
        msg[p, :, wide + 2 * LANES : wide + 8 * LANES] = rows[...]
        msg[p, :, wide + 8 * LANES : wide + 9 * LANES] = back


def tail_grads(lead, taps):
    return [sum(lead[s] * taps[m - s] for s in range(m + 1)) for m in range(3)]


def assemble(core, mine, theirs, lanes, full):
    half = mine.shape[0]
    full[pl.ds(pl.multiple_of(core * half, half), half), :] = mine[:, lanes]
    full[pl.ds(pl.multiple_of((1 - core) * half, half), half), :] = theirs[:, lanes]


def first_rows(mine, theirs, js, rows):
    at = slice((js + 2) * LANES, (js + 8) * LANES)
    total = mine[0:js, at] + theirs[0:js, at]
    for p in range(1, mine.shape[0] // js):
        total = total + mine[p * js : (p + 1) * js, at] + theirs[p * js : (p + 1) * js, at]
    rows[...] = total


def inner_kernel(
    scal, bx, bbc, bstep, blogs, bdy, rim, convx, convbc, skip,
    smine, sother, yi, gi, rise,
    xs, xt, ds, dys, bcs, wrow, out,
):
    row, length = scal[17], scal[16]
    n, js = bx.shape[0], bx.shape[1]
    conv_branch(bx, rim, convx, xs, xt, ds)
    live_dy(row, length, bdy, dys)
    taps = [convbc[i : i + 1, :] for i in range(4)]
    bc = silu(conv_rows(bbc[...], bc_halo(rim, 19), taps, bcs))
    b, c = bc[:, :STATE], bc[:, STATE:]
    b_t = left(b.T)
    scores = mm_nt(left(c), right_nt(b))
    scores_t = mm_nt(left(b), right_nt(c))
    run = running_sum(without_first(row, blogs[...]))
    wrow[...] = run
    parts = exact(branch_table(without_first(row, bstep[...]), run))
    causal = iota((n, n), 0) >= iota((n, n), 1)
    causal_t = iota((n, n), 0) <= iota((n, n), 1)
    low = iota((n, LANES), 1) < HEAD_DIM

    def head_pair(j, _):
        at = pl.ds(j, n, stride=js)
        steps = mm(parts, picker(0, j))
        runs = mm(parts, picker(32, j))
        x_conv = xt[at, :]
        dy = dys[at, :]
        gain = skip[pl.ds(j, 1), :]
        x_hat = x_conv * steps
        x_hi, x_lo = split2(x_hat)
        dy_b = dy.astype(BF16)
        zero = jnp.zeros_like(dy_b)
        out[:, block(j)] = mm(b_t, right(x_hat * jnp.exp(runs[n - 1 : n, :] - runs)))
        mix, mix_t = [], []
        for k in range(2):
            down = jnp.broadcast_to(runs[:, k * HEAD_DIM : k * HEAD_DIM + 1], (n, n))
            along = wrow[pl.ds(2 * j + k, 1), :]
            mix.append(split2(jnp.exp(jnp.where(causal, down - along, -1e30)) * scores))
            mix_t.append(split2(jnp.exp(jnp.where(causal_t, along - down, -1e30)) * scores_t))
        x_blk = [jnp.where(low, x_hi, zero), jnp.where(low, zero, x_hi)]
        x_rest = [jnp.where(low, x_lo, zero), jnp.where(low, zero, x_lo)]
        d_blk = [jnp.where(low, dy_b, zero), jnp.where(low, zero, dy_b)]
        y = mm(
            jnp.concatenate([mix[0][0], mix[1][0], mix[0][0], mix[1][0], mix[0][1], mix[1][1]], 1),
            jnp.concatenate(x_blk + x_rest + x_blk, 0),
        )
        yi[at, :] = y + gain * x_conv
        g = mm(
            jnp.concatenate([mix_t[0][0], mix_t[1][0], mix_t[0][1], mix_t[1][1]], 1),
            jnp.concatenate(d_blk + d_blk, 0),
        )
        slope = ds[at, :]
        gi[at, :] = (steps * g + gain * dy) * slope
        rise[at, :] = steps * slope
        return 0

    lax.fori_loop(0, js, head_pair, 0, unroll=2)
    for h, half_out in enumerate((smine, sother)):
        half_out[...] = out[part(h, row), :]


def carry_kernel(
    scal, bbc, bstep, blogs, rim, convx, convbc, yi, gi, rise,
    rmine, rtheirs, fmine, ftheirs,
    by, bgx, last, rims,
    xs, ys, bcs, rows, start, after,
):
    row, length = scal[17], scal[16]
    n, js = by.shape[0], by.shape[1]
    core = lax.rem(row, 2)
    assemble(core, fmine, ftheirs, slice(0, js * LANES), start)
    assemble(core, fmine, ftheirs, slice(js * LANES, 2 * js * LANES), after)
    first_rows(rmine, rtheirs, js, rows)
    taps = [convbc[i : i + 1, :] for i in range(4)]
    bc = silu(conv_rows(bbc[...], bc_halo(rim, 19), taps, bcs))
    b_l, c_l = left(bc[:, :STATE]), left(bc[:, STATE:])
    run = running_sum(without_first(row, blogs[...]))
    parts = exact(branch_table(without_first(row, bstep[...]), run))
    xs[n * js : (n + 8) * js, :] = jnp.zeros((8 * js, LANES), F32)

    def head_pair(j, _):
        at = pl.ds(j, n, stride=js)
        runs = mm(parts, picker(32, j))
        ys[at, :] = yi[at, :] + jnp.exp(runs) * mm(c_l, right(start[:, block(j)]))
        fall = jnp.exp(runs[n - 1 : n, :] - runs)
        xs[at, :] = gi[at, :] + rise[at, :] * fall * mm(b_l, right(after[:, block(j)]))
        return 0

    lax.fori_loop(0, js, head_pair, 0, unroll=4)

    @pl.when(row == 0)
    def _():
        for s in range(3):
            ys[s * js : (s + 1) * js, :] = rows[:, s * LANES : (s + 1) * LANES]
            xs[s * js : (s + 1) * js, :] = rows[:, (3 + s) * LANES : (4 + s) * LANES]

    def finish(c, _):
        at = pl.multiple_of(c * 16 * js, 16 * js)
        pos = row * n + c * 16 + iota((16, js, LANES), 0)
        y = ys[pl.ds(at, 16 * js), :].reshape(16, js, LANES)
        by[pl.ds(c * 16, 16)] = jnp.where(pos < length, y, 0.0).astype(BF16)
        g = jnp.zeros((16, js, LANES), F32)
        for i in range(4):
            g = g + convx[i][None] * xs[pl.ds(at + (3 - i) * js, 16 * js), :].reshape(
                16, js, LANES
            )
        bgx[pl.ds(c * 16, 16)] = g.astype(BF16)
        return 0

    lax.fori_loop(0, n // 16, finish, 0)
    for m in range(3):
        at = n - 3 + m
        last[m] = sum(
            convx[i] * xs[(at + 3 - i) * js : (at + 4 - i) * js, :] for i in range(4)
        )
    taps_x = [convx[i] for i in range(4)]
    for m, g in enumerate(tail_grads([xs[s * js : (s + 1) * js, :] for s in range(3)], taps_x)):
        rims[m, 0:js, :] = g


def prompt_kernel(
    scal, px, pbc, pstep, plogs, pdy, rim, convx, convbc, skip, mine, theirs,
    py, pgx, gbc, rims, forks,
    pxs, pbcs, wexp, rows, dxh, dbs, got, tail,
):
    row, col = scal[17], scal[18]
    span, js = px.shape[0], convx.shape[1]
    base = js * LANES
    core = lax.rem(row, 2)
    assemble(core, mine, theirs, slice(0, base + 2 * LANES), got)
    assemble(core, mine, theirs, slice(base + 8 * LANES, base + 9 * LANES), tail)
    first_rows(mine, theirs, js, rows)
    taps = [convbc[i : i + 1, :] for i in range(4)]
    fork_lead = [rows[:, (3 + s) * LANES : (4 + s) * LANES] for s in range(3)]
    for m, g in enumerate(tail_grads(fork_lead, [convx[i] for i in range(4)])):
        forks[m] = g
    own = [convx[i, pl.ds(col, 1), :] for i in range(4)]
    gain = skip[pl.ds(col, 1), :]
    x_pre = conv_rows(px[...], [rim[r, 16:17, :] for r in range(3)], own, pxs)
    bc_pre = conv_rows(pbc[...], bc_halo(rim, 17), taps, pbcs)
    x_p = silu(x_pre)
    bc_p = silu(bc_pre)
    b_p, c_p = bc_p[:, :STATE], bc_p[:, STATE:]
    b_l, c_l = left(b_p), left(c_p)
    scores = mm_nt(c_l, right_nt(b_p))
    scores_t = mm_nt(b_l, right_nt(c_p))
    prun = running_sum(plogs[...])
    ptable = prompt_table(pstep[...], prun)
    runs = halves(ptable[:, 0:1], ptable[:, 1:2], (span, LANES))
    steps = halves(ptable[:, 2:3], ptable[:, 3:4], (span, LANES))
    wexp[...] = runs
    x_hat = x_p * steps
    x_hi, x_lo = split2(x_hat)
    dy_b = pdy[...]
    dy = dy_b.astype(F32)
    low = iota((span, LANES), 1) < HEAD_DIM
    zero = jnp.zeros_like(x_hi)
    causal = iota((span, span), 0) >= iota((span, span), 1)
    causal_t = iota((span, span), 0) <= iota((span, span), 1)
    y = jnp.exp(runs) * mm(c_l, right(got[:, base : base + LANES])) + gain * x_p
    after = right(got[:, base + LANES : base + 2 * LANES])
    g = jnp.exp(runs[span - 1 : span, :] - runs) * mm(b_l, after)
    d_s = jnp.zeros((span, span), F32)
    d_st = jnp.zeros((span, span), F32)
    for k in range(2):
        keep = low if k == 0 else jnp.logical_not(low)
        xk_hi, xk_lo = jnp.where(keep, x_hi, zero), jnp.where(keep, x_lo, zero)
        dk = jnp.where(keep, dy_b, zero)
        down = jnp.broadcast_to(ptable[:, k : k + 1], (span, span))
        along = prun[k : k + 1, :]
        decay = jnp.exp(jnp.where(causal, down - along, -1e30))
        decay_t = jnp.exp(jnp.where(causal_t, along - down, -1e30))
        m_hi, m_lo = split2(decay * scores)
        t_hi, t_lo = split2(decay_t * scores_t)
        y = y + mm(
            jnp.concatenate([m_hi, m_hi, m_lo], 1), jnp.concatenate([xk_hi, xk_lo, xk_hi], 0)
        )
        g = g + mm(jnp.concatenate([t_hi, t_lo], 1), jnp.concatenate([dk, dk], 0))
        d_two = jnp.concatenate([dk, dk], 1)
        x_two = jnp.concatenate([x_hi, x_lo], 1)
        d_s = d_s + decay * mm_nt(d_two, x_two)
        d_st = d_st + decay_t * mm_nt(x_two, d_two)
    py[...] = y.astype(BF16)
    d_c = mm(left(d_s), right(b_p)) + mm_nt(
        left(jnp.exp(runs) * dy), right_nt(got[:, base : base + LANES])
    )
    d_b = mm(left(d_st), right(c_p)) + mm_nt(
        left(jnp.exp(runs[span - 1 : span, :] - runs) * x_hat),
        right_nt(got[:, base + LANES : base + 2 * LANES]),
    )
    dxh[...] = g
    dbs[...] = d_b
    pxs[0:span, :] = x_hat

    def fork(q, _):
        where = scal[q] - 1 - row * span

        @pl.when((where >= 0) & (where < span))
        def _():
            gap = wexp[pl.ds(where, 1), :] - wexp[...]
            u = jnp.exp(jnp.where(iota((span, LANES), 0) <= where, gap, -1e30))
            grad = got[:, block(q)]
            dxh[...] += u * mm(b_l, right(grad))
            dbs[...] += mm_nt(left(u * pxs[0:span, :]), right_nt(grad))

        return 0

    lax.fori_loop(0, js, fork, 0)
    pre_g = (steps * dxh[...] + gain * dy) * silu_slope(x_pre)
    pxs[0:span, :] = pre_g
    pxs[span : span + 8, :] = jnp.zeros((8, LANES), F32)
    pgx[...] = sum(own[i] * pxs[3 - i : 3 - i + span, :] for i in range(4))
    for m, v in enumerate(tail_grads([pxs[s : s + 1, :] for s in range(3)], own)):
        rims[m, 0:1, :] = v
    pbcs[0:span, :] = jnp.concatenate([dbs[...], d_c], axis=1) * silu_slope(bc_pre)
    pbcs[span : span + 8, :] = jnp.zeros((8, 2 * STATE), F32)
    grad = sum(taps[i] * pbcs[3 - i : 3 - i + span, :] for i in range(4))
    for m, v in enumerate(tail_grads([pbcs[s : s + 1, :] for s in range(3)], taps)):
        rims[m, 1:2, :] = v[:, :STATE]
        rims[m, 2:3, :] = v[:, STATE:]
    spot = iota((span, LANES), 0) - (scal[20] - 3 - row * span)
    lane = iota((span, LANES), 1)
    tails = exact(tail[...])
    into = []
    for half in range(2):
        hit = ((spot >= 0) & (spot < 3) & (lane == spot + 3 * half)).astype(F32).astype(BF16)
        into.append(mm_nt(jnp.concatenate([hit, hit, hit], 1), tails))
    gbc[...] = grad + jnp.concatenate(into, axis=1)


def packing_kernel(pgx, gbc, back, forks, msg, out):
    span, peers = pgx.shape[0], msg.shape[0]
    rows = span // peers
    out[...] = pgx[...]
    for m in range(3):
        at = slice(span - 3 + m, span - 2 + m)
        out[at, :] = pgx[at, :] + back[m, 0:1, :]
    for q in range(peers):
        msg[q, 0:rows, :] = gbc[q * rows : (q + 1) * rows, :STATE]
        msg[q, rows : 2 * rows, :] = gbc[q * rows : (q + 1) * rows, STATE:]
        for m in range(3):
            msg[q, 2 * rows + m : 2 * rows + m + 1, :] = forks[m, q : q + 1, :]
        msg[q, 2 * rows + 3 : 2 * rows + 8, :] = jnp.zeros((5, LANES), F32)
    for m in range(3):
        at = rows - 3 + m
        msg[peers - 1, at : at + 1, :] += back[m, 1:2, :]
        msg[peers - 1, rows + at : rows + at + 1, :] += back[m, 2:3, :]


def finish_kernel(scal, pgx, got, out_x, out_bc, tails):
    row = scal[17]
    span, peers = pgx.shape[0], got.shape[0]
    rows = span // peers
    total = got[0, 0 : 2 * rows, :]
    for p in range(1, peers):
        total = total + got[p, 0 : 2 * rows, :]
    out_bc[:, :STATE] = total[0:rows].astype(BF16)
    out_bc[:, STATE:] = total[rows : 2 * rows].astype(BF16)
    lane = iota((1, LANES), 1)
    spot = jnp.full((1, LANES), -1, jnp.int32)
    tails[...] = jnp.zeros((LANES, LANES), F32)
    for g in range(peers):
        tails[8 * g : 8 * g + 8, :] = got[g, 2 * rows : 2 * rows + 8, :]
        where = scal[g] - 3 - row * span + lane - 8 * g
        spot = jnp.where((lane >= 8 * g) & (lane < 8 * g + 3), where, spot)
    hit = (iota((span, LANES), 0) == spot).astype(F32).astype(BF16)
    into = mm(jnp.concatenate([hit, hit, hit], 1), jnp.concatenate(split3(tails[...]), 0))
    out_x[...] = (pgx[...] + into).astype(BF16)


def call(kernel, args, outs, scratch, scalars=1, flops=10**9, blocks=None, out_smem=0):
    vmem = pl.BlockSpec(memory_space=pltpu.VMEM)
    smem = pl.BlockSpec(memory_space=pltpu.SMEM)
    given = [smem] * scalars + [vmem] * (len(args) - scalars)
    for at, spec in (blocks or {}).items():
        given[at] = spec
    return pl.pallas_call(
        kernel,
        grid=(1,) if blocks else (),
        out_shape=[jax.ShapeDtypeStruct(s, d) for s, d in outs],
        in_specs=given,
        out_specs=[smem] * out_smem + [vmem] * (len(outs) - out_smem),
        scratch_shapes=[pltpu.VMEM(s, F32) for s in scratch],
        compiler_params=pltpu.CompilerParams(vmem_limit_bytes=VMEM_LIMIT),
        cost_estimate=pl.CostEstimate(flops=flops, bytes_accessed=10**6, transcendentals=0),
    )(*args)


def shards(
    prompt_x,
    prompt_bc,
    prompt_dt,
    branch_x,
    branch_bc,
    branch_dt,
    conv_x,
    conv_bc,
    a_log,
    dt_bias,
    d_skip,
    lengths,
    forks,
    holder,
    prompt_dy,
    branch_dy,
):
    count = lax.axis_size("prefix")
    js = lax.axis_size("branch")
    span = prompt_x.shape[0]
    n = branch_x.shape[1]
    heads = 2 * js
    ns = STATE // count
    chips = count // 2
    half = STATE // 2
    px = prompt_x.reshape(span, LANES)
    pbc = prompt_bc.reshape(span, 2 * STATE)
    pdt = prompt_dt.reshape(2, span)
    pdy = prompt_dy.reshape(span, LANES)
    bx = branch_x.reshape(n, js, LANES)
    bbc = branch_bc.reshape(n, 2 * STATE)
    bdt = branch_dt.reshape(heads, n)
    bdy = branch_dy.reshape(n, js, LANES)
    convx = conv_x.reshape(4, js, LANES)
    convbc = conv_bc.reshape(4, 2 * STATE)
    a_pair, bias_pair, skip_pair = (
        jnp.transpose(v.reshape(js, 2)) for v in (a_log, dt_bias, d_skip)
    )
    cores = [(i, i ^ 1) for i in range(count)]
    columns = [[i for i in range(count) if i % 2 == c] for c in range(2)]

    with jax.named_scope("setup"):
        scal, rim, step, logs, pstep, plogs, skip = call(
            setup_kernel,
            [forks, lengths, holder, bx, px, pbc, bbc, a_pair, bias_pair, skip_pair, bdt, pdt],
            [
                ((24,), jnp.int32),
                ((3, js + 5, LANES), F32),
                ((heads, n), F32),
                ((heads, n), F32),
                ((2, span), F32),
                ((2, span), F32),
                ((js, LANES), F32),
            ],
            [],
            scalars=3,
            out_smem=1,
            blocks={
                3: pl.BlockSpec((16, js, LANES), lambda i: (n // 16 - 1, 0, 0)),
                4: pl.BlockSpec((16, LANES), lambda i: (span // 16 - 1, 0)),
                5: pl.BlockSpec((16, 2 * STATE), lambda i: (span // 16 - 1, 0)),
                6: pl.BlockSpec((16, 2 * STATE), lambda i: (n // 16 - 1, 0)),
            },
        )
    rim = lax.ppermute(rim, "prefix", [(i, i + 1) for i in range(count - 1)])
    big = (n * js, LANES)
    tall = ((n + 8) * js, LANES)
    each = (half, js * LANES)
    piece = (ns, 2 * js * LANES)

    def across(v):
        return lax.ppermute(v, "prefix", cores)

    def round_chips(blocks):
        moved_on = [blocks[0]]
        for d in range(1, chips):
            pairs = [(i, (i + 2 * d) % count) for i in range(count)]
            moved_on.append(lax.ppermute(blocks[d], "prefix", pairs))
        return moved_on

    def between_chips(v):
        return lax.all_to_all(v, "prefix", 0, 0, axis_index_groups=columns, tiled=True)

    width = (2 * js + 3 + EARLY) * LANES
    with jax.named_scope("lead"):
        mine, other = call(
            lead_kernel,
            [scal, px, pbc, pstep, plogs, pdy, bx, bbc, step, logs, bdy, rim, convx, convbc],
            [((half, width), F32)] * 2,
            [
                big, (n + 8, 2 * STATE), (span + 8, LANES), (span + 8, 2 * STATE),
                (span, LANES), (span, LANES), (js, EARLY * LANES), (STATE, (2 * js + 3) * LANES),
            ],
        )
    theirs = across(other)
    with jax.named_scope("chip"):
        (joined,) = call(chip_kernel, [scal, mine, theirs], [((half, width), F32)], [])
    got = between_chips(joined.reshape(chips, ns, width))
    with jax.named_scope("inner"):
        smine, sother, yi, gi, rise = call(
            inner_kernel,
            [scal, bx, bbc, step, logs, bdy, rim, convx, convbc, skip],
            [(each, F32)] * 2 + [(big, F32)] * 3,
            [tall, big, big, big, (n + 8, 2 * STATE), (heads, n), (STATE, js * LANES)],
            flops=10**10,
        )
    stheirs = across(sother)
    with jax.named_scope("join_states"):
        (sjoined,) = call(
            join_states_kernel, [scal, mine, theirs, smine, stheirs], [(each, F32)], []
        )
    with jax.named_scope("slices"):
        msg, adj, pst, cols, early, *ablocks = call(
            slice_kernel,
            [scal, got, convbc, sjoined],
            [
                ((js, 2 * ns + 8, LANES), F32),
                ((3, ns, js * LANES), F32),
                ((chips, ns, LANES), F32),
                ((2 * ns, LANES), F32),
                ((ns, EARLY * LANES), F32),
            ]
            + [(piece, F32)] * 4,
            [(LANES, LANES), (2 * STATE, LANES), (chips, ns, js * LANES)],
        )
    moved = lax.all_to_all(msg, "branch", 0, 0, tiled=True)
    agot = round_chips(ablocks)
    moved, *agot = lax.optimization_barrier((moved, *agot))
    width3 = (js + 9) * LANES
    with jax.named_scope("chains"):
        (msg3,) = call(
            chain_kernel,
            [scal, got, moved, *agot, adj, pst, cols, early, convx, skip],
            [((chips, ns, width3 + js * LANES), F32)],
            [(js, 6 * LANES), (chips, ns, LANES), each],
        )
    got3 = between_chips(msg3).reshape(half, width3 + js * LANES)
    with jax.named_scope("spread_prompt"):
        rmine, rother = call(
            spread_prompt_kernel,
            [scal, got3, mine, theirs],
            [((half, width3), F32)] * 2,
            [],
        )
    both = (half, 2 * js * LANES)
    with jax.named_scope("spread_branch"):
        fmine, fother = call(
            spread_branch_kernel,
            [scal, got3, *agot, mine, theirs, smine, stheirs],
            [(both, F32)] * 2,
            [each],
        )
    rtheirs = across(rother)
    rtheirs, fother = lax.optimization_barrier((rtheirs, fother))
    ftheirs = across(fother)
    with jax.named_scope("prompt"):
        py, pgx, gbc, prims, fork_grads = call(
            prompt_kernel,
            [scal, px, pbc, pstep, plogs, pdy, rim, convx, convbc, skip, rmine, rtheirs],
            [
                ((span, LANES), BF16),
                ((span, LANES), F32),
                ((span, 2 * STATE), F32),
                ((3, 3, LANES), F32),
                ((3, js, LANES), F32),
            ],
            [
                (span + 8, LANES), (span + 8, 2 * STATE), (span, LANES), (js, 6 * LANES),
                (span, LANES), (span, STATE), (STATE, (js + 2) * LANES), (STATE, LANES),
            ],
        )
    backward = [(i, i - 1) for i in range(1, count)]
    pback = lax.ppermute(prims, "prefix", backward)
    with jax.named_scope("packing"):
        out_msg, pgx = call(
            packing_kernel,
            [pgx, gbc, pback, fork_grads],
            [((js, 2 * span // js + 8, LANES), F32), ((span, LANES), F32)],
            [],
            scalars=0,
        )
    end = lax.all_to_all(out_msg, "branch", 0, 0, tiled=True)
    with jax.named_scope("carry"):
        by, bgx, last, brims = call(
            carry_kernel,
            [
                scal, bbc, step, logs, rim, convx, convbc, yi, gi, rise,
                rmine, rtheirs, fmine, ftheirs,
            ],
            [
                ((n, js, LANES), BF16),
                ((n, js, LANES), BF16),
                ((3, js, LANES), F32),
                ((3, js, LANES), F32),
            ],
            [
                tall, big, (n + 8, 2 * STATE), (js, 6 * LANES),
                (STATE, js * LANES), (STATE, js * LANES),
            ],
            flops=10**10,
        )
    bback = lax.ppermute(brims, "prefix", backward)
    bgx = bgx.at[-3:].set((last + bback).astype(BF16))
    with jax.named_scope("finish"):
        prompt_gx, prompt_gbc = call(
            finish_kernel,
            [scal, pgx, end],
            [((span, LANES), BF16), ((span // js, 2 * STATE), BF16)],
            [(LANES, LANES)],
        )
    return (
        py.reshape(prompt_x.shape),
        by.reshape(branch_x.shape),
        prompt_gx.reshape(prompt_x.shape),
        bgx.reshape(branch_x.shape),
        prompt_gbc.reshape(span // js, 1, 2 * STATE),
    )


def solution(mesh):
    return jax.shard_map(
        shards,
        mesh=mesh,
        in_specs=(
            P("prefix", "branch", "tensor", None),
            P("prefix", "tensor", None),
            P("branch", "tensor", None, "prefix"),
            P("branch", "prefix", None, "tensor", None),
            P("branch", "prefix", "tensor", None),
            P("branch", None, "tensor", None, "prefix"),
            P(None, None, "tensor", None),
            P(None, "tensor", None),
            P(None, "tensor", None),
            P(None, "tensor", None),
            P(None, "tensor", None),
            P(),
            P(),
            P(),
            P("prefix", "branch", "tensor", None),
            P("branch", "prefix", None, "tensor", None),
        ),
        out_specs=(
            P("prefix", "branch", "tensor", None),
            P("branch", "prefix", None, "tensor", None),
            P("prefix", "branch", "tensor", None),
            P("branch", "prefix", None, "tensor", None),
            P(("prefix", "branch"), "tensor", None),
        ),
        check_vma=False,
    )
```

time: 246 us -> 183 us (0.74)
  blocking collectives: 90.4 us -> 21.3 us
  starting transfers between devices: 32.3 us -> 58.2 us
  Pallas kernels: 39.6 us -> 64.7 us
  local copies, waits for them, and re-layouts: 23.8 us -> 7.38 us
  other arithmetic: 16 us -> 1.34 us
  waiting for transfers between devices: 37.8 us -> 27.9 us
  matrix products: 3.47 us -> 0 us
    all_gather x1 -> x0, blocking collectives: 35.4 us -> none  [shards(): early = lax.all_gather(early, 'prefix')]
    all_to_all x1, blocking collectives: 55.1 us -> 21.3 us  [between_chips(): lax.all_to_all(v, 'prefix', 0, 0, axis_index_groups=columns, tiled=True)]
    pallas_call x4 -> x13, Pallas kernels: 39.6 us -> 64.7 us  [call(): pl.pallas_call(kernel, grid=(1,) if blocks else (), out_shape=[jax.ShapeD...]
    ppermute x2 -> x10, starting transfers between devices: 7.24 us -> 30.3 us  [the longest x3 11 us: round_chips(): moved_on.append(lax.ppermute(blocks[d], 'prefix', pairs))]
    ppermute x2 -> x10, waiting for transfers between devices: 2.08 us -> 23.9 us  [the longest x3 7.85 us: round_chips(): moved_on.append(lax.ppermute(blocks[d], 'prefix', pairs))]
    all_to_all x1, waiting for transfers between devices: 18.2 us -> 0.01 us  [shards(): moved = lax.all_to_all(msg, 'branch', 0, 0, tiled=True)]
    all_to_all x1, waiting for transfers between devices: 17.5 us -> 4.01 us  [shards(): end = lax.all_to_all(out_msg, 'branch', 0, 0, tiled=True)]
    all_to_all x1, starting transfers between devices: 5.3 us -> 11.5 us  [shards(): end = lax.all_to_all(out_msg, 'branch', 0, 0, tiled=True)]
  transfers between devices with their start and end apart: 5 -> 13, of which waited for: 3 -> 9; matrix products, arithmetic and copies ran while one was open for 12% -> 1% of each run, Pallas kernels for 0% -> 20%
where the time goes in v1:
time: 183 us; the launch traced here: 182 us
  Pallas kernels  64.7 us (35%)
  starting transfers between devices  58.2 us (32%)
  waiting for transfers between devices  27.9 us (15%)
  blocking collectives  21.3 us (12%)
  local copies, waits for them, and re-layouts  7.38 us (4%)
    pallas_call x13, Pallas kernels, call(): pl.pallas_call(kernel, grid=(1,) if blocks else (), out_shape=[jax.ShapeD...  64.7 us
    all_to_all x1, blocking collectives, between_chips(): lax.all_to_all(v, 'prefix', 0, 0, axis_index_groups=columns, tiled=True)  21.3 us
    all_to_all x1, starting transfers between devices, shards(): moved = lax.all_to_all(msg, 'branch', 0, 0, tiled=True)  13 us
    all_to_all x1, starting transfers between devices, shards(): end = lax.all_to_all(out_msg, 'branch', 0, 0, tiled=True)  11.5 us
    ppermute x3, starting transfers between devices, round_chips(): moved_on.append(lax.ppermute(blocks[d], 'prefix', pairs))  11 us
    ppermute x4, starting transfers between devices, across(): return lax.ppermute(v, 'prefix', cores)  10.6 us
    ppermute x3, waiting for transfers between devices, round_chips(): moved_on.append(lax.ppermute(blocks[d], 'prefix', pairs))  7.85 us
    unnamed x27, local copies, waits for them, and re-layouts  7.38 us
  transfers between devices with their start and end apart: 13, of which 9 were waited for; matrix products, arithmetic and copies ran while one was open for 1% of the time, Pallas kernels for 20%

profile of v1, /device:TPU:1, one launch (start us, length us, event | category | flops | bytes accessed | tf_op | source)
XLA Modules:
  0.0 181.7 jit_solution(10097143972613309613)
XLA Ops:
  0.6 2.2 %setup.1 = (s32[24]{0:T(128)}, f32[3,21,128]{2,1,0:T(8,128)}, f32[32,128]{1,0:T(8,128)}, f32[32,128]{1,0:T(8,128)}, f32[2,256]{1,0:T(2,128)}, /*index=5*/f32[2,256]{1,0:T(2,128)}, f32[16,128]{1,0:T(8,128)}) custom-call(s32[16]{0:T(128)} %forks.1, s32[16]{0:T(128)} %lengths.1, s32[16]{0:T(128)} %holder.1, bf16[128,16,128]{2,1,0:T(8,128)(2,1)} %bitcast.48, ...), custom_call_target="tpu_custom_call" | custom-call | flops 1000000000 | bytes 1000000 | tf_op jit(solution)/shard_map/setup/pallas_call | solution.py:937
  2.8 4.6 %collective-permute-start = (f32[3,21,128]{2,1,0:T(8,128)}, f32[3,21,128]{2,1,0:T(8,128)S(1)}, u32[]{:S(2)}, u32[]{:S(2)}) collective-permute-start(f32[3,21,128]{2,1,0:T(8,128)} %get-tuple-element.67), channel_id=1, source_target_pairs={{0,64},{64,128},{128,192},{192,256},{256,320},{320,384},{384,448},... | collective-permute-start | bytes 96776 | tf_op jit(solution)/shard_map/ppermute | solution.py:1014
  8.0 3.9 %collective-permute-done.rim = f32[3,21,128]{2,1,0:T(8,128)S(1)} collective-permute-done((f32[3,21,128]{2,1,0:T(8,128)}, f32[3,21,128]{2,1,0:T(8,128)S(1)}, u32[]{:S(2)}, u32[]{:S(2)}) %collective-permute-start) | collective-permute-done | bytes 32288 | tf_op jit(solution)/shard_map/ppermute | solution.py:1014
  12.5 9.4 %lead.1 = (f32[64,5888]{1,0:T(8,128)}, f32[64,5888]{1,0:T(8,128)}) custom-call(s32[24]{0:T(128)} %get-tuple-element.64.scal, bf16[256,128]{1,0:T(8,128)(2,1)} %bitcast.59, bf16[256,256]{1,0:T(8,128)(2,1)} %bitcast.56, f32[2,256]{1,0:T(2,128)} %get-tuple-element.65.pstep, f32[2,256]{1,0:T(2,128)} %get-tuple-element.66.plogs, bf16[256,128]{1,0:T(8,128)(2,1)} %bitcast.61, ...), custom_call_target="tpu_custom_call" | custom-call | flops 1000000000 | bytes 1000000 | tf_op jit(solution)/shard_map/lead/pallas_call | solution.py:937
  21.9 1.9 %collective-permute-start.1 = (f32[64,5888]{1,0:T(8,128)}, f32[64,5888]{1,0:T(8,128)S(1)}, u32[]{:S(2)}, u32[]{:S(2)}) collective-permute-start(f32[64,5888]{1,0:T(8,128)} %get-tuple-element.72), channel_id=1, source_target_pairs={{0,64},{64,0},{128,192},{192,128},{256,320},{320,256},{384,448},{4... | collective-permute-start | bytes 4521992 | tf_op jit(solution)/shard_map/ppermute | solution.py:1021
  23.8 3.5 %collective-permute-done.1.theirs = f32[64,5888]{1,0:T(8,128)S(1)} collective-permute-done((f32[64,5888]{1,0:T(8,128)}, f32[64,5888]{1,0:T(8,128)S(1)}, u32[]{:S(2)}, u32[]{:S(2)}) %collective-permute-start.1) | collective-permute-done | bytes 1507360 | tf_op jit(solution)/shard_map/ppermute | solution.py:1021
  28.4 3.4 %chip.1 = f32[64,5888]{1,0:T(8,128)} custom-call(s32[24]{0:T(128)} %get-tuple-element.64.scal, f32[64,5888]{1,0:T(8,128)} %get-tuple-element.71.mine, f32[64,5888]{1,0:T(8,128)} %copy-done), custom_call_target="tpu_custom_call" | custom-call | flops 1000000000 | bytes 1000000 | tf_op jit(solution)/shard_map/chip/pallas_call | solution.py:937
  31.8 3.6 %all-to-all-start = ((f32[4,16,5888]{2,1,0:T(8,128)}), f32[4,16,5888]{2,1,0:T(8,128)S(1)}, u32[]{:S(2)}, u32[]{:S(2)}) async-start(f32[4,16,5888]{2,1,0:T(8,128)} %bitcast.37), calls=%async_computation | async-start | bytes 3014656 | tf_op jit(solution)/shard_map/all_to_all | solution.py:1031
  35.4 12.6 %inner.1 = (f32[64,2048]{1,0:T(8,128)}, f32[64,2048]{1,0:T(8,128)}, f32[2048,128]{1,0:T(8,128)}, f32[2048,128]{1,0:T(8,128)}, f32[2048,128]{1,0:T(8,128)}) custom-call(s32[24]{0:T(128)} %get-tuple-element.64.scal, bf16[128,16,128]{2,1,0:T(8,128)(2,1)} %bitcast.50, bf16[128,256]{1,0:T(8,128)(2,1)} %bitcast.65, f32[32,128]{1,0:T(8,128)} %get-tuple-element.69.bstep, ...), custom_call_target="tpu_custom_call" | custom-call | flops 10000000000 | bytes 1000000 | tf_op jit(solution)/shard_map/inner/pallas_call | solution.py:937
  48.0 2.0 %collective-permute-start.2 = (f32[64,2048]{1,0:T(8,128)}, f32[64,2048]{1,0:T(8,128)S(1)}, u32[]{:S(2)}, u32[]{:S(2)}) collective-permute-start(f32[64,2048]{1,0:T(8,128)} %get-tuple-element.74), channel_id=1, source_target_pairs={{0,64},{64,0},{128,192},{192,128},{256,320},{320,256},{384,448},{4... | collective-permute-start | bytes 1572872 | tf_op jit(solution)/shard_map/ppermute | solution.py:1021
  50.0 2.0 %collective-permute-done.2.stheirs = f32[64,2048]{1,0:T(8,128)S(1)} collective-permute-done((f32[64,2048]{1,0:T(8,128)}, f32[64,2048]{1,0:T(8,128)S(1)}, u32[]{:S(2)}, u32[]{:S(2)}) %collective-permute-start.2) | collective-permute-done | bytes 524320 | tf_op jit(solution)/shard_map/ppermute | solution.py:1021
  52.8 3.3 %join_states.1.joined = f32[64,2048]{1,0:T(8,128)} custom-call(s32[24]{0:T(128)} %get-tuple-element.64.scal, f32[64,5888]{1,0:T(8,128)} %get-tuple-element.71.mine, f32[64,5888]{1,0:T(8,128)} %copy-done, f32[64,2048]{1,0:T(8,128)} %get-tuple-element.73.smine, f32[64,2048]{1,0:T(8,128)} %copy-done.2), custom_call_target="tpu_custom_call" | custom-call | flops 1000000000 | bytes 1000000 | tf_op jit(solution)/shard_map/join_states/pallas_call | solution.py:937
  57.3 3.5 %slices.1 = (f32[16,40,128]{2,1,0:T(8,128)}, f32[3,16,2048]{2,1,0:T(8,128)}, f32[4,16,128]{2,1,0:T(8,128)}, f32[32,128]{1,0:T(8,128)}, f32[16,1408]{1,0:T(8,128)...) custom-call(s32[24]{0:T(128)} %get-tuple-element.64.scal, ...), custom_call_target="tpu_custom_call" | custom-call | flops 1000000000 | bytes 1000000 | tf_op jit(solution)/shard_map/slices/pallas_call | solution.py:937
  60.7 13.0 %all-to-all-start.1 = ((f32[16,40,128]{2,1,0:T(8,128)}), f32[16,40,128]{2,1,0:T(8,128)S(1)}, u32[]{:S(2)}, u32[]{:S(2)}) async-start(f32[16,40,128]{2,1,0:T(8,128)} %get-tuple-element.75), calls=%async_computation.1 | async-start | bytes 655360 | tf_op jit(solution)/shard_map/all_to_all | solution.py:1075
  73.7 3.6 %collective-permute-start.3 = (f32[16,4096]{1,0:T(8,128)}, f32[16,4096]{1,0:T(8,128)S(1)}, u32[]{:S(2)}, u32[]{:S(2)}) collective-permute-start(f32[16,4096]{1,0:T(8,128)} %get-tuple-element.77), channel_id=1, source_target_pairs={{0,128},{64,192},{128,256},{192,320},{256,384},{320,448},{384,0},{... | collective-permute-start | bytes 786440 | tf_op jit(solution)/shard_map/ppermute | solution.py:1027
  77.4 4.3 %collective-permute-start.4 = (f32[16,4096]{1,0:T(8,128)}, f32[16,4096]{1,0:T(8,128)S(1)}, u32[]{:S(2)}, u32[]{:S(2)}) collective-permute-start(f32[16,4096]{1,0:T(8,128)} %get-tuple-element.78), channel_id=1, source_target_pairs={{0,256},{64,320},{128,384},{192,448},{256,0},{320,64},{384,128},{4... | collective-permute-start | bytes 786440 | tf_op jit(solution)/shard_map/ppermute | solution.py:1027
  81.7 3.1 %collective-permute-start.5 = (f32[16,4096]{1,0:T(8,128)}, f32[16,4096]{1,0:T(8,128)S(1)}, u32[]{:S(2)}, u32[]{:S(2)}) collective-permute-start(f32[16,4096]{1,0:T(8,128)} %get-tuple-element.79), channel_id=1, source_target_pairs={{0,384},{64,448},{128,0},{192,64},{256,128},{320,192},{384,256},{4... | collective-permute-start | bytes 786440 | tf_op jit(solution)/shard_map/ppermute | solution.py:1027
  84.8 6.5 %collective-permute-done.4.s2.p2 = f32[16,4096]{1,0:T(8,128)S(1)} collective-permute-done((f32[16,4096]{1,0:T(8,128)}, f32[16,4096]{1,0:T(8,128)S(1)}, u32[]{:S(2)}, u32[]{:S(2)}) %collective-permute-start.4) | collective-permute-done | bytes 262176 | tf_op jit(solution)/shard_map/ppermute | solution.py:1027
  93.5 4.3 %chains.1 = f32[4,16,5248]{2,1,0:T(8,128)} custom-call(s32[24]{0:T(128)} %get-tuple-element.64.scal, f32[4,16,5888]{2,1,0:T(8,128)} %copy-done.1, f32[16,40,128]{2,1,0:T(8,128)} %copy-done.3, f32[16,4096]{1,0:T(8,128)} %get-tuple-element.81.s0.p0, f32[16,4096]{1,0:T(8,128)} %copy-done.4, f32[16,4096]{1,0:T(8,128)} %copy-done.5, f32[16,4096]{1,0:T(8,128)} %copy-done.6, ...), custom_call_target="tpu_custom_call" | custom-call | flops 1000000000 | bytes 1000000 | tf_op jit(solution)/shard_map/chains/pallas_call | solution.py:937
  97.7 21.3 %all_to_all.20 = f32[4,16,5248]{2,1,0:T(8,128)} all-to-all(f32[4,16,5248]{2,1,0:T(8,128)} %chains.1), channel_id=1, replica_groups={{0,128,256,384},{64,192,320,448},{1,129,257,385},{65,193,321,449},{2,13..., dimensions={0} | all-to-all | bytes 2686976 | tf_op jit(solution)/shard_map/all_to_all | solution.py:1031
  119.0 3.6 %spread_prompt.1 = (f32[64,3200]{1,0:T(8,128)}, f32[64,3200]{1,0:T(8,128)}) custom-call(s32[24]{0:T(128)} %get-tuple-element.64.scal, f32[64,5248]{1,0:T(8,128)} %bitcast.35, f32[64,5888]{1,0:T(8,128)} %get-tuple-element.71.mine, f32[64,5888]{1,0:T(8,128)} %copy-done), custom_call_target="tpu_custom_call" | custom-call | flops 1000000000 | bytes 1000000 | tf_op jit(solution)/shard_map/spread_prompt/pallas_call | solution.py:937
  122.6 4.6 %collective-permute-start.6 = (f32[64,3200]{1,0:T(8,128)}, f32[64,3200]{1,0:T(8,128)S(1)}, u32[]{:S(2)}, u32[]{:S(2)}) collective-permute-start(f32[64,3200]{1,0:T(8,128)} %get-tuple-element.90), channel_id=1, source_target_pairs={{0,64},{64,0},{128,192},{192,128},{256,320},{320,256},{384,448},{4... | collective-permute-start | bytes 2457608 | tf_op jit(solution)/shard_map/ppermute | solution.py:1021
  127.1 4.7 %spread_branch.1 = (f32[64,4096]{1,0:T(8,128)}, f32[64,4096]{1,0:T(8,128)}) custom-call(s32[24]{0:T(128)} %get-tuple-element.64.scal, f32[64,5248]{1,0:T(8,128)} %bitcast.36, f32[16,4096]{1,0:T(8,128)} %get-tuple-element.81.s0.p0, f32[16,4096]{1,0:T(8,128)} %copy-done.4, f32[16,4096]{1,0:T(8,128)} %copy-done.5, f32[16,4096]{1,0:T(8,128)} %copy-done.6, ...), custom_call_target="tpu_custom_call" | custom-call | flops 1000000000 | bytes 1000000 | tf_op jit(solution)/shard_map/spread_branch/pallas_call | solution.py:937
  131.9 2.1 %collective-permute-start.7 = (f32[64,4096]{1,0:T(8,128)}, f32[64,4096]{1,0:T(8,128)S(1)}, u32[]{:S(2)}, u32[]{:S(2)}) collective-permute-start(f32[64,4096]{1,0:T(8,128)} %get-tuple-element.98), channel_id=1, source_target_pairs={{0,64},{64,0},{128,192},{192,128},{256,320},{320,256},{384,448},{4... | collective-permute-start | bytes 3145736 | tf_op jit(solution)/shard_map/ppermute | solution.py:1021
  134.0 6.0 %prompt.1 = (bf16[256,128]{1,0:T(8,128)(2,1)}, f32[256,128]{1,0:T(8,128)}, f32[256,256]{1,0:T(8,128)}, f32[3,3,128]{2,1,0:T(4,128)}, f32[3,16,128]{2,1,0:T(8,128)}) custom-call(s32[24]{0:T(128)} %get-tuple-element.64.scal, bf16[256,128]{1,0:T(8,128)(2,1)} %bitcast.60, bf16[256,256]{1,0:T(8,128)(2,1)} %bitcast.57, f32[2,256]{1,0:T(2,128)} %get-tuple-element.65.pstep, ...), custom_call_target="tpu_custom_call" | custom-call | flops 1000000000 | bytes 1000000 | tf_op jit(solution)/shard_map/prompt/pallas_call | solution.py:937
  140.0 2.1 %collective-permute-start.8 = (f32[3,3,128]{2,1,0:T(4,128)}, f32[3,3,128]{2,1,0:T(4,128)S(1)}, u32[]{:S(2)}, u32[]{:S(2)}) collective-permute-start(f32[3,3,128]{2,1,0:T(4,128)} %get-tuple-element.102), channel_id=1, source_target_pairs={{64,0},{128,64},{192,128},{256,192},{320,256},{384,320},{448,384},... | collective-permute-start | bytes 13832 | tf_op jit(solution)/shard_map/ppermute | solution.py:1122
  142.2 3.0 %collective-permute-done.8.back = f32[3,3,128]{2,1,0:T(4,128)S(1)} collective-permute-done((f32[3,3,128]{2,1,0:T(4,128)}, f32[3,3,128]{2,1,0:T(4,128)S(1)}, u32[]{:S(2)}, u32[]{:S(2)}) %collective-permute-start.8) | collective-permute-done | bytes 4640 | tf_op jit(solution)/shard_map/ppermute | solution.py:1122
  147.5 11.5 %all-to-all-start.3 = ((f32[16,40,128]{2,1,0:T(8,128)}), f32[16,40,128]{2,1,0:T(8,128)S(1)}, u32[]{:S(2)}, u32[]{:S(2)}) async-start(f32[16,40,128]{2,1,0:T(8,128)} %get-tuple-element.105), calls=%async_computation.3 | async-start | bytes 655360 | tf_op jit(solution)/shard_map/all_to_all | solution.py:1131
  160.0 8.1 %carry.1 = (bf16[128,16,128]{2,1,0:T(8,128)(2,1)}, bf16[128,16,128]{2,1,0:T(8,128)(2,1)}, f32[3,16,128]{2,1,0:T(8,128)}, f32[3,16,128]{2,1,0:T(8,128)}) custom-call(s32[24]{0:T(128)} %get-tuple-element.64.scal, bf16[128,256]{1,0:T(8,128)(2,1)} %bitcast.66, f32[32,128]{1,0:T(8,128)} %get-tuple-element.69.bstep, f32[32,128]{1,0:T(8,128)} %get-tuple-element.70.blogs, ...), custom_call_target="tpu_custom_call" | custom-call | flops 10000000000 | bytes 1000000 | tf_op jit(solution)/shard_map/carry/pallas_call | solution.py:937
  168.1 1.9 %collective-permute-start.9 = (f32[3,16,128]{2,1,0:T(8,128)}, f32[3,16,128]{2,1,0:T(8,128)S(1)}, u32[]{:S(2)}, u32[]{:S(2)}) collective-permute-start(f32[3,16,128]{2,1,0:T(8,128)} %get-tuple-element.109), channel_id=1, source_target_pairs={{64,0},{128,64},{192,128},{256,192},{320,256},{384,320},{448,384},... | collective-permute-start | bytes 73736 | tf_op jit(solution)/shard_map/ppermute | solution.py:1151
  170.0 3.7 %collective-permute-done.9 = f32[3,16,128]{2,1,0:T(8,128)S(1)} collective-permute-done((f32[3,16,128]{2,1,0:T(8,128)}, f32[3,16,128]{2,1,0:T(8,128)S(1)}, u32[]{:S(2)}, u32[]{:S(2)}) %collective-permute-start.9) | collective-permute-done | bytes 24608 | tf_op jit(solution)/shard_map/ppermute | solution.py:1151
  175.1 4.0 %all-to-all-done.3.got = f32[16,40,128]{2,1,0:T(8,128)S(1)} async-done(((f32[16,40,128]{2,1,0:T(8,128)}), f32[16,40,128]{2,1,0:T(8,128)S(1)}, u32[]{:S(2)}, u32[]{:S(2)}) %all-to-all-start.3) | async-done | bytes 327712 | tf_op jit(solution)/shard_map/all_to_all | solution.py:1131
  (36 shorter events, 13.8 us)
Async XLA Ops:
  0.6 6.8 %copy-start.8 = (f32[4,1,256]{2,1,0:T(1,128)S(1)}, f32[4,1,256]{2,1,0:T(1,128)}, u32[]{:S(2)}) copy-start(f32[4,1,256]{2,1,0:T(1,128)} %param.25) | copy-start | bytes 12292
  2.8 9.1 %collective-permute-start = (f32[3,21,128]{2,1,0:T(8,128)}, f32[3,21,128]{2,1,0:T(8,128)S(1)}, u32[]{:S(2)}, u32[]{:S(2)}) collective-permute-start(f32[3,21,128]{2,1,0:T(8,128)} %get-tuple-element.67), channel_id=1, source_target_pairs={{0,64},{64,128},{128,192},{192,256},{256,320},{320,384},{384,448},... | collective-permute-start | bytes 96776 | tf_op jit(solution)/shard_map/ppermute | solution.py:1014
  11.9 0.6 copy-start.11
  21.9 5.4 %collective-permute-start.1 = (f32[64,5888]{1,0:T(8,128)}, f32[64,5888]{1,0:T(8,128)S(1)}, u32[]{:S(2)}, u32[]{:S(2)}) collective-permute-start(f32[64,5888]{1,0:T(8,128)} %get-tuple-element.72), channel_id=1, source_target_pairs={{0,64},{64,0},{128,192},{192,128},{256,320},{320,256},{384,448},{4... | collective-permute-start | bytes 4521992 | tf_op jit(solution)/shard_map/ppermute | solution.py:1021
  27.3 1.1 copy-start
  31.8 24.3 %all-to-all-start = ((f32[4,16,5888]{2,1,0:T(8,128)}), f32[4,16,5888]{2,1,0:T(8,128)S(1)}, u32[]{:S(2)}, u32[]{:S(2)}) async-start(f32[4,16,5888]{2,1,0:T(8,128)} %bitcast.37), calls=%async_computation | async-start | bytes 3014656 | tf_op jit(solution)/shard_map/all_to_all | solution.py:1031
  48.0 4.0 %collective-permute-start.2 = (f32[64,2048]{1,0:T(8,128)}, f32[64,2048]{1,0:T(8,128)S(1)}, u32[]{:S(2)}, u32[]{:S(2)}) collective-permute-start(f32[64,2048]{1,0:T(8,128)} %get-tuple-element.74), channel_id=1, source_target_pairs={{0,64},{64,0},{128,192},{192,128},{256,320},{320,256},{384,448},{4... | collective-permute-start | bytes 1572872 | tf_op jit(solution)/shard_map/ppermute | solution.py:1021
  52.0 0.8 copy-start.2
  56.1 1.2 copy-start.1
  60.7 31.9 %all-to-all-start.1 = ((f32[16,40,128]{2,1,0:T(8,128)}), f32[16,40,128]{2,1,0:T(8,128)S(1)}, u32[]{:S(2)}, u32[]{:S(2)}) async-start(f32[16,40,128]{2,1,0:T(8,128)} %get-tuple-element.75), calls=%async_computation.1 | async-start | bytes 655360 | tf_op jit(solution)/shard_map/all_to_all | solution.py:1075
  73.7 11.1 %collective-permute-start.3 = (f32[16,4096]{1,0:T(8,128)}, f32[16,4096]{1,0:T(8,128)S(1)}, u32[]{:S(2)}, u32[]{:S(2)}) collective-permute-start(f32[16,4096]{1,0:T(8,128)} %get-tuple-element.77), channel_id=1, source_target_pairs={{0,128},{64,192},{128,256},{192,320},{256,384},{320,448},{384,0},{... | collective-permute-start | bytes 786440 | tf_op jit(solution)/shard_map/ppermute | solution.py:1027
  77.4 13.9 %collective-permute-start.4 = (f32[16,4096]{1,0:T(8,128)}, f32[16,4096]{1,0:T(8,128)S(1)}, u32[]{:S(2)}, u32[]{:S(2)}) collective-permute-start(f32[16,4096]{1,0:T(8,128)} %get-tuple-element.78), channel_id=1, source_target_pairs={{0,256},{64,320},{128,384},{192,448},{256,0},{320,64},{384,128},{4... | collective-permute-start | bytes 786440 | tf_op jit(solution)/shard_map/ppermute | solution.py:1027
  81.7 11.0 %collective-permute-start.5 = (f32[16,4096]{1,0:T(8,128)}, f32[16,4096]{1,0:T(8,128)S(1)}, u32[]{:S(2)}, u32[]{:S(2)}) collective-permute-start(f32[16,4096]{1,0:T(8,128)} %get-tuple-element.79), channel_id=1, source_target_pairs={{0,384},{64,448},{128,0},{192,64},{256,128},{320,192},{384,256},{4... | collective-permute-start | bytes 786440 | tf_op jit(solution)/shard_map/ppermute | solution.py:1027
  84.8 7.8 %copy-start.4 = (f32[16,4096]{1,0:T(8,128)}, f32[16,4096]{1,0:T(8,128)S(1)}, u32[]{:S(2)}) copy-start(f32[16,4096]{1,0:T(8,128)S(1)} %collective-permute-done.3.s1.p1) | copy-start | bytes 786436
  91.3 1.3 copy-start.5
  92.6 0.7 copy-start.6
  92.6 0.8 copy-start.3
  122.6 9.3 %collective-permute-start.6 = (f32[64,3200]{1,0:T(8,128)}, f32[64,3200]{1,0:T(8,128)S(1)}, u32[]{:S(2)}, u32[]{:S(2)}) collective-permute-start(f32[64,3200]{1,0:T(8,128)} %get-tuple-element.90), channel_id=1, source_target_pairs={{0,64},{64,0},{128,192},{192,128},{256,320},{320,256},{384,448},{4... | collective-permute-start | bytes 2457608 | tf_op jit(solution)/shard_map/ppermute | solution.py:1021
  131.9 2.1 %copy-start.10 = (f32[64,3200]{1,0:T(8,128)}, f32[64,3200]{1,0:T(8,128)S(1)}, u32[]{:S(2)}) copy-start(f32[64,3200]{1,0:T(8,128)S(1)} %collective-permute-done.6.theirs.rtheirs) | copy-start | bytes 2457604
  131.9 27.1 %collective-permute-start.7 = (f32[64,4096]{1,0:T(8,128)}, f32[64,4096]{1,0:T(8,128)S(1)}, u32[]{:S(2)}, u32[]{:S(2)}) collective-permute-start(f32[64,4096]{1,0:T(8,128)} %get-tuple-element.98), channel_id=1, source_target_pairs={{0,64},{64,0},{128,192},{192,128},{256,320},{320,256},{384,448},{4... | collective-permute-start | bytes 3145736 | tf_op jit(solution)/shard_map/ppermute | solution.py:1021
  140.0 5.1 %collective-permute-start.8 = (f32[3,3,128]{2,1,0:T(4,128)}, f32[3,3,128]{2,1,0:T(4,128)S(1)}, u32[]{:S(2)}, u32[]{:S(2)}) collective-permute-start(f32[3,3,128]{2,1,0:T(4,128)} %get-tuple-element.102), channel_id=1, source_target_pairs={{64,0},{128,64},{192,128},{256,192},{320,256},{384,320},{448,384},... | collective-permute-start | bytes 13832 | tf_op jit(solution)/shard_map/ppermute | solution.py:1122
  145.2 0.6 copy-start.12
  147.5 31.5 %all-to-all-start.3 = ((f32[16,40,128]{2,1,0:T(8,128)}), f32[16,40,128]{2,1,0:T(8,128)S(1)}, u32[]{:S(2)}, u32[]{:S(2)}) async-start(f32[16,40,128]{2,1,0:T(8,128)} %get-tuple-element.105), calls=%async_computation.3 | async-start | bytes 655360 | tf_op jit(solution)/shard_map/all_to_all | solution.py:1131
  159.0 1.0 copy-start.9
  168.1 5.6 %collective-permute-start.9 = (f32[3,16,128]{2,1,0:T(8,128)}, f32[3,16,128]{2,1,0:T(8,128)S(1)}, u32[]{:S(2)}, u32[]{:S(2)}) collective-permute-start(f32[3,16,128]{2,1,0:T(8,128)} %get-tuple-element.109), channel_id=1, source_target_pairs={{64,0},{128,64},{192,128},{256,192},{320,256},{384,320},{448,384},... | collective-permute-start | bytes 73736 | tf_op jit(solution)/shard_map/ppermute | solution.py:1151
  179.1 0.7 copy-start.7

commit v2 on v1

--- a/solution.py
+++ b/solution.py
@@ -247,36 +247,77 @@
     lax.fori_loop(0, n // 16, fill, 0)
 
 
-def lead_kernel(
-    scal, px, pbc, pstep, plogs, pdy, bx, bbc, bstep, blogs, bdy, rim, convx, convbc,
-    mine, other, dys, bcs, pxs, pbcs, wexp, tab, early, out,
+def early_kernel(
+    scal, px, pbc, pstep, plogs, bx, bbc, bstep, blogs, bdy,
+    early, dys, table, run, ptable, prun,
 ):
-    row, col, length = scal[17], scal[18], scal[16]
-    n, js = bdy.shape[0], bdy.shape[1]
+    row, length = scal[17], scal[16]
+    js = bdy.shape[1]
     span = px.shape[0]
     live_dy(row, length, bdy, dys)
+    step, logs = bstep[...], blogs[...]
+    sums = running_sum(without_first(row, logs))
+    run[...] = sums
+    table[...] = branch_table(without_first(row, step), sums)
+    sums = running_sum(plogs[...])
+    prun[...] = sums
+    ptable[...] = prompt_table(pstep[...], sums)
+    first = (row == 0).astype(F32)
+    lane2 = iota((js, span), 1)
+    spot = jnp.zeros((js, span), jnp.int32)
+    for g in range(js):
+        spot = jnp.where(iota((js, span), 0) == g, scal[g] - 3 - row * span, spot)
+    hits = jnp.concatenate([(lane2 == spot + r).astype(F32).astype(BF16) for r in range(3)], 0)
+    tails = mm(hits, px[...])
+    own_spot = scal[20] - 3 - row * span + iota((js, span), 0)
+    hit = ((lane2 == own_spot) & (iota((js, span), 0) < 3)).astype(F32).astype(BF16)
+    tail_bc = mm(hit, pbc[...])
+    raw_bc = bbc[...].astype(F32) * first
+    raw = jnp.concatenate([step, logs, jnp.zeros((64, LANES), F32)], axis=0).T
+    early[...] = jnp.zeros(early.shape, F32)
+    for r in range(3):
+        early[:, (TAIL_X + r) * LANES : (TAIL_X + r + 1) * LANES] = tails[r * js : (r + 1) * js]
+        early[:, (ROW_X + r) * LANES : (ROW_X + r + 1) * LANES] = bx[r].astype(F32) * first
+        early[:, (ROW_DY + r) * LANES : (ROW_DY + r + 1) * LANES] = bdy[r].astype(F32) * (
+            first * (r < length).astype(F32)
+        )
+        for half in range(2):
+            at = slice(half * STATE, (half + 1) * STATE)
+            early[2 * r + half : 2 * r + half + 1, ROW_BC * LANES : (ROW_BC + 1) * LANES] = (
+                tail_bc[r : r + 1, at]
+            )
+            early[6 + 2 * r + half : 7 + 2 * r + half, ROW_BC * LANES : (ROW_BC + 1) * LANES] = (
+                raw_bc[r : r + 1, at]
+            )
+    early[0:8, ROW_STEP * LANES : (ROW_STEP + 1) * LANES] = raw[0:8] * first
+
+
+def lead_kernel(
+    scal, px, pbc, pdy, bbc, rim, convx, convbc, early, dys, table, tab,
+    mine, other, bcs, pxs, pbcs, wexp, out,
+):
+    row, col = scal[17], scal[18]
+    js = convx.shape[1]
+    n = bbc.shape[0]
+    span = px.shape[0]
     taps = [convbc[i : i + 1, :] for i in range(4)]
     bc = silu(conv_rows(bbc[...], bc_halo(rim, 19), taps, bcs))
     c_t = left(bc[:, STATE:].T)
-    step, log = without_first(row, bstep[...]), without_first(row, blogs[...])
-    table = branch_table(step, running_sum(log))
-    parts = exact(table)
-
-    def head_pair(j, _):
-        at = pl.ds(j, n, stride=js)
-        runs = mm(parts, picker(32, j))
-        out[:, block(j)] = mm(c_t, right(dys[at, :] * jnp.exp(runs)))
-        return 0
-
-    lax.fori_loop(0, js, head_pair, 0, unroll=4)
+
+    runs = table[...]
+    grown = jnp.exp(runs)
+    for j in range(0, js, 2):
+        dy = [
+            dys[pl.ds(q, n, stride=js), :] * head_lanes(grown, 32, q) for q in (j, j + 1)
+        ]
+        out[:, j * LANES : (j + 2) * LANES] = mm(c_t, right(jnp.concatenate(dy, axis=1)))
 
     own = [convx[i, pl.ds(col, 1), :] for i in range(4)]
     x_p = silu(conv_rows(px[...], [rim[r, 16:17, :] for r in range(3)], own, pxs))
     bc_p = silu(conv_rows(pbc[...], bc_halo(rim, 17), taps, pbcs))
     b_pt = left(bc_p[:, :STATE].T)
     c_pt = left(bc_p[:, STATE:].T)
-    ptable = prompt_table(pstep[...], running_sum(plogs[...]))
-    tab[...] = ptable
+    ptable = tab[...]
     runs = halves(ptable[:, 0:1], ptable[:, 1:2], (span, LANES))
     steps = halves(ptable[:, 2:3], ptable[:, 3:4], (span, LANES))
     wexp[...] = runs
@@ -313,34 +354,6 @@
     misc = jnp.where((lane >= 32) & (lane < 64), table[n - 1 : n, :], misc)
     out[:, base + 2 * LANES : base + 3 * LANES] = jnp.broadcast_to(misc, (STATE, LANES))
 
-    first = (row == 0).astype(F32)
-    lane2 = iota((js, span), 1)
-    spot = jnp.zeros((js, span), jnp.int32)
-    for g in range(js):
-        spot = jnp.where(iota((js, span), 0) == g, scal[g] - 3 - row * span, spot)
-    hits = jnp.concatenate([(lane2 == spot + r).astype(F32).astype(BF16) for r in range(3)], 0)
-    tails = mm(hits, px[...])
-    own_spot = scal[20] - 3 - row * span + iota((js, span), 0)
-    hit = ((lane2 == own_spot) & (iota((js, span), 0) < 3)).astype(F32).astype(BF16)
-    tail_bc = mm(hit, pbc[...])
-    raw_bc = bbc[0:16].astype(F32) * first
-    raw = jnp.concatenate([bstep[...], blogs[...], jnp.zeros((64, LANES), F32)], axis=0).T
-    early[...] = jnp.zeros(early.shape, F32)
-    for r in range(3):
-        early[:, (TAIL_X + r) * LANES : (TAIL_X + r + 1) * LANES] = tails[r * js : (r + 1) * js]
-        early[:, (ROW_X + r) * LANES : (ROW_X + r + 1) * LANES] = bx[r].astype(F32) * first
-        early[:, (ROW_DY + r) * LANES : (ROW_DY + r + 1) * LANES] = bdy[r].astype(F32) * (
-            first * (r < length).astype(F32)
-        )
-        for half in range(2):
-            at = slice(half * STATE, (half + 1) * STATE)
-            early[2 * r + half : 2 * r + half + 1, ROW_BC * LANES : (ROW_BC + 1) * LANES] = (
-                tail_bc[r : r + 1, at]
-            )
-            early[6 + 2 * r + half : 7 + 2 * r + half, ROW_BC * LANES : (ROW_BC + 1) * LANES] = (
-                raw_bc[r : r + 1, at]
-            )
-    early[0:8, ROW_STEP * LANES : (ROW_STEP + 1) * LANES] = raw[0:8] * first
     for h, half_out in enumerate((mine, other)):
         half_out[:, : base + 3 * LANES] = out[part(h, row), :]
         for q in range(half_out.shape[0] // js):
@@ -349,7 +362,12 @@
 
 def pair_falls(even, odd, column):
     both = jnp.concatenate([even[0:1, column], odd[0:1, column], jnp.zeros((6, LANES), F32)], 0)
-    return both, exact(both)
+    return both, jnp.exp(both)
+
+
+def head_lanes(values, base, j):
+    at = base + 2 * j
+    return halves(values[:, at : at + 1], values[:, at + 1 : at + 2], values.shape)
 
 
 def in_odd(scal, g, span):
@@ -369,18 +387,20 @@
     pl.when(core == 1)(functools.partial(run, False))
 
 
-def chip_kernel(scal, mine, theirs, out):
+def chip_kernel(scal, mine, theirs, out, keep_mine, keep_theirs):
     row, span = scal[17], scal[19]
     half = theirs.shape[0]
     js = 16
     base = 2 * js * LANES
     column = slice(base + 2 * LANES, base + 3 * LANES)
+    keep_mine[...] = mine[:, base : base + 3 * LANES]
+    keep_theirs[...] = theirs[:, base : base + 3 * LANES]
 
     def join(is_even):
         even, odd = (mine, theirs) if is_even else (theirs, mine)
         both, parts = pair_falls(even, odd, column)
         for j in range(js):
-            fall = jnp.exp(mm(parts, picker(32, j)))
+            fall = head_lanes(parts, 32, j)
             at = slice(j * LANES, (j + 1) * LANES)
             out[:, at] = even[:, at] + fall[0:1] * odd[:, at]
         fall = jnp.exp(halves(both[:, 0:1], both[:, 1:2], (8, LANES)))
@@ -406,36 +426,6 @@
     by_core(row, join)
 
 
-def spread_prompt_kernel(scal, got, mine, theirs, to_mine, to_other):
-    row, span = scal[17], scal[19]
-    js = 16
-    base = 2 * js * LANES
-    at0 = js * LANES
-    column = slice(base + 2 * LANES, base + 3 * LANES)
-
-    def split(is_even):
-        even, odd = (mine, theirs) if is_even else (theirs, mine)
-        to_even, to_odd = (to_mine, to_other) if is_even else (to_other, to_mine)
-        both, _ = pair_falls(even, odd, column)
-        fall = jnp.exp(halves(both[:, 0:1], both[:, 1:2], (8, LANES)))
-        start = got[:, at0 : at0 + LANES]
-        to_even[:, at0 : at0 + LANES] = start
-        to_odd[:, at0 : at0 + LANES] = even[:, base : base + LANES] + fall[0:1] * start
-        after = got[:, at0 + LANES : at0 + 2 * LANES]
-        end = odd[:, base + LANES : base + 2 * LANES] + fall[1:2] * after
-        for g in range(js):
-            gain = in_odd(scal, g, span).astype(F32) * reach_of(both[1:2], g)
-            grad = got[:, g * LANES : (g + 1) * LANES]
-            end = end + gain * grad
-        to_even[:, at0 + LANES : at0 + 2 * LANES] = end
-        to_odd[:, at0 + LANES : at0 + 2 * LANES] = after
-        for dst in (to_even, to_odd):
-            dst[:, :at0] = got[:, :at0]
-            dst[:, at0 + 2 * LANES :] = got[:, at0 + 2 * LANES : at0 + 9 * LANES]
-
-    by_core(row, split)
-
-
 def by_chip(row, pieces):
     chips = len(pieces)
     chip = lax.div(row, 2)
@@ -459,7 +449,7 @@
         to_even, to_odd = (to_mine, to_other) if is_even else (to_other, to_mine)
         _, parts = pair_falls(even, odd, column)
         for j in range(js):
-            fall = jnp.exp(mm(parts, picker(32, j)))
+            fall = head_lanes(parts, 32, j)
             at = slice(j * LANES, (j + 1) * LANES)
             start = got[:, (js + 9 + j) * LANES : (js + 10 + j) * LANES]
             to_even[:, at] = start
@@ -475,14 +465,14 @@
 def join_states_kernel(scal, mine, theirs, smine, stheirs, out):
     row = scal[17]
     js = 16
-    column = slice((2 * js + 2) * LANES, (2 * js + 3) * LANES)
+    column = slice(2 * LANES, 3 * LANES)
 
     def join(is_even):
         even, odd = (mine, theirs) if is_even else (theirs, mine)
         first, second = (smine, stheirs) if is_even else (stheirs, smine)
         _, parts = pair_falls(even, odd, column)
         for j in range(js):
-            fall = jnp.exp(mm(parts, picker(32, j)))
+            fall = head_lanes(parts, 32, j)
             at = slice(j * LANES, (j + 1) * LANES)
             out[:, at] = fall[1:2] * first[:, at] + second[:, at]
 
@@ -520,12 +510,13 @@
     cols[ns : 2 * ns, :] = c_col
     c_all = silu(c_col)
     misc = got[:, 0, base + 2 * LANES : base + 3 * LANES]
-    misc_parts = exact(misc)
-    log_parts = exact(early[0:8, ROW_STEP * LANES : (ROW_STEP + 1) * LANES])
+    falls_all = jnp.exp(misc)
+    token = early[0:8, ROW_STEP * LANES : (ROW_STEP + 1) * LANES]
+    token_falls = jnp.exp(token)
     for j in range(js):
         at = slice(j * LANES, (j + 1) * LANES)
-        fall = jnp.exp(mm(misc_parts, picker(32, j)))
-        falls = jnp.exp(mm(log_parts, picker(32, j)))
+        fall = head_lanes(falls_all, 32, j)
+        falls = head_lanes(token_falls, 32, j)
         a = jnp.zeros((ns, LANES), F32)
         for p in reversed(range(count)):
             aft[p, :, at] = a
@@ -575,15 +566,16 @@
     for piece, first_row in by_chip(row, (s0, s1, s2, s3)):
         states[pl.ds(first_row, ns), :] = piece[:, js * LANES :]
     misc = got[:, 0, base + 2 * LANES : base + 3 * LANES]
-    misc_parts = exact(misc)
-    log_parts = exact(early[0:8, ROW_STEP * LANES : (ROW_STEP + 1) * LANES])
+    falls_all = jnp.exp(misc)
+    token = early[0:8, ROW_STEP * LANES : (ROW_STEP + 1) * LANES]
+    token_falls = jnp.exp(token)
     sum_b = [jnp.zeros((ns, LANES), F32) for _ in range(3)]
     sum_c = [jnp.zeros((ns, LANES), F32) for _ in range(3)]
     for j in range(js):
         at = slice(j * LANES, (j + 1) * LANES)
-        fall = jnp.exp(mm(misc_parts, picker(32, j)))
-        falls = jnp.exp(mm(log_parts, picker(32, j)))
-        steps = mm(log_parts, picker(0, j))
+        fall = head_lanes(falls_all, 32, j)
+        falls = head_lanes(token_falls, 32, j)
+        steps = head_lanes(token, 0, j)
         seq = [moved[j, 2 * ns + r : 2 * ns + r + 1, :] for r in range(3)] + [
             early[j : j + 1, (ROW_X + s) * LANES : (ROW_X + s + 1) * LANES] for s in range(3)
         ]
@@ -658,43 +650,45 @@
 
 
 def inner_kernel(
-    scal, bx, bbc, bstep, blogs, bdy, rim, convx, convbc, skip,
+    scal, bx, bbc, rim, convx, convbc, skip, dys, table, wrow,
     smine, sother, yi, gi, rise,
-    xs, xt, ds, dys, bcs, wrow, out,
+    xs, xt, ds, bcs, out,
 ):
-    row, length = scal[17], scal[16]
+    row = scal[17]
     n, js = bx.shape[0], bx.shape[1]
     conv_branch(bx, rim, convx, xs, xt, ds)
-    live_dy(row, length, bdy, dys)
     taps = [convbc[i : i + 1, :] for i in range(4)]
     bc = silu(conv_rows(bbc[...], bc_halo(rim, 19), taps, bcs))
     b, c = bc[:, :STATE], bc[:, STATE:]
     b_t = left(b.T)
     scores = mm_nt(left(c), right_nt(b))
     scores_t = mm_nt(left(b), right_nt(c))
-    run = running_sum(without_first(row, blogs[...]))
-    wrow[...] = run
-    parts = exact(branch_table(without_first(row, bstep[...]), run))
     causal = iota((n, n), 0) >= iota((n, n), 1)
     causal_t = iota((n, n), 0) <= iota((n, n), 1)
     low = iota((n, LANES), 1) < HEAD_DIM
 
-    def head_pair(j, _):
+    runs = table[...]
+    fall = jnp.exp(runs[n - 1 : n, :] - runs)
+    faded = []
+    for j in range(js):
         at = pl.ds(j, n, stride=js)
-        steps = mm(parts, picker(0, j))
-        runs = mm(parts, picker(32, j))
+        steps = head_lanes(runs, 0, j)
         x_conv = xt[at, :]
         dy = dys[at, :]
-        gain = skip[pl.ds(j, 1), :]
+        gain = skip[j : j + 1, :]
         x_hat = x_conv * steps
         x_hi, x_lo = split2(x_hat)
         dy_b = dy.astype(BF16)
         zero = jnp.zeros_like(dy_b)
-        out[:, block(j)] = mm(b_t, right(x_hat * jnp.exp(runs[n - 1 : n, :] - runs)))
+        faded.append(x_hat * head_lanes(fall, 32, j))
+        if j % 2 == 1:
+            out[:, (j - 1) * LANES : (j + 1) * LANES] = mm(
+                b_t, right(jnp.concatenate(faded[-2:], axis=1))
+            )
         mix, mix_t = [], []
         for k in range(2):
-            down = jnp.broadcast_to(runs[:, k * HEAD_DIM : k * HEAD_DIM + 1], (n, n))
-            along = wrow[pl.ds(2 * j + k, 1), :]
+            down = jnp.broadcast_to(runs[:, 32 + 2 * j + k : 33 + 2 * j + k], (n, n))
+            along = wrow[2 * j + k : 2 * j + k + 1, :]
             mix.append(split2(jnp.exp(jnp.where(causal, down - along, -1e30)) * scores))
             mix_t.append(split2(jnp.exp(jnp.where(causal_t, along - down, -1e30)) * scores_t))
         x_blk = [jnp.where(low, x_hi, zero), jnp.where(low, zero, x_hi)]
@@ -711,42 +705,36 @@
         )
         slope = ds[at, :]
         gi[at, :] = (steps * g + gain * dy) * slope
-        rise[at, :] = steps * slope
-        return 0
-
-    lax.fori_loop(0, js, head_pair, 0, unroll=2)
+        rise[at, :] = steps * slope * head_lanes(fall, 32, j)
     for h, half_out in enumerate((smine, sother)):
         half_out[...] = out[part(h, row), :]
 
 
 def carry_kernel(
-    scal, bbc, bstep, blogs, rim, convx, convbc, yi, gi, rise,
-    rmine, rtheirs, fmine, ftheirs,
+    scal, bbc, rim, convx, convbc, yi, gi, rise, table, rows, fmine, ftheirs,
     by, bgx, last, rims,
-    xs, ys, bcs, rows, start, after,
+    xs, ys, bcs, start, after,
 ):
     row, length = scal[17], scal[16]
     n, js = by.shape[0], by.shape[1]
     core = lax.rem(row, 2)
     assemble(core, fmine, ftheirs, slice(0, js * LANES), start)
     assemble(core, fmine, ftheirs, slice(js * LANES, 2 * js * LANES), after)
-    first_rows(rmine, rtheirs, js, rows)
     taps = [convbc[i : i + 1, :] for i in range(4)]
     bc = silu(conv_rows(bbc[...], bc_halo(rim, 19), taps, bcs))
     b_l, c_l = left(bc[:, :STATE]), left(bc[:, STATE:])
-    run = running_sum(without_first(row, blogs[...]))
-    parts = exact(branch_table(without_first(row, bstep[...]), run))
     xs[n * js : (n + 8) * js, :] = jnp.zeros((8 * js, LANES), F32)
 
-    def head_pair(j, _):
-        at = pl.ds(j, n, stride=js)
-        runs = mm(parts, picker(32, j))
-        ys[at, :] = yi[at, :] + jnp.exp(runs) * mm(c_l, right(start[:, block(j)]))
-        fall = jnp.exp(runs[n - 1 : n, :] - runs)
-        xs[at, :] = gi[at, :] + rise[at, :] * fall * mm(b_l, right(after[:, block(j)]))
-        return 0
-
-    lax.fori_loop(0, js, head_pair, 0, unroll=4)
+    grown = jnp.exp(table[...])
+    for j in range(0, js, 2):
+        both = slice(j * LANES, (j + 2) * LANES)
+        y = mm(c_l, right(start[:, both]))
+        g = mm(b_l, right(after[:, both]))
+        for q in range(2):
+            at = pl.ds(j + q, n, stride=js)
+            half = slice(q * LANES, (q + 1) * LANES)
+            ys[at, :] = yi[at, :] + head_lanes(grown, 32, j + q) * y[:, half]
+            xs[at, :] = gi[at, :] + rise[at, :] * g[:, half]
 
     @pl.when(row == 0)
     def _():
@@ -778,48 +766,36 @@
         rims[m, 0:js, :] = g
 
 
-def prompt_kernel(
-    scal, px, pbc, pstep, plogs, pdy, rim, convx, convbc, skip, mine, theirs,
-    py, pgx, gbc, rims, forks,
-    pxs, pbcs, wexp, rows, dxh, dbs, got, tail,
+def prompt_inner_kernel(
+    scal, px, pbc, pdy, rim, convx, convbc, skip, tab, prun,
+    yp, gp, dbp, dcp, xh, xpre, bcpre, pxs, pbcs,
 ):
-    row, col = scal[17], scal[18]
-    span, js = px.shape[0], convx.shape[1]
-    base = js * LANES
-    core = lax.rem(row, 2)
-    assemble(core, mine, theirs, slice(0, base + 2 * LANES), got)
-    assemble(core, mine, theirs, slice(base + 8 * LANES, base + 9 * LANES), tail)
-    first_rows(mine, theirs, js, rows)
+    col = scal[18]
+    span = px.shape[0]
     taps = [convbc[i : i + 1, :] for i in range(4)]
-    fork_lead = [rows[:, (3 + s) * LANES : (4 + s) * LANES] for s in range(3)]
-    for m, g in enumerate(tail_grads(fork_lead, [convx[i] for i in range(4)])):
-        forks[m] = g
     own = [convx[i, pl.ds(col, 1), :] for i in range(4)]
     gain = skip[pl.ds(col, 1), :]
     x_pre = conv_rows(px[...], [rim[r, 16:17, :] for r in range(3)], own, pxs)
     bc_pre = conv_rows(pbc[...], bc_halo(rim, 17), taps, pbcs)
+    xpre[...] = x_pre
+    bcpre[...] = bc_pre
     x_p = silu(x_pre)
     bc_p = silu(bc_pre)
     b_p, c_p = bc_p[:, :STATE], bc_p[:, STATE:]
-    b_l, c_l = left(b_p), left(c_p)
-    scores = mm_nt(c_l, right_nt(b_p))
-    scores_t = mm_nt(b_l, right_nt(c_p))
-    prun = running_sum(plogs[...])
-    ptable = prompt_table(pstep[...], prun)
-    runs = halves(ptable[:, 0:1], ptable[:, 1:2], (span, LANES))
+    scores = mm_nt(left(c_p), right_nt(b_p))
+    scores_t = mm_nt(left(b_p), right_nt(c_p))
+    ptable = tab[...]
     steps = halves(ptable[:, 2:3], ptable[:, 3:4], (span, LANES))
-    wexp[...] = runs
     x_hat = x_p * steps
+    xh[...] = x_hat
     x_hi, x_lo = split2(x_hat)
     dy_b = pdy[...]
-    dy = dy_b.astype(F32)
     low = iota((span, LANES), 1) < HEAD_DIM
     zero = jnp.zeros_like(x_hi)
     causal = iota((span, span), 0) >= iota((span, span), 1)
     causal_t = iota((span, span), 0) <= iota((span, span), 1)
-    y = jnp.exp(runs) * mm(c_l, right(got[:, base : base + LANES])) + gain * x_p
-    after = right(got[:, base + LANES : base + 2 * LANES])
-    g = jnp.exp(runs[span - 1 : span, :] - runs) * mm(b_l, after)
+    y = gain * x_p
+    g = jnp.zeros((span, LANES), F32)
     d_s = jnp.zeros((span, span), F32)
     d_st = jnp.zeros((span, span), F32)
     for k in range(2):
@@ -840,17 +816,67 @@
         x_two = jnp.concatenate([x_hi, x_lo], 1)
         d_s = d_s + decay * mm_nt(d_two, x_two)
         d_st = d_st + decay_t * mm_nt(x_two, d_two)
-    py[...] = y.astype(BF16)
-    d_c = mm(left(d_s), right(b_p)) + mm_nt(
-        left(jnp.exp(runs) * dy), right_nt(got[:, base : base + LANES])
-    )
-    d_b = mm(left(d_st), right(c_p)) + mm_nt(
-        left(jnp.exp(runs[span - 1 : span, :] - runs) * x_hat),
-        right_nt(got[:, base + LANES : base + 2 * LANES]),
-    )
-    dxh[...] = g
-    dbs[...] = d_b
-    pxs[0:span, :] = x_hat
+    yp[...] = y
+    gp[...] = g
+    dcp[...] = mm(left(d_s), right(b_p))
+    dbp[...] = mm(left(d_st), right(c_p))
+
+
+def prompt_kernel(
+    scal, pdy, convx, convbc, skip, tab, yp, gp, dbp, dcp, xh, xpre, bcpre,
+    mine, theirs, keep_mine, keep_theirs, keep_far,
+    py, pgx, msg, rims, rows,
+    pxs, pbcs, wexp, dxh, dbs, got, tail, near,
+):
+    row, col = scal[17], scal[18]
+    span, js = pdy.shape[0], convx.shape[1]
+    base = js * LANES
+    core = lax.rem(row, 2)
+    assemble(core, mine, theirs, slice(0, base + 2 * LANES), got)
+    assemble(core, mine, theirs, slice(base + 8 * LANES, base + 9 * LANES), tail)
+    near[part(0, row), :] = keep_theirs[...]
+    near[part(1, row), :] = keep_far[...]
+    first_rows(mine, theirs, js, rows)
+    mark = keep_theirs[0:1, 2 * LANES : 3 * LANES]
+    fall = jnp.exp(halves(mark[:, 0:1], mark[:, 1:2], (1, LANES)))
+    begin, end = slice(base, base + LANES), slice(base + LANES, base + 2 * LANES)
+
+    @pl.when(core == 1)
+    def _():
+        got[:, begin] = near[:, :LANES] + fall * got[:, begin]
+
+    @pl.when(core == 0)
+    def _():
+        got[:, end] = near[:, LANES : 2 * LANES] + fall * got[:, end]
+        for g in range(js):
+
+            @pl.when(in_odd(scal, g, span))
+            def _():
+                got[:, end] += reach_of(mark, g) * got[:, g * LANES : (g + 1) * LANES]
+
+    taps_x = [convx[i] for i in range(4)]
+    fork_lead = [rows[:, (3 + s) * LANES : (4 + s) * LANES] for s in range(3)]
+    chunk = span // js
+    for m, v in enumerate(tail_grads(fork_lead, taps_x)):
+        for q in range(js):
+            msg[q, 2 * chunk + m : 2 * chunk + m + 1, :] = v[q : q + 1]
+    taps = [convbc[i : i + 1, :] for i in range(4)]
+    own = [convx[i, pl.ds(col, 1), :] for i in range(4)]
+    gain = skip[pl.ds(col, 1), :]
+    x_hat = xh[...]
+    bc_p = silu(bcpre[...])
+    b_l, c_l = left(bc_p[:, :STATE]), left(bc_p[:, STATE:])
+    ptable = tab[...]
+    runs = halves(ptable[:, 0:1], ptable[:, 1:2], (span, LANES))
+    steps = halves(ptable[:, 2:3], ptable[:, 3:4], (span, LANES))
+    wexp[...] = runs
+    dy = pdy[...].astype(F32)
+    grown = jnp.exp(runs)
+    rest = jnp.exp(runs[span - 1 : span, :] - runs)
+    py[...] = (yp[...] + grown * mm(c_l, right(got[:, begin]))).astype(BF16)
+    dxh[...] = gp[...] + rest * mm(b_l, right(got[:, end]))
+    d_c = dcp[...] + mm_nt(left(grown * dy), right_nt(got[:, begin]))
+    dbs[...] = dbp[...] + mm_nt(left(rest * x_hat), right_nt(got[:, end]))
 
     def fork(q, _):
         where = scal[q] - 1 - row * span
@@ -861,18 +887,17 @@
             u = jnp.exp(jnp.where(iota((span, LANES), 0) <= where, gap, -1e30))
             grad = got[:, block(q)]
             dxh[...] += u * mm(b_l, right(grad))
-            dbs[...] += mm_nt(left(u * pxs[0:span, :]), right_nt(grad))
+            dbs[...] += mm_nt(left(u * xh[...]), right_nt(grad))
 
         return 0
 
     lax.fori_loop(0, js, fork, 0)
-    pre_g = (steps * dxh[...] + gain * dy) * silu_slope(x_pre)
-    pxs[0:span, :] = pre_g
+    pxs[0:span, :] = (steps * dxh[...] + gain * dy) * silu_slope(xpre[...])
     pxs[span : span + 8, :] = jnp.zeros((8, LANES), F32)
     pgx[...] = sum(own[i] * pxs[3 - i : 3 - i + span, :] for i in range(4))
     for m, v in enumerate(tail_grads([pxs[s : s + 1, :] for s in range(3)], own)):
         rims[m, 0:1, :] = v
-    pbcs[0:span, :] = jnp.concatenate([dbs[...], d_c], axis=1) * silu_slope(bc_pre)
+    pbcs[0:span, :] = jnp.concatenate([dbs[...], d_c], axis=1) * silu_slope(bcpre[...])
     pbcs[span : span + 8, :] = jnp.zeros((8, 2 * STATE), F32)
     grad = sum(taps[i] * pbcs[3 - i : 3 - i + span, :] for i in range(4))
     for m, v in enumerate(tail_grads([pbcs[s : s + 1, :] for s in range(3)], taps)):
@@ -881,33 +906,28 @@
     spot = iota((span, LANES), 0) - (scal[20] - 3 - row * span)
     lane = iota((span, LANES), 1)
     tails = exact(tail[...])
-    into = []
     for half in range(2):
         hit = ((spot >= 0) & (spot < 3) & (lane == spot + 3 * half)).astype(F32).astype(BF16)
-        into.append(mm_nt(jnp.concatenate([hit, hit, hit], 1), tails))
-    gbc[...] = grad + jnp.concatenate(into, axis=1)
-
-
-def packing_kernel(pgx, gbc, back, forks, msg, out):
-    span, peers = pgx.shape[0], msg.shape[0]
-    rows = span // peers
-    out[...] = pgx[...]
+        into = mm_nt(jnp.concatenate([hit, hit, hit], 1), tails)
+        total = grad[:, half * STATE : (half + 1) * STATE] + into
+        for q in range(js):
+            msg[q, half * chunk : (half + 1) * chunk, :] = total[
+                q * chunk : (q + 1) * chunk
+            ]
+    for q in range(js):
+        msg[q, 2 * chunk + 3 : 2 * chunk + 8, :] = jnp.zeros((5, LANES), F32)
+
+
+def rim_kernel(msg, back, out):
+    rows = (msg.shape[1] - 8) // 2
+    out[...] = msg[...]
     for m in range(3):
-        at = slice(span - 3 + m, span - 2 + m)
-        out[at, :] = pgx[at, :] + back[m, 0:1, :]
-    for q in range(peers):
-        msg[q, 0:rows, :] = gbc[q * rows : (q + 1) * rows, :STATE]
-        msg[q, rows : 2 * rows, :] = gbc[q * rows : (q + 1) * rows, STATE:]
-        for m in range(3):
-            msg[q, 2 * rows + m : 2 * rows + m + 1, :] = forks[m, q : q + 1, :]
-        msg[q, 2 * rows + 3 : 2 * rows + 8, :] = jnp.zeros((5, LANES), F32)
-    for m in range(3):
-        at = rows - 3 + m
-        msg[peers - 1, at : at + 1, :] += back[m, 1:2, :]
-        msg[peers - 1, rows + at : rows + at + 1, :] += back[m, 2:3, :]
-
-
-def finish_kernel(scal, pgx, got, out_x, out_bc, tails):
+        for half in range(2):
+            at = (half + 1) * rows - 3 + m
+            out[0, at : at + 1, :] = msg[0, at : at + 1, :] + back[m, 1 + half : 2 + half, :]
+
+
+def finish_kernel(scal, pgx, back, got, out_x, out_bc, tails):
     row = scal[17]
     span, peers = pgx.shape[0], got.shape[0]
     rows = span // peers
@@ -925,21 +945,32 @@
         spot = jnp.where((lane >= 8 * g) & (lane < 8 * g + 3), where, spot)
     hit = (iota((span, LANES), 0) == spot).astype(F32).astype(BF16)
     into = mm(jnp.concatenate([hit, hit, hit], 1), jnp.concatenate(split3(tails[...]), 0))
-    out_x[...] = (pgx[...] + into).astype(BF16)
-
-
-def call(kernel, args, outs, scratch, scalars=1, flops=10**9, blocks=None, out_smem=0):
+    total = pgx[...] + into
+    where = iota((span, LANES), 0)
+    for m in range(3):
+        total = total + jnp.where(where == span - 3 + m, back[m, 0:1, :], 0.0)
+    out_x[...] = total.astype(BF16)
+
+
+def call(
+    kernel, args, outs, scratch, scalars=1, flops=10**9, blocks=None, out_smem=0,
+    out_blocks=None, aliases=None,
+):
     vmem = pl.BlockSpec(memory_space=pltpu.VMEM)
     smem = pl.BlockSpec(memory_space=pltpu.SMEM)
     given = [smem] * scalars + [vmem] * (len(args) - scalars)
     for at, spec in (blocks or {}).items():
         given[at] = spec
+    taken = [smem] * out_smem + [vmem] * (len(outs) - out_smem)
+    for at, spec in (out_blocks or {}).items():
+        taken[at] = spec
     return pl.pallas_call(
         kernel,
         grid=(1,) if blocks else (),
         out_shape=[jax.ShapeDtypeStruct(s, d) for s, d in outs],
         in_specs=given,
-        out_specs=[smem] * out_smem + [vmem] * (len(outs) - out_smem),
+        out_specs=taken,
+        input_output_aliases=aliases or {},
         scratch_shapes=[pltpu.VMEM(s, F32) for s in scratch],
         compiler_params=pltpu.CompilerParams(vmem_limit_bytes=VMEM_LIMIT),
         cost_estimate=pl.CostEstimate(flops=flops, bytes_accessed=10**6, transcendentals=0),
@@ -1030,34 +1061,61 @@
     def between_chips(v):
         return lax.all_to_all(v, "prefix", 0, 0, axis_index_groups=columns, tiled=True)
 
+    with jax.named_scope("early"):
+        early_part, dys, table, run, tab, prun = call(
+            early_kernel,
+            [scal, px, pbc, pstep, plogs, bx, bbc, step, logs, bdy],
+            [
+                ((js, EARLY * LANES), F32),
+                (big, F32),
+                ((n, LANES), F32),
+                ((heads, n), F32),
+                ((span, LANES), F32),
+                ((2, span), F32),
+            ],
+            [],
+            blocks={
+                5: pl.BlockSpec((16, js, LANES), lambda i: (0, 0, 0)),
+                6: pl.BlockSpec((16, 2 * STATE), lambda i: (0, 0)),
+            },
+        )
     width = (2 * js + 3 + EARLY) * LANES
     with jax.named_scope("lead"):
         mine, other = call(
             lead_kernel,
-            [scal, px, pbc, pstep, plogs, pdy, bx, bbc, step, logs, bdy, rim, convx, convbc],
+            [
+                scal, px, pbc, pdy, bbc, rim, convx, convbc, early_part, dys, table, tab,
+            ],
             [((half, width), F32)] * 2,
             [
-                big, (n + 8, 2 * STATE), (span + 8, LANES), (span + 8, 2 * STATE),
-                (span, LANES), (span, LANES), (js, EARLY * LANES), (STATE, (2 * js + 3) * LANES),
+                (n + 8, 2 * STATE), (span + 8, LANES), (span + 8, 2 * STATE),
+                (span, LANES), (STATE, (2 * js + 3) * LANES),
             ],
         )
     theirs = across(other)
     with jax.named_scope("chip"):
-        (joined,) = call(chip_kernel, [scal, mine, theirs], [((half, width), F32)], [])
+        joined, keep_mine, keep_theirs = call(
+            chip_kernel,
+            [scal, mine, theirs],
+            [((half, width), F32)] + [((half, 3 * LANES), F32)] * 2,
+            [],
+        )
     got = between_chips(joined.reshape(chips, ns, width))
     with jax.named_scope("inner"):
         smine, sother, yi, gi, rise = call(
             inner_kernel,
-            [scal, bx, bbc, step, logs, bdy, rim, convx, convbc, skip],
+            [scal, bx, bbc, rim, convx, convbc, skip, dys, table, run],
             [(each, F32)] * 2 + [(big, F32)] * 3,
-            [tall, big, big, big, (n + 8, 2 * STATE), (heads, n), (STATE, js * LANES)],
+            [tall, big, big, (n + 8, 2 * STATE), (STATE, js * LANES)],
             flops=10**10,
         )
     stheirs = across(sother)
+    keep_far = across(keep_mine)
     with jax.named_scope("join_states"):
         (sjoined,) = call(
-            join_states_kernel, [scal, mine, theirs, smine, stheirs], [(each, F32)], []
-        )
+            join_states_kernel, [scal, keep_mine, keep_theirs, smine, stheirs], [(each, F32)], []
+        )
+    got, keep_far = lax.optimization_barrier((got, keep_far))
     with jax.named_scope("slices"):
         msg, adj, pst, cols, early, *ablocks = call(
             slice_kernel,
@@ -1083,14 +1141,20 @@
             [((chips, ns, width3 + js * LANES), F32)],
             [(js, 6 * LANES), (chips, ns, LANES), each],
         )
+    msg3, tab3 = lax.optimization_barrier((msg3, tab))
     got3 = between_chips(msg3).reshape(half, width3 + js * LANES)
-    with jax.named_scope("spread_prompt"):
-        rmine, rother = call(
-            spread_prompt_kernel,
-            [scal, got3, mine, theirs],
-            [((half, width3), F32)] * 2,
-            [],
-        )
+    narrow = ((span, LANES), F32)
+    wide2 = ((span, 2 * STATE), F32)
+    with jax.named_scope("prompt_inner"):
+        inner_parts = call(
+            prompt_inner_kernel,
+            [scal, px, pbc, pdy, rim, convx, convbc, skip, tab3, prun],
+            [narrow] * 6 + [wide2],
+            [(span + 8, LANES), (span + 8, 2 * STATE)],
+            flops=10**10,
+        )
+    got3, *inner_parts = lax.optimization_barrier((got3, *inner_parts))
+    theirs3 = across(got3)
     both = (half, 2 * js * LANES)
     with jax.named_scope("spread_branch"):
         fmine, fother = call(
@@ -1099,42 +1163,49 @@
             [(both, F32)] * 2,
             [each],
         )
-    rtheirs = across(rother)
-    rtheirs, fother = lax.optimization_barrier((rtheirs, fother))
+    theirs3, fother = lax.optimization_barrier((theirs3, fother))
     ftheirs = across(fother)
+    peers = (js, 2 * span // js + 8, LANES)
     with jax.named_scope("prompt"):
-        py, pgx, gbc, prims, fork_grads = call(
+        py, pgx, out_msg, prims, rows = call(
             prompt_kernel,
-            [scal, px, pbc, pstep, plogs, pdy, rim, convx, convbc, skip, rmine, rtheirs],
+            [
+                scal, pdy, convx, convbc, skip, tab, *inner_parts,
+                got3, theirs3, keep_mine, keep_theirs, keep_far,
+            ],
             [
                 ((span, LANES), BF16),
-                ((span, LANES), F32),
-                ((span, 2 * STATE), F32),
+                narrow,
+                (peers, F32),
                 ((3, 3, LANES), F32),
-                ((3, js, LANES), F32),
+                ((js, 6 * LANES), F32),
             ],
             [
-                (span + 8, LANES), (span + 8, 2 * STATE), (span, LANES), (js, 6 * LANES),
+                (span + 8, LANES), (span + 8, 2 * STATE), (span, LANES),
                 (span, LANES), (span, STATE), (STATE, (js + 2) * LANES), (STATE, LANES),
+                (STATE, 3 * LANES),
             ],
         )
     backward = [(i, i - 1) for i in range(1, count)]
     pback = lax.ppermute(prims, "prefix", backward)
-    with jax.named_scope("packing"):
-        out_msg, pgx = call(
-            packing_kernel,
-            [pgx, gbc, pback, fork_grads],
-            [((js, 2 * span // js + 8, LANES), F32), ((span, LANES), F32)],
+    final = pl.BlockSpec((1,) + peers[1:], lambda i: (js - 1, 0, 0))
+    with jax.named_scope("rim"):
+        (out_msg,) = call(
+            rim_kernel,
+            [out_msg, pback],
+            [(peers, F32)],
             [],
             scalars=0,
+            blocks={0: final},
+            out_blocks={0: final},
+            aliases={0: 0},
         )
     end = lax.all_to_all(out_msg, "branch", 0, 0, tiled=True)
     with jax.named_scope("carry"):
         by, bgx, last, brims = call(
             carry_kernel,
             [
-                scal, bbc, step, logs, rim, convx, convbc, yi, gi, rise,
-                rmine, rtheirs, fmine, ftheirs,
+                scal, bbc, rim, convx, convbc, yi, gi, rise, table, rows, fmine, ftheirs,
             ],
             [
                 ((n, js, LANES), BF16),
@@ -1143,8 +1214,7 @@
                 ((3, js, LANES), F32),
             ],
             [
-                tall, big, (n + 8, 2 * STATE), (js, 6 * LANES),
-                (STATE, js * LANES), (STATE, js * LANES),
+                tall, big, (n + 8, 2 * STATE), (STATE, js * LANES), (STATE, js * LANES),
             ],
             flops=10**10,
         )
@@ -1153,7 +1223,7 @@
     with jax.named_scope("finish"):
         prompt_gx, prompt_gbc = call(
             finish_kernel,
-            [scal, pgx, end],
+            [scal, pgx, pback, end],
             [((span, LANES), BF16), ((span // js, 2 * STATE), BF16)],
             [(LANES, LANES)],
         )

time: 183 us -> 172 us (0.940)
  blocking collectives: 21.3 us -> 0 us
  waiting for transfers between devices: 27.9 us -> 41.2 us
  Pallas kernels: 64.7 us -> 54.1 us
  starting transfers between devices: 58.2 us -> 65.3 us
    all_to_all x1 -> x0, blocking collectives: 21.3 us -> none  [between_chips(): lax.all_to_all(v, 'prefix', 0, 0, axis_index_groups=columns, tiled=True)]
    all_to_all x1 -> x2, waiting for transfers between devices: 0.01 us -> 15.7 us  [between_chips(): lax.all_to_all(v, 'prefix', 0, 0, axis_index_groups=columns, tiled=True)]
    pallas_call x13 -> x14, Pallas kernels: 64.7 us -> 54.1 us  [call(): pl.pallas_call(kernel, grid=(1,) if blocks else (), out_shape=[jax.ShapeD...]
    ppermute x4 -> x5, starting transfers between devices: 10.6 us -> 16 us  [across(): return lax.ppermute(v, 'prefix', cores)]
    all_to_all x1 -> x2, starting transfers between devices: 3.56 us -> 8.13 us  [between_chips(): lax.all_to_all(v, 'prefix', 0, 0, axis_index_groups=columns, tiled=True)]
    ppermute x3, starting transfers between devices: 11 us -> 8.41 us  [round_chips(): moved_on.append(lax.ppermute(blocks[d], 'prefix', pairs))]
    ppermute x1, waiting for transfers between devices: 3.87 us -> 1.3 us  [shards(): rim = lax.ppermute(rim, 'prefix', [(i, i + 1) for i in range(count - 1)])]
    ppermute x4 -> x5, waiting for transfers between devices: 5.48 us -> 3.14 us  [across(): return lax.ppermute(v, 'prefix', cores)]
  transfers between devices with their start and end apart: 13 -> 15, of which waited for: 9 -> 10; matrix products, arithmetic and copies ran while one was open for 1% -> 1% of each run, Pallas kernels for 20% -> 20%
where the time goes in v2:
time: 172 us; the launch traced here: 170 us
  starting transfers between devices  65.3 us (38%)
  Pallas kernels  54.1 us (31%)
  waiting for transfers between devices  41.2 us (24%)
  local copies, waits for them, and re-layouts  7.39 us (4%)
    pallas_call x14, Pallas kernels, call(): pl.pallas_call(kernel, grid=(1,) if blocks else (), out_shape=[jax.ShapeD...  54.1 us
    ppermute x5, starting transfers between devices, across(): return lax.ppermute(v, 'prefix', cores)  16 us
    all_to_all x2, waiting for transfers between devices, between_chips(): lax.all_to_all(v, 'prefix', 0, 0, axis_index_groups=columns, tiled=True)  15.7 us
    all_to_all x1, starting transfers between devices, shards(): moved = lax.all_to_all(msg, 'branch', 0, 0, tiled=True)  12 us
    all_to_all x1, starting transfers between devices, shards(): end = lax.all_to_all(out_msg, 'branch', 0, 0, tiled=True)  11.1 us
    ppermute x3, waiting for transfers between devices, round_chips(): moved_on.append(lax.ppermute(blocks[d], 'prefix', pairs))  10.1 us
    ppermute x3, starting transfers between devices, round_chips(): moved_on.append(lax.ppermute(blocks[d], 'prefix', pairs))  8.41 us
    all_to_all x2, starting transfers between devices, between_chips(): lax.all_to_all(v, 'prefix', 0, 0, axis_index_groups=columns, tiled=True)  8.13 us
  transfers between devices with their start and end apart: 15, of which 10 were waited for; matrix products, arithmetic and copies ran while one was open for 1% of the time, Pallas kernels for 20%

profile of v2, /device:TPU:1, one launch (start us, length us, event | category | flops | bytes accessed | tf_op | source)
XLA Modules:
  0.0 170.2 jit_solution(9869961441224156852)
XLA Ops:
  0.6 2.2 %setup.1 = (s32[24]{0:T(128)}, f32[3,21,128]{2,1,0:T(8,128)}, f32[32,128]{1,0:T(8,128)}, f32[32,128]{1,0:T(8,128)}, f32[2,256]{1,0:T(2,128)}, /*index=5*/f32[2,256]{1,0:T(2,128)}, f32[16,128]{1,0:T(8,128)}) custom-call(s32[16]{0:T(128)} %forks.1, s32[16]{0:T(128)} %lengths.1, s32[16]{0:T(128)} %holder.1, bf16[128,16,128]{2,1,0:T(8,128)(2,1)} %bitcast.55, ...), custom_call_target="tpu_custom_call" | custom-call | flops 1000000000 | bytes 1000000 | tf_op jit(solution)/shard_map/setup/pallas_call | solution.py:967
  2.8 4.6 %collective-permute-start = (f32[3,21,128]{2,1,0:T(8,128)}, f32[3,21,128]{2,1,0:T(8,128)S(1)}, u32[]{:S(2)}, u32[]{:S(2)}) collective-permute-start(f32[3,21,128]{2,1,0:T(8,128)} %get-tuple-element.95), channel_id=1, source_target_pairs={{0,64},{64,128},{128,192},{192,256},{256,320},{320,384},{384,448},... | collective-permute-start | bytes 96776 | tf_op jit(solution)/shard_map/ppermute | solution.py:1045
  7.4 2.5 %early.1 = (f32[16,1408]{1,0:T(8,128)}, f32[2048,128]{1,0:T(8,128)}, f32[128,128]{1,0:T(8,128)}, f32[32,128]{1,0:T(8,128)}, f32[256,128]{1,0:T(8,128)}, /*index=5*/f32[2,256]{1,0:T(2,128)}) custom-call(s32[24]{0:T(128)} %get-tuple-element.88.scal, bf16[256,128]{1,0:T(8,128)(2,1)} %bitcast.65, bf16[256,256]{1,0:T(8,128)(2,1)} %bitcast.61, ...), custom_call_target="tpu_custom_call" | custom-call | flops 1000000000 | bytes 1000000 | tf_op jit(solution)/shard_map/early/pallas_call | solution.py:967
  12.5 5.4 %lead.1 = (f32[64,5888]{1,0:T(8,128)}, f32[64,5888]{1,0:T(8,128)}) custom-call(s32[24]{0:T(128)} %get-tuple-element.88.scal, bf16[256,128]{1,0:T(8,128)(2,1)} %bitcast.66, bf16[256,256]{1,0:T(8,128)(2,1)} %bitcast.62, bf16[256,128]{1,0:T(8,128)(2,1)} %bitcast.45, bf16[128,256]{1,0:T(8,128)(2,1)} %bitcast.70, f32[3,21,128]{2,1,0:T(8,128)} %copy-done.14, ...), custom_call_target="tpu_custom_call" | custom-call | flops 1000000000 | bytes 1000000 | tf_op jit(solution)/shard_map/lead/pallas_call | solution.py:967
  17.9 4.6 %collective-permute-start.1 = (f32[64,5888]{1,0:T(8,128)}, f32[64,5888]{1,0:T(8,128)S(1)}, u32[]{:S(2)}, u32[]{:S(2)}) collective-permute-start(f32[64,5888]{1,0:T(8,128)} %get-tuple-element.100), channel_id=1, source_target_pairs={{0,64},{64,0},{128,192},{192,128},{256,320},{320,256},{384,448},{4... | collective-permute-start | bytes 4521992 | tf_op jit(solution)/shard_map/ppermute | solution.py:1052
  22.5 3.1 %collective-permute-done.1.theirs = f32[64,5888]{1,0:T(8,128)S(1)} collective-permute-done((f32[64,5888]{1,0:T(8,128)}, f32[64,5888]{1,0:T(8,128)S(1)}, u32[]{:S(2)}, u32[]{:S(2)}) %collective-permute-start.1) | collective-permute-done | bytes 1507360 | tf_op jit(solution)/shard_map/ppermute | solution.py:1052
  26.8 3.3 %chip.1 = (f32[64,5888]{1,0:T(8,128)}, f32[64,384]{1,0:T(8,128)}, f32[64,384]{1,0:T(8,128)}) custom-call(s32[24]{0:T(128)} %get-tuple-element.88.scal, f32[64,5888]{1,0:T(8,128)} %get-tuple-element.99.mine, f32[64,5888]{1,0:T(8,128)} %copy-done.2), custom_call_target="tpu_custom_call" | custom-call | flops 1000000000 | bytes 1000000 | tf_op jit(solution)/shard_map/chip/pallas_call | solution.py:967
  30.1 3.6 %all-to-all-start = ((f32[4,16,5888]{2,1,0:T(8,128)}), f32[4,16,5888]{2,1,0:T(8,128)S(1)}, u32[]{:S(2)}, u32[]{:S(2)}) async-start(f32[4,16,5888]{2,1,0:T(8,128)} %bitcast.38), calls=%async_computation | async-start | bytes 3014656 | tf_op jit(solution)/shard_map/all_to_all | solution.py:1062
  33.6 9.4 %inner.1 = (f32[64,2048]{1,0:T(8,128)}, f32[64,2048]{1,0:T(8,128)}, f32[2048,128]{1,0:T(8,128)}, f32[2048,128]{1,0:T(8,128)}, f32[2048,128]{1,0:T(8,128)}) custom-call(s32[24]{0:T(128)} %get-tuple-element.88.scal, bf16[128,16,128]{2,1,0:T(8,128)(2,1)} %bitcast.57, bf16[128,256]{1,0:T(8,128)(2,1)} %bitcast.71, f32[3,21,128]{2,1,0:T(8,128)} %copy-done.14, ...), custom_call_target="tpu_custom_call" | custom-call | flops 10000000000 | bytes 1000000 | tf_op jit(solution)/shard_map/inner/pallas_call | solution.py:967
  43.0 2.3 %collective-permute-start.3 = (f32[64,2048]{1,0:T(8,128)}, f32[64,2048]{1,0:T(8,128)S(1)}, u32[]{:S(2)}, u32[]{:S(2)}) collective-permute-start(f32[64,2048]{1,0:T(8,128)} %get-tuple-element.107), channel_id=1, source_target_pairs={{0,64},{64,0},{128,192},{192,128},{256,320},{320,256},{384,448},{4... | collective-permute-start | bytes 1572872 | tf_op jit(solution)/shard_map/ppermute | solution.py:1052
  45.3 2.0 %collective-permute-start.2 = (f32[64,384]{1,0:T(8,128)S(1)}, f32[64,384]{1,0:T(8,128)S(1)}, u32[]{:S(2)}, u32[]{:S(2)}) collective-permute-start(f32[64,384]{1,0:T(8,128)S(1)} %copy-done.10), channel_id=1, source_target_pairs={{0,64},{64,0},{128,192},{192,128},{256,320},{320,256},{384,448},{4... | collective-permute-start | bytes 294920 | tf_op jit(solution)/shard_map/ppermute | solution.py:1052
  48.2 2.3 %join_states.1.joined = f32[64,2048]{1,0:T(8,128)} custom-call(s32[24]{0:T(128)} %get-tuple-element.88.scal, f32[64,384]{1,0:T(8,128)} %get-tuple-element.102.mine.keep_mine, f32[64,384]{1,0:T(8,128)} %get-tuple-element.104.theirs.keep_theirs, f32[64,2048]{1,0:T(8,128)} %get-tuple-element.106.smine, f32[64,2048]{1,0:T(8,128)} %copy-done.8), custom_call_target="tpu_custom_call" | custom-call | flops 1000000000 | bytes 1000000 | tf_op jit(solution)/shard_map/join_states/pallas_call | solution.py:967
  50.5 2.9 %all-to-all-done.got = f32[4,16,5888]{2,1,0:T(8,128)S(1)} async-done(((f32[4,16,5888]{2,1,0:T(8,128)}), f32[4,16,5888]{2,1,0:T(8,128)S(1)}, u32[]{:S(2)}, u32[]{:S(2)}) %all-to-all-start) | async-done | bytes 1507360 | tf_op jit(solution)/shard_map/all_to_all | solution.py:1062
  54.5 3.2 %slices.1 = (f32[16,40,128]{2,1,0:T(8,128)}, f32[3,16,2048]{2,1,0:T(8,128)}, f32[4,16,128]{2,1,0:T(8,128)}, f32[32,128]{1,0:T(8,128)}, f32[16,1408]{1,0:T(8,128)...) custom-call(s32[24]{0:T(128)} %get-tuple-element.88.scal, ...), custom_call_target="tpu_custom_call" | custom-call | flops 1000000000 | bytes 1000000 | tf_op jit(solution)/shard_map/slices/pallas_call | solution.py:967
  57.7 12.0 %all-to-all-start.1 = ((f32[16,40,128]{2,1,0:T(8,128)}), f32[16,40,128]{2,1,0:T(8,128)S(1)}, u32[]{:S(2)}, u32[]{:S(2)}) async-start(f32[16,40,128]{2,1,0:T(8,128)} %get-tuple-element.108), calls=%async_computation.1 | async-start | bytes 655360 | tf_op jit(solution)/shard_map/all_to_all | solution.py:1133
  69.7 2.2 %collective-permute-start.4 = (f32[16,4096]{1,0:T(8,128)}, f32[16,4096]{1,0:T(8,128)S(1)}, u32[]{:S(2)}, u32[]{:S(2)}) collective-permute-start(f32[16,4096]{1,0:T(8,128)} %get-tuple-element.110), channel_id=1, source_target_pairs={{0,128},{64,192},{128,256},{192,320},{256,384},{320,448},{384,0},{... | collective-permute-start | bytes 786440 | tf_op jit(solution)/shard_map/ppermute | solution.py:1058
  71.9 3.7 %collective-permute-start.5 = (f32[16,4096]{1,0:T(8,128)}, f32[16,4096]{1,0:T(8,128)S(1)}, u32[]{:S(2)}, u32[]{:S(2)}) collective-permute-start(f32[16,4096]{1,0:T(8,128)} %get-tuple-element.111), channel_id=1, source_target_pairs={{0,256},{64,320},{128,384},{192,448},{256,0},{320,64},{384,128},{4... | collective-permute-start | bytes 786440 | tf_op jit(solution)/shard_map/ppermute | solution.py:1058
  75.6 2.5 %collective-permute-start.6 = (f32[16,4096]{1,0:T(8,128)}, f32[16,4096]{1,0:T(8,128)S(1)}, u32[]{:S(2)}, u32[]{:S(2)}) collective-permute-start(f32[16,4096]{1,0:T(8,128)} %get-tuple-element.112), channel_id=1, source_target_pairs={{0,384},{64,448},{128,0},{192,64},{256,128},{320,192},{384,256},{4... | collective-permute-start | bytes 786440 | tf_op jit(solution)/shard_map/ppermute | solution.py:1058
  79.9 4.5 %collective-permute-done.5.s2.p2 = f32[16,4096]{1,0:T(8,128)S(1)} collective-permute-done((f32[16,4096]{1,0:T(8,128)}, f32[16,4096]{1,0:T(8,128)S(1)}, u32[]{:S(2)}, u32[]{:S(2)}) %collective-permute-start.5) | collective-permute-done | bytes 262176 | tf_op jit(solution)/shard_map/ppermute | solution.py:1058
  84.3 3.9 %collective-permute-done.6.s3.p3 = f32[16,4096]{1,0:T(8,128)S(1)} collective-permute-done((f32[16,4096]{1,0:T(8,128)}, f32[16,4096]{1,0:T(8,128)S(1)}, u32[]{:S(2)}, u32[]{:S(2)}) %collective-permute-start.6) | collective-permute-done | bytes 262176 | tf_op jit(solution)/shard_map/ppermute | solution.py:1058
  89.0 4.1 %chains.1 = f32[4,16,5248]{2,1,0:T(8,128)} custom-call(s32[24]{0:T(128)} %get-tuple-element.88.scal, f32[4,16,5888]{2,1,0:T(8,128)} %copy-done.1, f32[16,40,128]{2,1,0:T(8,128)} %copy-done.4, f32[16,4096]{1,0:T(8,128)} %get-tuple-element.114.s0.p0, f32[16,4096]{1,0:T(8,128)} %copy-done.5, f32[16,4096]{1,0:T(8,128)} %copy-done.6, f32[16,4096]{1,0:T(8,128)} %copy-done.7, ...), custom_call_target="tpu_custom_call" | custom-call | flops 1000000000 | bytes 1000000 | tf_op jit(solution)/shard_map/chains/pallas_call | solution.py:967
  93.2 4.6 %all-to-all-start.2 = ((f32[4,16,5248]{2,1,0:T(8,128)}), f32[4,16,5248]{2,1,0:T(8,128)S(1)}, u32[]{:S(2)}, u32[]{:S(2)}) async-start(f32[4,16,5248]{2,1,0:T(8,128)} %chains.1), calls=%async_computation.2 | async-start | bytes 2686976 | tf_op jit(solution)/shard_map/all_to_all | solution.py:1062
  97.7 3.2 %prompt_inner.1 = (f32[256,128]{1,0:T(8,128)}, f32[256,128]{1,0:T(8,128)}, f32[256,128]{1,0:T(8,128)}, f32[256,128]{1,0:T(8,128)}, f32[256,128]{1,0:T(8,128)}, /*index=5*/f32[256,128]{1,0:T(8,128)}, f32[256,256]{1,0:T(8,128)}) custom-call(s32[24]{0:T(128)} %get-tuple-element.88.scal, bf16[256,128]{1,0:T(8,128)(2,1)} %bitcast.67, bf16[256,256]{1,0:T(8,128)(2,1)} %bitcast.63, ...), custom_call_target="tpu_custom_call" | custom-call | flops 10000000000 | bytes 1000000 | tf_op jit(solution)/shard_map/prompt_inner/pallas_call | solution.py:967
  100.9 12.8 %all-to-all-done.2 = f32[4,16,5248]{2,1,0:T(8,128)S(1)} async-done(((f32[4,16,5248]{2,1,0:T(8,128)}), f32[4,16,5248]{2,1,0:T(8,128)S(1)}, u32[]{:S(2)}, u32[]{:S(2)}) %all-to-all-start.2) | async-done | bytes 1343520 | tf_op jit(solution)/shard_map/all_to_all | solution.py:1062
  113.7 5.2 %collective-permute-start.7 = (f32[64,5248]{1,0:T(8,128)S(1)}, f32[64,5248]{1,0:T(8,128)S(1)}, u32[]{:S(2)}, u32[]{:S(2)}) collective-permute-start(f32[64,5248]{1,0:T(8,128)S(1)} %bitcast.35), channel_id=1, source_target_pairs={{0,64},{64,0},{128,192},{192,128},{256,320},{320,256},{384,448},{4... | collective-permute-start | bytes 4030472 | tf_op jit(solution)/shard_map/ppermute | solution.py:1052
  118.9 4.5 %spread_branch.1 = (f32[64,4096]{1,0:T(8,128)}, f32[64,4096]{1,0:T(8,128)}) custom-call(s32[24]{0:T(128)} %get-tuple-element.88.scal, f32[64,5248]{1,0:T(8,128)} %bitcast.36, f32[16,4096]{1,0:T(8,128)} %get-tuple-element.114.s0.p0, f32[16,4096]{1,0:T(8,128)} %copy-done.5, f32[16,4096]{1,0:T(8,128)} %copy-done.6, f32[16,4096]{1,0:T(8,128)} %copy-done.7, ...), custom_call_target="tpu_custom_call" | custom-call | flops 1000000000 | bytes 1000000 | tf_op jit(solution)/shard_map/spread_branch/pallas_call | solution.py:967
  125.3 4.5 %prompt.1 = (bf16[256,128]{1,0:T(8,128)(2,1)}, f32[256,128]{1,0:T(8,128)}, f32[16,40,128]{2,1,0:T(8,128)}, f32[3,3,128]{2,1,0:T(4,128)}, f32[16,768]{1,0:T(8,128)}) custom-call(s32[24]{0:T(128)} %get-tuple-element.88.scal, bf16[256,128]{1,0:T(8,128)(2,1)} %bitcast.47, f32[4,16,128]{2,1,0:T(8,128)} %bitcast.43, f32[4,256]{1,0:T(4,128)} %bitcast.52, ...), custom_call_target="tpu_custom_call" | custom-call | flops 1000000000 | bytes 1000000 | tf_op jit(solution)/shard_map/prompt/pallas_call | solution.py:967
  129.8 3.2 %collective-permute-start.9 = (f32[3,3,128]{2,1,0:T(4,128)}, f32[3,3,128]{2,1,0:T(4,128)S(1)}, u32[]{:S(2)}, u32[]{:S(2)}) collective-permute-start(f32[3,3,128]{2,1,0:T(4,128)} %get-tuple-element.152), channel_id=1, source_target_pairs={{64,0},{128,64},{192,128},{256,192},{320,256},{384,320},{448,384},... | collective-permute-start | bytes 13832 | tf_op jit(solution)/shard_map/ppermute | solution.py:1190
  136.9 11.1 %all-to-all-start.3 = ((f32[16,40,128]{2,1,0:T(8,128)}), f32[16,40,128]{2,1,0:T(8,128)S(1)}, u32[]{:S(2)}, u32[]{:S(2)}) async-start(f32[16,40,128]{2,1,0:T(8,128)} %rim.1), calls=%async_computation.3 | async-start | bytes 655360 | tf_op jit(solution)/shard_map/all_to_all | solution.py:1203
  149.0 6.2 %carry.1 = (bf16[128,16,128]{2,1,0:T(8,128)(2,1)}, bf16[128,16,128]{2,1,0:T(8,128)(2,1)}, f32[3,16,128]{2,1,0:T(8,128)}, f32[3,16,128]{2,1,0:T(8,128)}) custom-call(s32[24]{0:T(128)} %get-tuple-element.88.scal, bf16[128,256]{1,0:T(8,128)(2,1)} %bitcast.72, f32[3,21,128]{2,1,0:T(8,128)} %copy-done.14, f32[4,16,128]{2,1,0:T(8,128)} %bitcast.44, ...), custom_call_target="tpu_custom_call" | custom-call | flops 10000000000 | bytes 1000000 | tf_op jit(solution)/shard_map/carry/pallas_call | solution.py:967
  157.2 3.7 %collective-permute-done.10 = f32[3,16,128]{2,1,0:T(8,128)S(1)} collective-permute-done((f32[3,16,128]{2,1,0:T(8,128)}, f32[3,16,128]{2,1,0:T(8,128)S(1)}, u32[]{:S(2)}, u32[]{:S(2)}) %collective-permute-start.10) | collective-permute-done | bytes 24608 | tf_op jit(solution)/shard_map/ppermute | solution.py:1221
  162.2 5.3 %all-to-all-done.3.got = f32[16,40,128]{2,1,0:T(8,128)S(1)} async-done(((f32[16,40,128]{2,1,0:T(8,128)}), f32[16,40,128]{2,1,0:T(8,128)S(1)}, u32[]{:S(2)}, u32[]{:S(2)}) %all-to-all-start.3) | async-done | bytes 327712 | tf_op jit(solution)/shard_map/all_to_all | solution.py:1203
  (46 shorter events, 20.8 us)
Async XLA Ops:
  2.8 9.1 %collective-permute-start = (f32[3,21,128]{2,1,0:T(8,128)}, f32[3,21,128]{2,1,0:T(8,128)S(1)}, u32[]{:S(2)}, u32[]{:S(2)}) collective-permute-start(f32[3,21,128]{2,1,0:T(8,128)} %get-tuple-element.95), channel_id=1, source_target_pairs={{0,64},{64,128},{128,192},{192,256},{256,320},{320,384},{384,448},... | collective-permute-start | bytes 96776 | tf_op jit(solution)/shard_map/ppermute | solution.py:1045
  7.4 2.6 %copy-start.12 = (f32[4,1,256]{2,1,0:T(1,128)S(1)}, f32[4,1,256]{2,1,0:T(1,128)}, u32[]{:S(2)}) copy-start(f32[4,1,256]{2,1,0:T(1,128)} %param.25) | copy-start | bytes 12292
  11.9 0.6 copy-start.14
  17.9 7.7 %collective-permute-start.1 = (f32[64,5888]{1,0:T(8,128)}, f32[64,5888]{1,0:T(8,128)S(1)}, u32[]{:S(2)}, u32[]{:S(2)}) collective-permute-start(f32[64,5888]{1,0:T(8,128)} %get-tuple-element.100), channel_id=1, source_target_pairs={{0,64},{64,0},{128,192},{192,128},{256,320},{320,256},{384,448},{4... | collective-permute-start | bytes 4521992 | tf_op jit(solution)/shard_map/ppermute | solution.py:1052
  25.6 1.1 copy-start.2
  30.1 23.3 %all-to-all-start = ((f32[4,16,5888]{2,1,0:T(8,128)}), f32[4,16,5888]{2,1,0:T(8,128)S(1)}, u32[]{:S(2)}, u32[]{:S(2)}) async-start(f32[4,16,5888]{2,1,0:T(8,128)} %bitcast.38), calls=%async_computation | async-start | bytes 3014656 | tf_op jit(solution)/shard_map/all_to_all | solution.py:1062
  33.6 11.7 %copy-start.10 = (f32[64,384]{1,0:T(8,128)S(1)}, f32[64,384]{1,0:T(8,128)}, u32[]{:S(2)}) copy-start(f32[64,384]{1,0:T(8,128)} %get-tuple-element.102.mine.keep_mine) | copy-start | bytes 294916
  43.0 4.3 %collective-permute-start.3 = (f32[64,2048]{1,0:T(8,128)}, f32[64,2048]{1,0:T(8,128)S(1)}, u32[]{:S(2)}, u32[]{:S(2)}) collective-permute-start(f32[64,2048]{1,0:T(8,128)} %get-tuple-element.107), channel_id=1, source_target_pairs={{0,64},{64,0},{128,192},{192,128},{256,320},{320,256},{384,448},{4... | collective-permute-start | bytes 1572872 | tf_op jit(solution)/shard_map/ppermute | solution.py:1052
  45.3 5.1 %collective-permute-start.2 = (f32[64,384]{1,0:T(8,128)S(1)}, f32[64,384]{1,0:T(8,128)S(1)}, u32[]{:S(2)}, u32[]{:S(2)}) collective-permute-start(f32[64,384]{1,0:T(8,128)S(1)} %copy-done.10), channel_id=1, source_target_pairs={{0,64},{64,0},{128,192},{192,128},{256,320},{320,256},{384,448},{4... | collective-permute-start | bytes 294920 | tf_op jit(solution)/shard_map/ppermute | solution.py:1052
  47.4 0.8 copy-start.8
  50.4 42.7 %copy-start.11 = (f32[64,384]{1,0:T(8,128)}, f32[64,384]{1,0:T(8,128)S(1)}, u32[]{:S(2)}) copy-start(f32[64,384]{1,0:T(8,128)S(1)} %collective-permute-done.2.keep_far) | copy-start | bytes 294916
  53.4 1.1 copy-start.1
  57.7 30.5 %all-to-all-start.1 = ((f32[16,40,128]{2,1,0:T(8,128)}), f32[16,40,128]{2,1,0:T(8,128)S(1)}, u32[]{:S(2)}, u32[]{:S(2)}) async-start(f32[16,40,128]{2,1,0:T(8,128)} %get-tuple-element.108), calls=%async_computation.1 | async-start | bytes 655360 | tf_op jit(solution)/shard_map/all_to_all | solution.py:1133
  69.7 10.2 %collective-permute-start.4 = (f32[16,4096]{1,0:T(8,128)}, f32[16,4096]{1,0:T(8,128)S(1)}, u32[]{:S(2)}, u32[]{:S(2)}) collective-permute-start(f32[16,4096]{1,0:T(8,128)} %get-tuple-element.110), channel_id=1, source_target_pairs={{0,128},{64,192},{128,256},{192,320},{256,384},{320,448},{384,0},{... | collective-permute-start | bytes 786440 | tf_op jit(solution)/shard_map/ppermute | solution.py:1058
  71.9 12.4 %collective-permute-start.5 = (f32[16,4096]{1,0:T(8,128)}, f32[16,4096]{1,0:T(8,128)S(1)}, u32[]{:S(2)}, u32[]{:S(2)}) collective-permute-start(f32[16,4096]{1,0:T(8,128)} %get-tuple-element.111), channel_id=1, source_target_pairs={{0,256},{64,320},{128,384},{192,448},{256,0},{320,64},{384,128},{4... | collective-permute-start | bytes 786440 | tf_op jit(solution)/shard_map/ppermute | solution.py:1058
  75.6 12.6 %collective-permute-start.6 = (f32[16,4096]{1,0:T(8,128)}, f32[16,4096]{1,0:T(8,128)S(1)}, u32[]{:S(2)}, u32[]{:S(2)}) collective-permute-start(f32[16,4096]{1,0:T(8,128)} %get-tuple-element.112), channel_id=1, source_target_pairs={{0,384},{64,448},{128,0},{192,64},{256,128},{320,192},{384,256},{4... | collective-permute-start | bytes 786440 | tf_op jit(solution)/shard_map/ppermute | solution.py:1058
  79.9 8.3 %copy-start.5 = (f32[16,4096]{1,0:T(8,128)}, f32[16,4096]{1,0:T(8,128)S(1)}, u32[]{:S(2)}) copy-start(f32[16,4096]{1,0:T(8,128)S(1)} %collective-permute-done.4.s1.p1) | copy-start | bytes 786436
  84.3 3.9 %copy-start.6 = (f32[16,4096]{1,0:T(8,128)}, f32[16,4096]{1,0:T(8,128)S(1)}, u32[]{:S(2)}) copy-start(f32[16,4096]{1,0:T(8,128)S(1)} %collective-permute-done.5.s2.p2) | copy-start | bytes 786436
  88.2 0.7 copy-start.7
  88.2 0.8 copy-start.4
  93.2 20.5 %all-to-all-start.2 = ((f32[4,16,5248]{2,1,0:T(8,128)}), f32[4,16,5248]{2,1,0:T(8,128)S(1)}, u32[]{:S(2)}, u32[]{:S(2)}) async-start(f32[4,16,5248]{2,1,0:T(8,128)} %chains.1), calls=%async_computation.2 | async-start | bytes 2686976 | tf_op jit(solution)/shard_map/all_to_all | solution.py:1062
  113.7 5.2 %copy-start = (f32[4,16,5248]{2,1,0:T(8,128)}, f32[4,16,5248]{2,1,0:T(8,128)S(1)}, u32[]{:S(2)}) copy-start(f32[4,16,5248]{2,1,0:T(8,128)S(1)} %all-to-all-done.2) | copy-start | bytes 4030468
  113.7 9.7 %collective-permute-start.7 = (f32[64,5248]{1,0:T(8,128)S(1)}, f32[64,5248]{1,0:T(8,128)S(1)}, u32[]{:S(2)}, u32[]{:S(2)}) collective-permute-start(f32[64,5248]{1,0:T(8,128)S(1)} %bitcast.35), channel_id=1, source_target_pairs={{0,64},{64,0},{128,192},{192,128},{256,320},{320,256},{384,448},{4... | collective-permute-start | bytes 4030472 | tf_op jit(solution)/shard_map/ppermute | solution.py:1052
  123.3 1.9 %copy-start.3 = (f32[64,5248]{1,0:T(8,128)}, f32[64,5248]{1,0:T(8,128)S(1)}, u32[]{:S(2)}) copy-start(f32[64,5248]{1,0:T(8,128)S(1)} %collective-permute-done.7.theirs) | copy-start | bytes 4030468
  123.3 24.7 %collective-permute-start.8 = (f32[64,4096]{1,0:T(8,128)}, f32[64,4096]{1,0:T(8,128)S(1)}, u32[]{:S(2)}, u32[]{:S(2)}) collective-permute-start(f32[64,4096]{1,0:T(8,128)} %get-tuple-element.149), channel_id=1, source_target_pairs={{0,64},{64,0},{128,192},{192,128},{256,320},{320,256},{384,448},{4... | collective-permute-start | bytes 3145736 | tf_op jit(solution)/shard_map/ppermute | solution.py:1052
  129.8 5.1 %collective-permute-start.9 = (f32[3,3,128]{2,1,0:T(4,128)}, f32[3,3,128]{2,1,0:T(4,128)S(1)}, u32[]{:S(2)}, u32[]{:S(2)}) collective-permute-start(f32[3,3,128]{2,1,0:T(4,128)} %get-tuple-element.152), channel_id=1, source_target_pairs={{64,0},{128,64},{192,128},{256,192},{320,256},{384,320},{448,384},... | collective-permute-start | bytes 13832 | tf_op jit(solution)/shard_map/ppermute | solution.py:1190
  135.0 0.6 copy-start.15
  136.9 30.6 %all-to-all-start.3 = ((f32[16,40,128]{2,1,0:T(8,128)}), f32[16,40,128]{2,1,0:T(8,128)S(1)}, u32[]{:S(2)}, u32[]{:S(2)}) async-start(f32[16,40,128]{2,1,0:T(8,128)} %rim.1), calls=%async_computation.3 | async-start | bytes 655360 | tf_op jit(solution)/shard_map/all_to_all | solution.py:1203
  148.0 1.0 copy-start.13
  155.2 5.6 %collective-permute-start.10 = (f32[3,16,128]{2,1,0:T(8,128)}, f32[3,16,128]{2,1,0:T(8,128)S(1)}, u32[]{:S(2)}, u32[]{:S(2)}) collective-permute-start(f32[3,16,128]{2,1,0:T(8,128)} %get-tuple-element.157), channel_id=1, source_target_pairs={{64,0},{128,64},{192,128},{256,192},{320,256},{384,320},{448,384},... | collective-permute-start | bytes 73736 | tf_op jit(solution)/shard_map/ppermute | solution.py:1221
  167.5 0.7 copy-start.9

commit v3 on v2

--- a/solution.py
+++ b/solution.py
@@ -22,6 +22,7 @@
 EARLY = 11
 
 VMEM_LIMIT = 56 * 1024 * 1024
+VMEM_SMALL = 20 * 1024 * 1024
 
 
 def split2(a):
@@ -954,7 +955,7 @@
 
 def call(
     kernel, args, outs, scratch, scalars=1, flops=10**9, blocks=None, out_smem=0,
-    out_blocks=None, aliases=None,
+    out_blocks=None, aliases=None, limit=VMEM_LIMIT,
 ):
     vmem = pl.BlockSpec(memory_space=pltpu.VMEM)
     smem = pl.BlockSpec(memory_space=pltpu.SMEM)
@@ -972,7 +973,7 @@
         out_specs=taken,
         input_output_aliases=aliases or {},
         scratch_shapes=[pltpu.VMEM(s, F32) for s in scratch],
-        compiler_params=pltpu.CompilerParams(vmem_limit_bytes=VMEM_LIMIT),
+        compiler_params=pltpu.CompilerParams(vmem_limit_bytes=limit),
         cost_estimate=pl.CostEstimate(flops=flops, bytes_accessed=10**6, transcendentals=0),
     )(*args)
 
@@ -1091,6 +1092,7 @@
                 (n + 8, 2 * STATE), (span + 8, LANES), (span + 8, 2 * STATE),
                 (span, LANES), (STATE, (2 * js + 3) * LANES),
             ],
+            limit=VMEM_SMALL,
         )
     theirs = across(other)
     with jax.named_scope("chip"):
@@ -1099,6 +1101,7 @@
             [scal, mine, theirs],
             [((half, width), F32)] + [((half, 3 * LANES), F32)] * 2,
             [],
+            limit=VMEM_SMALL,
         )
     got = between_chips(joined.reshape(chips, ns, width))
     with jax.named_scope("inner"):
@@ -1226,6 +1229,7 @@
             [scal, pgx, pback, end],
             [((span, LANES), BF16), ((span // js, 2 * STATE), BF16)],
             [(LANES, LANES)],
+            limit=VMEM_SMALL,
         )
     return (
         py.reshape(prompt_x.shape),

time: 172 us -> 170 us (0.988)
  Pallas kernels: 54.1 us -> 50.3 us
    pallas_call x14, Pallas kernels: 54.1 us -> 50.3 us  [call(): pl.pallas_call(kernel, grid=(1,) if blocks else (), out_shape=[jax.ShapeD...]
    unnamed x33 -> x63, local copies, waits for them, and re-layouts: 7.39 us -> 8.92 us
  transfers between devices with their start and end apart: 15 -> 15, of which waited for: 10 -> 10; matrix products, arithmetic and copies ran while one was open for 1% -> 1% of each run, Pallas kernels for 20% -> 21%
where the time goes in v3:
time: 170 us; the launch traced here: 167 us
  starting transfers between devices  64.5 us (38%)
  Pallas kernels  50.3 us (30%)
  waiting for transfers between devices  40.7 us (24%)
  local copies, waits for them, and re-layouts  8.92 us (5%)
    pallas_call x14, Pallas kernels, call(): pl.pallas_call(kernel, grid=(1,) if blocks else (), out_shape=[jax.ShapeD...  50.3 us
    all_to_all x2, waiting for transfers between devices, between_chips(): lax.all_to_all(v, 'prefix', 0, 0, axis_index_groups=columns, tiled=True)  15.7 us
    ppermute x5, starting transfers between devices, across(): return lax.ppermute(v, 'prefix', cores)  15.6 us
    all_to_all x1, starting transfers between devices, shards(): moved = lax.all_to_all(msg, 'branch', 0, 0, tiled=True)  11.6 us
    all_to_all x1, starting transfers between devices, shards(): end = lax.all_to_all(out_msg, 'branch', 0, 0, tiled=True)  11.1 us
    ppermute x3, waiting for transfers between devices, round_chips(): moved_on.append(lax.ppermute(blocks[d], 'prefix', pairs))  10.1 us
    unnamed x63, local copies, waits for them, and re-layouts  8.92 us
    ppermute x3, starting transfers between devices, round_chips(): moved_on.append(lax.ppermute(blocks[d], 'prefix', pairs))  8.41 us
  transfers between devices with their start and end apart: 15, of which 10 were waited for; matrix products, arithmetic and copies ran while one was open for 1% of the time, Pallas kernels for 21%

profile of v3, /device:TPU:1, one launch (start us, length us, event | category | flops | bytes accessed | tf_op | source)
XLA Modules:
  0.0 166.9 jit_solution(2311624915577402550)
XLA Ops:
  0.6 2.2 %setup.1 = (s32[24]{0:T(128)}, f32[3,21,128]{2,1,0:T(8,128)}, f32[32,128]{1,0:T(8,128)}, f32[32,128]{1,0:T(8,128)}, f32[2,256]{1,0:T(2,128)}, /*index=5*/f32[2,256]{1,0:T(2,128)}, f32[16,128]{1,0:T(8,128)}) custom-call(s32[16]{0:T(128)} %forks.1, s32[16]{0:T(128)} %lengths.1, s32[16]{0:T(128)} %holder.1, bf16[128,16,128]{2,1,0:T(8,128)(2,1)} %bitcast.67, ...), custom_call_target="tpu_custom_call" | custom-call | flops 1000000000 | bytes 1000000 | tf_op jit(solution)/shard_map/setup/pallas_call | solution.py:968
  2.8 4.6 %collective-permute-start = (f32[3,21,128]{2,1,0:T(8,128)}, f32[3,21,128]{2,1,0:T(8,128)S(1)}, u32[]{:S(2)}, u32[]{:S(2)}) collective-permute-start(f32[3,21,128]{2,1,0:T(8,128)} %get-tuple-element.95), channel_id=1, source_target_pairs={{0,64},{64,128},{128,192},{192,256},{256,320},{320,384},{384,448},... | collective-permute-start | bytes 96776 | tf_op jit(solution)/shard_map/ppermute | solution.py:1046
  7.5 2.6 %early.1 = (f32[16,1408]{1,0:T(8,128)}, f32[2048,128]{1,0:T(8,128)}, f32[128,128]{1,0:T(8,128)}, f32[32,128]{1,0:T(8,128)}, f32[256,128]{1,0:T(8,128)}, /*index=5*/f32[2,256]{1,0:T(2,128)}) custom-call(s32[24]{0:T(128)} %get-tuple-element.88.scal, bf16[256,128]{1,0:T(8,128)(2,1)} %bitcast.55, bf16[256,256]{1,0:T(8,128)(2,1)} %bitcast.51, ...), custom_call_target="tpu_custom_call" | custom-call | flops 1000000000 | bytes 1000000 | tf_op jit(solution)/shard_map/early/pallas_call | solution.py:968
  15.8 3.2 %lead.1 = (f32[64,5888]{1,0:T(8,128)S(1)}, f32[64,5888]{1,0:T(8,128)S(1)}) custom-call(s32[24]{0:T(128)S(1)} %copy-done.8, bf16[256,128]{1,0:T(8,128)(2,1)S(1)} %bitcast.57, bf16[256,256]{1,0:T(8,128)(2,1)S(1)} %bitcast.53, bf16[256,128]{1,0:T(8,128)(2,1)S(1)} %bitcast.43, bf16[128,256]{1,0:T(8,128)(2,1)S(1)} %bitcast.62, ...), custom_call_target="tpu_custom_call" | custom-call | flops 1000000000 | bytes 1000000 | tf_op jit(solution)/shard_map/lead/pallas_call | solution.py:968
  19.0 4.2 %collective-permute-start.1 = (f32[64,5888]{1,0:T(8,128)S(1)}, f32[64,5888]{1,0:T(8,128)S(1)}, u32[]{:S(2)}, u32[]{:S(2)}) collective-permute-start(f32[64,5888]{1,0:T(8,128)S(1)} %get-tuple-element.100), channel_id=1, source_target_pairs={{0,64},{64,0},{128,192},{192,128},{256,320},{320,256},{384,448},{4... | collective-permute-start | bytes 4521992 | tf_op jit(solution)/shard_map/ppermute | solution.py:1053
  23.2 2.9 %collective-permute-done.1.theirs = f32[64,5888]{1,0:T(8,128)S(1)} collective-permute-done((f32[64,5888]{1,0:T(8,128)S(1)}, f32[64,5888]{1,0:T(8,128)S(1)}, u32[]{:S(2)}, u32[]{:S(2)}) %collective-permute-start.1) | collective-permute-done | bytes 1507360 | tf_op jit(solution)/shard_map/ppermute | solution.py:1053
  26.1 2.0 %chip.1 = (f32[64,5888]{1,0:T(8,128)}, f32[64,384]{1,0:T(8,128)S(1)}, f32[64,384]{1,0:T(8,128)S(1)}) custom-call(s32[24]{0:T(128)S(1)} %copy-done.8, f32[64,5888]{1,0:T(8,128)S(1)} %get-tuple-element.99.mine, f32[64,5888]{1,0:T(8,128)S(1)} %collective-permute-done.1.theirs), custom_call_target="tpu_custom_call" | custom-call | flops 1000000000 | bytes 1000000 | tf_op jit(solution)/shard_map/chip/pallas_call | solution.py:968
  28.7 3.6 %all-to-all-start = ((f32[4,16,5888]{2,1,0:T(8,128)}), f32[4,16,5888]{2,1,0:T(8,128)S(1)}, u32[]{:S(2)}, u32[]{:S(2)}) async-start(f32[4,16,5888]{2,1,0:T(8,128)} %bitcast.15), calls=%async_computation | async-start | bytes 3014656 | tf_op jit(solution)/shard_map/all_to_all | solution.py:1063
  32.3 9.3 %inner.1 = (f32[64,2048]{1,0:T(8,128)}, f32[64,2048]{1,0:T(8,128)}, f32[2048,128]{1,0:T(8,128)}, f32[2048,128]{1,0:T(8,128)}, f32[2048,128]{1,0:T(8,128)}) custom-call(s32[24]{0:T(128)} %get-tuple-element.88.scal, bf16[128,16,128]{2,1,0:T(8,128)(2,1)} %bitcast.69, bf16[128,256]{1,0:T(8,128)(2,1)} %bitcast.60, f32[3,21,128]{2,1,0:T(8,128)} %copy-done.14, ...), custom_call_target="tpu_custom_call" | custom-call | flops 10000000000 | bytes 1000000 | tf_op jit(solution)/shard_map/inner/pallas_call | solution.py:968
  41.6 2.3 %collective-permute-start.3 = (f32[64,2048]{1,0:T(8,128)}, f32[64,2048]{1,0:T(8,128)S(1)}, u32[]{:S(2)}, u32[]{:S(2)}) collective-permute-start(f32[64,2048]{1,0:T(8,128)} %get-tuple-element.107), channel_id=1, source_target_pairs={{0,64},{64,0},{128,192},{192,128},{256,320},{320,256},{384,448},{4... | collective-permute-start | bytes 1572872 | tf_op jit(solution)/shard_map/ppermute | solution.py:1053
  43.9 2.0 %collective-permute-start.2 = (f32[64,384]{1,0:T(8,128)S(1)}, f32[64,384]{1,0:T(8,128)S(1)}, u32[]{:S(2)}, u32[]{:S(2)}) collective-permute-start(f32[64,384]{1,0:T(8,128)S(1)} %get-tuple-element.102.mine.keep_mine), channel_id=1, source_target_pairs={{0,64},{64,0},{128,192},{192,128},{256,320},{320,256},{384,448},{4... | collective-permute-start | bytes 294920 | tf_op jit(solution)/shard_map/ppermute | solution.py:1053
  46.8 2.3 %join_states.1.joined = f32[64,2048]{1,0:T(8,128)} custom-call(s32[24]{0:T(128)} %get-tuple-element.88.scal, f32[64,384]{1,0:T(8,128)} %copy-done.4, f32[64,384]{1,0:T(8,128)} %copy-done.5, f32[64,2048]{1,0:T(8,128)} %get-tuple-element.106.smine, f32[64,2048]{1,0:T(8,128)} %copy-done.27), custom_call_target="tpu_custom_call" | custom-call | flops 1000000000 | bytes 1000000 | tf_op jit(solution)/shard_map/join_states/pallas_call | solution.py:968
  49.0 2.9 %all-to-all-done.got = f32[4,16,5888]{2,1,0:T(8,128)S(1)} async-done(((f32[4,16,5888]{2,1,0:T(8,128)}), f32[4,16,5888]{2,1,0:T(8,128)S(1)}, u32[]{:S(2)}, u32[]{:S(2)}) %all-to-all-start) | async-done | bytes 1507360 | tf_op jit(solution)/shard_map/all_to_all | solution.py:1063
  53.1 3.2 %slices.1 = (f32[16,40,128]{2,1,0:T(8,128)}, f32[3,16,2048]{2,1,0:T(8,128)}, f32[4,16,128]{2,1,0:T(8,128)}, f32[32,128]{1,0:T(8,128)}, f32[16,1408]{1,0:T(8,128)...) custom-call(s32[24]{0:T(128)} %get-tuple-element.88.scal, ...), custom_call_target="tpu_custom_call" | custom-call | flops 1000000000 | bytes 1000000 | tf_op jit(solution)/shard_map/slices/pallas_call | solution.py:968
  56.3 11.6 %all-to-all-start.1 = ((f32[16,40,128]{2,1,0:T(8,128)}), f32[16,40,128]{2,1,0:T(8,128)S(1)}, u32[]{:S(2)}, u32[]{:S(2)}) async-start(f32[16,40,128]{2,1,0:T(8,128)} %get-tuple-element.108), calls=%async_computation.1 | async-start | bytes 655360 | tf_op jit(solution)/shard_map/all_to_all | solution.py:1136
  67.9 2.2 %collective-permute-start.4 = (f32[16,4096]{1,0:T(8,128)}, f32[16,4096]{1,0:T(8,128)S(1)}, u32[]{:S(2)}, u32[]{:S(2)}) collective-permute-start(f32[16,4096]{1,0:T(8,128)} %get-tuple-element.110), channel_id=1, source_target_pairs={{0,128},{64,192},{128,256},{192,320},{256,384},{320,448},{384,0},{... | collective-permute-start | bytes 786440 | tf_op jit(solution)/shard_map/ppermute | solution.py:1059
  70.1 3.7 %collective-permute-start.5 = (f32[16,4096]{1,0:T(8,128)}, f32[16,4096]{1,0:T(8,128)S(1)}, u32[]{:S(2)}, u32[]{:S(2)}) collective-permute-start(f32[16,4096]{1,0:T(8,128)} %get-tuple-element.111), channel_id=1, source_target_pairs={{0,256},{64,320},{128,384},{192,448},{256,0},{320,64},{384,128},{4... | collective-permute-start | bytes 786440 | tf_op jit(solution)/shard_map/ppermute | solution.py:1059
  73.8 2.5 %collective-permute-start.6 = (f32[16,4096]{1,0:T(8,128)}, f32[16,4096]{1,0:T(8,128)S(1)}, u32[]{:S(2)}, u32[]{:S(2)}) collective-permute-start(f32[16,4096]{1,0:T(8,128)} %get-tuple-element.112), channel_id=1, source_target_pairs={{0,384},{64,448},{128,0},{192,64},{256,128},{320,192},{384,256},{4... | collective-permute-start | bytes 786440 | tf_op jit(solution)/shard_map/ppermute | solution.py:1059
  78.1 4.5 %collective-permute-done.5.s2.p2 = f32[16,4096]{1,0:T(8,128)S(1)} collective-permute-done((f32[16,4096]{1,0:T(8,128)}, f32[16,4096]{1,0:T(8,128)S(1)}, u32[]{:S(2)}, u32[]{:S(2)}) %collective-permute-start.5) | collective-permute-done | bytes 262176 | tf_op jit(solution)/shard_map/ppermute | solution.py:1059
  82.5 3.9 %collective-permute-done.6.s3.p3 = f32[16,4096]{1,0:T(8,128)S(1)} collective-permute-done((f32[16,4096]{1,0:T(8,128)}, f32[16,4096]{1,0:T(8,128)S(1)}, u32[]{:S(2)}, u32[]{:S(2)}) %collective-permute-start.6) | collective-permute-done | bytes 262176 | tf_op jit(solution)/shard_map/ppermute | solution.py:1059
  87.2 4.1 %chains.1 = f32[4,16,5248]{2,1,0:T(8,128)} custom-call(s32[24]{0:T(128)} %get-tuple-element.88.scal, f32[4,16,5888]{2,1,0:T(8,128)} %copy-done.21, f32[16,40,128]{2,1,0:T(8,128)} %copy-done.23, f32[16,4096]{1,0:T(8,128)} %get-tuple-element.114.s0.p0, f32[16,4096]{1,0:T(8,128)} %copy-done.24, f32[16,4096]{1,0:T(8,128)} %copy-done.25, f32[16,4096]{1,0:T(8,128)} %copy-done.26, ...), custom_call_target="tpu_custom_call" | custom-call | flops 1000000000 | bytes 1000000 | tf_op jit(solution)/shard_map/chains/pallas_call | solution.py:968
  91.4 4.6 %all-to-all-start.2 = ((f32[4,16,5248]{2,1,0:T(8,128)}), f32[4,16,5248]{2,1,0:T(8,128)S(1)}, u32[]{:S(2)}, u32[]{:S(2)}) async-start(f32[4,16,5248]{2,1,0:T(8,128)} %chains.1), calls=%async_computation.2 | async-start | bytes 2686976 | tf_op jit(solution)/shard_map/all_to_all | solution.py:1063
  96.0 3.2 %prompt_inner.1 = (f32[256,128]{1,0:T(8,128)}, f32[256,128]{1,0:T(8,128)}, f32[256,128]{1,0:T(8,128)}, f32[256,128]{1,0:T(8,128)}, f32[256,128]{1,0:T(8,128)}, /*index=5*/f32[256,128]{1,0:T(8,128)}, f32[256,256]{1,0:T(8,128)}) custom-call(s32[24]{0:T(128)} %get-tuple-element.88.scal, bf16[256,128]{1,0:T(8,128)(2,1)} %bitcast.56, bf16[256,256]{1,0:T(8,128)(2,1)} %bitcast.52, ...), custom_call_target="tpu_custom_call" | custom-call | flops 10000000000 | bytes 1000000 | tf_op jit(solution)/shard_map/prompt_inner/pallas_call | solution.py:968
  99.2 12.8 %all-to-all-done.2 = f32[4,16,5248]{2,1,0:T(8,128)S(1)} async-done(((f32[4,16,5248]{2,1,0:T(8,128)}), f32[4,16,5248]{2,1,0:T(8,128)S(1)}, u32[]{:S(2)}, u32[]{:S(2)}) %all-to-all-start.2) | async-done | bytes 1343520 | tf_op jit(solution)/shard_map/all_to_all | solution.py:1063
  111.9 5.1 %collective-permute-start.7 = (f32[64,5248]{1,0:T(8,128)S(1)}, f32[64,5248]{1,0:T(8,128)S(1)}, u32[]{:S(2)}, u32[]{:S(2)}) collective-permute-start(f32[64,5248]{1,0:T(8,128)S(1)} %bitcast.63), channel_id=1, source_target_pairs={{0,64},{64,0},{128,192},{192,128},{256,320},{320,256},{384,448},{4... | collective-permute-start | bytes 4030472 | tf_op jit(solution)/shard_map/ppermute | solution.py:1053
  117.1 4.5 %spread_branch.1 = (f32[64,4096]{1,0:T(8,128)}, f32[64,4096]{1,0:T(8,128)}) custom-call(s32[24]{0:T(128)} %get-tuple-element.88.scal, f32[64,5248]{1,0:T(8,128)} %bitcast.64, f32[16,4096]{1,0:T(8,128)} %get-tuple-element.114.s0.p0, f32[16,4096]{1,0:T(8,128)} %copy-done.24, f32[16,4096]{1,0:T(8,128)} %copy-done.25, f32[16,4096]{1,0:T(8,128)} %copy-done.26, ...), custom_call_target="tpu_custom_call" | custom-call | flops 1000000000 | bytes 1000000 | tf_op jit(solution)/shard_map/spread_branch/pallas_call | solution.py:968
  123.6 4.8 %prompt.1 = (bf16[256,128]{1,0:T(8,128)(2,1)}, f32[256,128]{1,0:T(8,128)}, f32[16,40,128]{2,1,0:T(8,128)}, f32[3,3,128]{2,1,0:T(4,128)}, f32[16,768]{1,0:T(8,128)}) custom-call(s32[24]{0:T(128)} %get-tuple-element.88.scal, bf16[256,128]{1,0:T(8,128)(2,1)} %bitcast.42, f32[4,16,128]{2,1,0:T(8,128)} %bitcast.38, f32[4,256]{1,0:T(4,128)} %bitcast.48, ...), custom_call_target="tpu_custom_call" | custom-call | flops 1000000000 | bytes 1000000 | tf_op jit(solution)/shard_map/prompt/pallas_call | solution.py:968
  128.4 3.2 %collective-permute-start.9 = (f32[3,3,128]{2,1,0:T(4,128)}, f32[3,3,128]{2,1,0:T(4,128)S(1)}, u32[]{:S(2)}, u32[]{:S(2)}) collective-permute-start(f32[3,3,128]{2,1,0:T(4,128)} %get-tuple-element.152), channel_id=1, source_target_pairs={{64,0},{128,64},{192,128},{256,192},{320,256},{384,320},{448,384},... | collective-permute-start | bytes 13832 | tf_op jit(solution)/shard_map/ppermute | solution.py:1193
  135.5 11.1 %all-to-all-start.3 = ((f32[16,40,128]{2,1,0:T(8,128)}), f32[16,40,128]{2,1,0:T(8,128)S(1)}, u32[]{:S(2)}, u32[]{:S(2)}) async-start(f32[16,40,128]{2,1,0:T(8,128)} %rim.1), calls=%async_computation.3 | async-start | bytes 655360 | tf_op jit(solution)/shard_map/all_to_all | solution.py:1206
  147.6 6.2 %carry.1 = (bf16[128,16,128]{2,1,0:T(8,128)(2,1)}, bf16[128,16,128]{2,1,0:T(8,128)(2,1)}, f32[3,16,128]{2,1,0:T(8,128)}, f32[3,16,128]{2,1,0:T(8,128)}) custom-call(s32[24]{0:T(128)} %get-tuple-element.88.scal, bf16[128,256]{1,0:T(8,128)(2,1)} %bitcast.61, f32[3,21,128]{2,1,0:T(8,128)} %copy-done.14, f32[4,16,128]{2,1,0:T(8,128)} %bitcast.39, ...), custom_call_target="tpu_custom_call" | custom-call | flops 10000000000 | bytes 1000000 | tf_op jit(solution)/shard_map/carry/pallas_call | solution.py:968
  155.8 3.7 %collective-permute-done.10 = f32[3,16,128]{2,1,0:T(8,128)S(1)} collective-permute-done((f32[3,16,128]{2,1,0:T(8,128)}, f32[3,16,128]{2,1,0:T(8,128)S(1)}, u32[]{:S(2)}, u32[]{:S(2)}) %collective-permute-start.10) | collective-permute-done | bytes 24608 | tf_op jit(solution)/shard_map/ppermute | solution.py:1224
  160.8 4.6 %all-to-all-done.3.got = f32[16,40,128]{2,1,0:T(8,128)S(1)} async-done(((f32[16,40,128]{2,1,0:T(8,128)}), f32[16,40,128]{2,1,0:T(8,128)S(1)}, u32[]{:S(2)}, u32[]{:S(2)}) %all-to-all-start.3) | async-done | bytes 327712 | tf_op jit(solution)/shard_map/all_to_all | solution.py:1206
  (76 shorter events, 22.2 us)
Async XLA Ops:
  2.8 9.1 %collective-permute-start = (f32[3,21,128]{2,1,0:T(8,128)}, f32[3,21,128]{2,1,0:T(8,128)S(1)}, u32[]{:S(2)}, u32[]{:S(2)}) collective-permute-start(f32[3,21,128]{2,1,0:T(8,128)} %get-tuple-element.95), channel_id=1, source_target_pairs={{0,64},{64,128},{128,192},{192,256},{256,320},{320,384},{384,448},... | collective-permute-start | bytes 96776 | tf_op jit(solution)/shard_map/ppermute | solution.py:1046
  7.4 4.5 %copy-start.3 = (f32[4,16,1,128]{3,2,1,0:T(1,128)S(1)}, f32[4,16,1,128]{3,2,1,0:T(1,128)}, u32[]{:S(2)}) copy-start(f32[4,16,1,128]{3,2,1,0:T(1,128)} %param.24) | copy-start | bytes 98308
  7.4 4.5 %copy-start.6 = (bf16[256,1,1,128]{3,0,2,1:T(8,128)(2,1)S(1)}, bf16[256,1,1,128]{3,0,2,1:T(8,128)(2,1)}, u32[]{:S(2)}) copy-start(bf16[256,1,1,128]{3,0,2,1:T(8,128)(2,1)} %param.32) | copy-start | bytes 196612
  7.4 4.4 %copy-start.8 = (s32[24]{0:T(128)S(1)}, s32[24]{0:T(128)}, u32[]{:S(2)}) copy-start(s32[24]{0:T(128)} %get-tuple-element.88.scal) | copy-start | bytes 292
  7.5 4.4 %copy-start.10 = (bf16[256,1,256]{2,0,1:T(8,128)(2,1)S(1)}, bf16[256,1,256]{2,0,1:T(8,128)(2,1)}, u32[]{:S(2)}) copy-start(bf16[256,1,256]{2,0,1:T(8,128)(2,1)} %param.19) | copy-start | bytes 393220
  7.5 4.4 %copy-start.12 = (bf16[256,1,1,128]{3,0,2,1:T(8,128)(2,1)S(1)}, bf16[256,1,1,128]{3,0,2,1:T(8,128)(2,1)}, u32[]{:S(2)}) copy-start(bf16[256,1,1,128]{3,0,2,1:T(8,128)(2,1)} %param.18) | copy-start | bytes 196612
  7.5 4.4 %copy-start.13 = (bf16[1,128,1,256]{3,1,2,0:T(8,128)(2,1)S(1)}, bf16[1,128,1,256]{3,1,2,0:T(8,128)(2,1)}, u32[]{:S(2)}) copy-start(bf16[1,128,1,256]{3,1,2,0:T(8,128)(2,1)} %param.22) | copy-start | bytes 196612
  10.1 8.8 %copy-start.7 = (f32[4,1,256]{2,0,1:T(4,128)}, f32[4,1,256]{2,0,1:T(4,128)S(1)}, u32[]{:S(2)}) copy-start(f32[4,1,256]{2,0,1:T(4,128)S(1)} %copy.26) | copy-start | bytes 12292
  11.9 7.1 %copy-start.14 = (f32[3,21,128]{2,1,0:T(8,128)}, f32[3,21,128]{2,1,0:T(8,128)S(1)}, u32[]{:S(2)}) copy-start(f32[3,21,128]{2,1,0:T(8,128)S(1)} %collective-permute-done.rim) | copy-start | bytes 96772
  19.0 9.1 %copy-start = (f32[64,5888]{1,0:T(8,128)}, f32[64,5888]{1,0:T(8,128)S(1)}, u32[]{:S(2)}) copy-start(f32[64,5888]{1,0:T(8,128)S(1)} %get-tuple-element.99.mine) | copy-start | bytes 4521988
  19.0 7.1 %collective-permute-start.1 = (f32[64,5888]{1,0:T(8,128)S(1)}, f32[64,5888]{1,0:T(8,128)S(1)}, u32[]{:S(2)}, u32[]{:S(2)}) collective-permute-start(f32[64,5888]{1,0:T(8,128)S(1)} %get-tuple-element.100), channel_id=1, source_target_pairs={{0,64},{64,0},{128,192},{192,128},{256,320},{320,256},{384,448},{4... | collective-permute-start | bytes 4521992 | tf_op jit(solution)/shard_map/ppermute | solution.py:1053
  28.7 15.2 %copy-start.4 = (f32[64,384]{1,0:T(8,128)}, f32[64,384]{1,0:T(8,128)S(1)}, u32[]{:S(2)}) copy-start(f32[64,384]{1,0:T(8,128)S(1)} %get-tuple-element.102.mine.keep_mine) | copy-start | bytes 294916
  28.7 23.3 %all-to-all-start = ((f32[4,16,5888]{2,1,0:T(8,128)}), f32[4,16,5888]{2,1,0:T(8,128)S(1)}, u32[]{:S(2)}, u32[]{:S(2)}) async-start(f32[4,16,5888]{2,1,0:T(8,128)} %bitcast.15), calls=%async_computation | async-start | bytes 3014656 | tf_op jit(solution)/shard_map/all_to_all | solution.py:1063
  41.6 4.3 %collective-permute-start.3 = (f32[64,2048]{1,0:T(8,128)}, f32[64,2048]{1,0:T(8,128)S(1)}, u32[]{:S(2)}, u32[]{:S(2)}) collective-permute-start(f32[64,2048]{1,0:T(8,128)} %get-tuple-element.107), channel_id=1, source_target_pairs={{0,64},{64,0},{128,192},{192,128},{256,320},{320,256},{384,448},{4... | collective-permute-start | bytes 1572872 | tf_op jit(solution)/shard_map/ppermute | solution.py:1053
  43.9 5.2 %collective-permute-start.2 = (f32[64,384]{1,0:T(8,128)S(1)}, f32[64,384]{1,0:T(8,128)S(1)}, u32[]{:S(2)}, u32[]{:S(2)}) collective-permute-start(f32[64,384]{1,0:T(8,128)S(1)} %get-tuple-element.102.mine.keep_mine), channel_id=1, source_target_pairs={{0,64},{64,0},{128,192},{192,128},{256,320},{320,256},{384,448},{4... | collective-permute-start | bytes 294920 | tf_op jit(solution)/shard_map/ppermute | solution.py:1053
  49.0 42.3 %copy-start.28 = (f32[64,384]{1,0:T(8,128)}, f32[64,384]{1,0:T(8,128)S(1)}, u32[]{:S(2)}) copy-start(f32[64,384]{1,0:T(8,128)S(1)} %collective-permute-done.2.keep_far) | copy-start | bytes 294916
  56.3 30.1 %all-to-all-start.1 = ((f32[16,40,128]{2,1,0:T(8,128)}), f32[16,40,128]{2,1,0:T(8,128)S(1)}, u32[]{:S(2)}, u32[]{:S(2)}) async-start(f32[16,40,128]{2,1,0:T(8,128)} %get-tuple-element.108), calls=%async_computation.1 | async-start | bytes 655360 | tf_op jit(solution)/shard_map/all_to_all | solution.py:1136
  67.9 10.2 %collective-permute-start.4 = (f32[16,4096]{1,0:T(8,128)}, f32[16,4096]{1,0:T(8,128)S(1)}, u32[]{:S(2)}, u32[]{:S(2)}) collective-permute-start(f32[16,4096]{1,0:T(8,128)} %get-tuple-element.110), channel_id=1, source_target_pairs={{0,128},{64,192},{128,256},{192,320},{256,384},{320,448},{384,0},{... | collective-permute-start | bytes 786440 | tf_op jit(solution)/shard_map/ppermute | solution.py:1059
  70.1 12.4 %collective-permute-start.5 = (f32[16,4096]{1,0:T(8,128)}, f32[16,4096]{1,0:T(8,128)S(1)}, u32[]{:S(2)}, u32[]{:S(2)}) collective-permute-start(f32[16,4096]{1,0:T(8,128)} %get-tuple-element.111), channel_id=1, source_target_pairs={{0,256},{64,320},{128,384},{192,448},{256,0},{320,64},{384,128},{4... | collective-permute-start | bytes 786440 | tf_op jit(solution)/shard_map/ppermute | solution.py:1059
  73.8 12.6 %collective-permute-start.6 = (f32[16,4096]{1,0:T(8,128)}, f32[16,4096]{1,0:T(8,128)S(1)}, u32[]{:S(2)}, u32[]{:S(2)}) collective-permute-start(f32[16,4096]{1,0:T(8,128)} %get-tuple-element.112), channel_id=1, source_target_pairs={{0,384},{64,448},{128,0},{192,64},{256,128},{320,192},{384,256},{4... | collective-permute-start | bytes 786440 | tf_op jit(solution)/shard_map/ppermute | solution.py:1059
  78.1 8.3 %copy-start.24 = (f32[16,4096]{1,0:T(8,128)}, f32[16,4096]{1,0:T(8,128)S(1)}, u32[]{:S(2)}) copy-start(f32[16,4096]{1,0:T(8,128)S(1)} %collective-permute-done.4.s1.p1) | copy-start | bytes 786436
  82.5 3.9 %copy-start.25 = (f32[16,4096]{1,0:T(8,128)}, f32[16,4096]{1,0:T(8,128)S(1)}, u32[]{:S(2)}) copy-start(f32[16,4096]{1,0:T(8,128)S(1)} %collective-permute-done.5.s2.p2) | copy-start | bytes 786436
  91.4 20.5 %all-to-all-start.2 = ((f32[4,16,5248]{2,1,0:T(8,128)}), f32[4,16,5248]{2,1,0:T(8,128)S(1)}, u32[]{:S(2)}, u32[]{:S(2)}) async-start(f32[4,16,5248]{2,1,0:T(8,128)} %chains.1), calls=%async_computation.2 | async-start | bytes 2686976 | tf_op jit(solution)/shard_map/all_to_all | solution.py:1063
  111.9 5.2 %copy-start.20 = (f32[4,16,5248]{2,1,0:T(8,128)}, f32[4,16,5248]{2,1,0:T(8,128)S(1)}, u32[]{:S(2)}) copy-start(f32[4,16,5248]{2,1,0:T(8,128)S(1)} %all-to-all-done.2) | copy-start | bytes 4030468
  111.9 9.7 %collective-permute-start.7 = (f32[64,5248]{1,0:T(8,128)S(1)}, f32[64,5248]{1,0:T(8,128)S(1)}, u32[]{:S(2)}, u32[]{:S(2)}) collective-permute-start(f32[64,5248]{1,0:T(8,128)S(1)} %bitcast.63), channel_id=1, source_target_pairs={{0,64},{64,0},{128,192},{192,128},{256,320},{320,256},{384,448},{4... | collective-permute-start | bytes 4030472 | tf_op jit(solution)/shard_map/ppermute | solution.py:1053
  121.6 25.0 %collective-permute-start.8 = (f32[64,4096]{1,0:T(8,128)}, f32[64,4096]{1,0:T(8,128)S(1)}, u32[]{:S(2)}, u32[]{:S(2)}) collective-permute-start(f32[64,4096]{1,0:T(8,128)} %get-tuple-element.149), channel_id=1, source_target_pairs={{0,64},{64,0},{128,192},{192,128},{256,320},{320,256},{384,448},{4... | collective-permute-start | bytes 3145736 | tf_op jit(solution)/shard_map/ppermute | solution.py:1053
  128.4 5.1 %collective-permute-start.9 = (f32[3,3,128]{2,1,0:T(4,128)}, f32[3,3,128]{2,1,0:T(4,128)S(1)}, u32[]{:S(2)}, u32[]{:S(2)}) collective-permute-start(f32[3,3,128]{2,1,0:T(4,128)} %get-tuple-element.152), channel_id=1, source_target_pairs={{64,0},{128,64},{192,128},{256,192},{320,256},{384,320},{448,384},... | collective-permute-start | bytes 13832 | tf_op jit(solution)/shard_map/ppermute | solution.py:1193
  135.5 30.0 %all-to-all-start.3 = ((f32[16,40,128]{2,1,0:T(8,128)}), f32[16,40,128]{2,1,0:T(8,128)S(1)}, u32[]{:S(2)}, u32[]{:S(2)}) async-start(f32[16,40,128]{2,1,0:T(8,128)} %rim.1), calls=%async_computation.3 | async-start | bytes 655360 | tf_op jit(solution)/shard_map/all_to_all | solution.py:1206
  147.6 17.9 %copy-start.9 = (s32[24]{0:T(128)S(1)}, s32[24]{0:T(128)}, u32[]{:S(2)}) copy-start(s32[24]{0:T(128)} %get-tuple-element.88.scal) | copy-start | bytes 292
  147.6 17.9 %copy-start.11 = (f32[256,128]{1,0:T(8,128)S(1)}, f32[256,128]{1,0:T(8,128)}, u32[]{:S(2)}) copy-start(f32[256,128]{1,0:T(8,128)} %get-tuple-element.151.pgx) | copy-start | bytes 393220
  147.6 17.9 %copy-start.16 = (f32[3,3,128]{2,1,0:T(4,128)S(1)}, f32[3,3,128]{2,1,0:T(4,128)}, u32[]{:S(2)}) copy-start(f32[3,3,128]{2,1,0:T(4,128)} %copy-done.15) | copy-start | bytes 13828
  153.8 5.6 %collective-permute-start.10 = (f32[3,16,128]{2,1,0:T(8,128)}, f32[3,16,128]{2,1,0:T(8,128)S(1)}, u32[]{:S(2)}, u32[]{:S(2)}) collective-permute-start(f32[3,16,128]{2,1,0:T(8,128)} %get-tuple-element.157), channel_id=1, source_target_pairs={{64,0},{128,64},{192,128},{256,192},{320,256},{384,320},{448,384},... | collective-permute-start | bytes 73736 | tf_op jit(solution)/shard_map/ppermute | solution.py:1224
  (14 other events, 16.2 us)

commit v4 on v3

--- a/solution.py
+++ b/solution.py
@@ -1079,6 +1079,7 @@
                 5: pl.BlockSpec((16, js, LANES), lambda i: (0, 0, 0)),
                 6: pl.BlockSpec((16, 2 * STATE), lambda i: (0, 0)),
             },
+            limit=VMEM_SMALL,
         )
     width = (2 * js + 3 + EARLY) * LANES
     with jax.named_scope("lead"):

time: 170 us -> 169 us (level); the launches traced: 167 us -> 168 us
    all_to_all x1, waiting for transfers between devices: 4.64 us -> 6.98 us  [shards(): end = lax.all_to_all(out_msg, 'branch', 0, 0, tiled=True)]
    ppermute x1, waiting for transfers between devices: 1.76 us -> 0.01 us  [shards(): rim = lax.ppermute(rim, 'prefix', [(i, i + 1) for i in range(count - 1)])]
    unnamed x63 -> x79, local copies, waits for them, and re-layouts: 8.92 us -> 9.06 us
  transfers between devices with their start and end apart: 15 -> 15, of which waited for: 10 -> 9; matrix products, arithmetic and copies ran while one was open for 1% -> 1% of each run, Pallas kernels for 21% -> 20%
where the time goes in v4:
time: 169 us; the launch traced here: 168 us
  starting transfers between devices  65.9 us (39%)
  Pallas kernels  49.2 us (29%)
  waiting for transfers between devices  41.8 us (25%)
  local copies, waits for them, and re-layouts  9.06 us (5%)
    pallas_call x14, Pallas kernels, call(): pl.pallas_call(kernel, grid=(1,) if blocks else (), out_shape=[jax.ShapeD...  49.2 us
    ppermute x5, starting transfers between devices, across(): return lax.ppermute(v, 'prefix', cores)  16.9 us
    all_to_all x2, waiting for transfers between devices, between_chips(): lax.all_to_all(v, 'prefix', 0, 0, axis_index_groups=columns, tiled=True)  15.8 us
    all_to_all x1, starting transfers between devices, shards(): moved = lax.all_to_all(msg, 'branch', 0, 0, tiled=True)  12 us
    all_to_all x1, starting transfers between devices, shards(): end = lax.all_to_all(out_msg, 'branch', 0, 0, tiled=True)  11.1 us
    ppermute x3, waiting for transfers between devices, round_chips(): moved_on.append(lax.ppermute(blocks[d], 'prefix', pairs))  10.1 us
    unnamed x79, local copies, waits for them, and re-layouts  9.06 us
    ppermute x3, starting transfers between devices, round_chips(): moved_on.append(lax.ppermute(blocks[d], 'prefix', pairs))  8.41 us
  transfers between devices with their start and end apart: 15, of which 9 were waited for; matrix products, arithmetic and copies ran while one was open for 1% of the time, Pallas kernels for 20%

profile of v4, /device:TPU:1, one launch (start us, length us, event | category | flops | bytes accessed | tf_op | source)
XLA Modules:
  0.0 168.4 jit_solution(5157723729264550258)
XLA Ops:
  0.7 2.2 %setup.1 = (s32[24]{0:T(128)}, f32[3,21,128]{2,1,0:T(8,128)}, f32[32,128]{1,0:T(8,128)}, f32[32,128]{1,0:T(8,128)}, f32[2,256]{1,0:T(2,128)}, /*index=5*/f32[2,256]{1,0:T(2,128)}, f32[16,128]{1,0:T(8,128)}) custom-call(s32[16]{0:T(128)} %forks.1, s32[16]{0:T(128)} %lengths.1, s32[16]{0:T(128)} %holder.1, bf16[128,16,128]{2,1,0:T(8,128)(2,1)} %bitcast.51, ...), custom_call_target="tpu_custom_call" | custom-call | flops 1000000000 | bytes 1000000 | tf_op jit(solution)/shard_map/setup/pallas_call | solution.py:968
  2.9 4.6 %collective-permute-start = (f32[3,21,128]{2,1,0:T(8,128)}, f32[3,21,128]{2,1,0:T(8,128)S(1)}, u32[]{:S(2)}, u32[]{:S(2)}) collective-permute-start(f32[3,21,128]{2,1,0:T(8,128)} %get-tuple-element.95), channel_id=1, source_target_pairs={{0,64},{64,128},{128,192},{192,256},{256,320},{320,384},{384,448},... | collective-permute-start | bytes 96776 | tf_op jit(solution)/shard_map/ppermute | solution.py:1046
  12.7 3.4 %lead.1 = (f32[64,5888]{1,0:T(8,128)S(1)}, f32[64,5888]{1,0:T(8,128)S(1)}) custom-call(s32[24]{0:T(128)S(1)} %copy-done.9, bf16[256,128]{1,0:T(8,128)(2,1)S(1)} %bitcast.61, bf16[256,256]{1,0:T(8,128)(2,1)S(1)} %bitcast.57, bf16[256,128]{1,0:T(8,128)(2,1)S(1)} %bitcast.43, bf16[128,256]{1,0:T(8,128)(2,1)S(1)} %bitcast.66, ...), custom_call_target="tpu_custom_call" | custom-call | flops 1000000000 | bytes 1000000 | tf_op jit(solution)/shard_map/lead/pallas_call | solution.py:968
  16.1 5.5 %collective-permute-start.1 = (f32[64,5888]{1,0:T(8,128)S(1)}, f32[64,5888]{1,0:T(8,128)S(1)}, u32[]{:S(2)}, u32[]{:S(2)}) collective-permute-start(f32[64,5888]{1,0:T(8,128)S(1)} %get-tuple-element.100), channel_id=1, source_target_pairs={{0,64},{64,0},{128,192},{192,128},{256,320},{320,256},{384,448},{4... | collective-permute-start | bytes 4521992 | tf_op jit(solution)/shard_map/ppermute | solution.py:1053
  21.6 2.9 %collective-permute-done.1.theirs = f32[64,5888]{1,0:T(8,128)S(1)} collective-permute-done((f32[64,5888]{1,0:T(8,128)S(1)}, f32[64,5888]{1,0:T(8,128)S(1)}, u32[]{:S(2)}, u32[]{:S(2)}) %collective-permute-start.1) | collective-permute-done | bytes 1507360 | tf_op jit(solution)/shard_map/ppermute | solution.py:1053
  24.6 2.0 %chip.1 = (f32[64,5888]{1,0:T(8,128)}, f32[64,384]{1,0:T(8,128)S(1)}, f32[64,384]{1,0:T(8,128)S(1)}) custom-call(s32[24]{0:T(128)S(1)} %copy-done.9, f32[64,5888]{1,0:T(8,128)S(1)} %get-tuple-element.99.mine, f32[64,5888]{1,0:T(8,128)S(1)} %collective-permute-done.1.theirs), custom_call_target="tpu_custom_call" | custom-call | flops 1000000000 | bytes 1000000 | tf_op jit(solution)/shard_map/chip/pallas_call | solution.py:968
  27.2 3.6 %all-to-all-start = ((f32[4,16,5888]{2,1,0:T(8,128)}), f32[4,16,5888]{2,1,0:T(8,128)S(1)}, u32[]{:S(2)}, u32[]{:S(2)}) async-start(f32[4,16,5888]{2,1,0:T(8,128)} %bitcast.15), calls=%async_computation | async-start | bytes 3014656 | tf_op jit(solution)/shard_map/all_to_all | solution.py:1063
  30.8 9.3 %inner.1 = (f32[64,2048]{1,0:T(8,128)}, f32[64,2048]{1,0:T(8,128)}, f32[2048,128]{1,0:T(8,128)}, f32[2048,128]{1,0:T(8,128)}, f32[2048,128]{1,0:T(8,128)}) custom-call(s32[24]{0:T(128)} %get-tuple-element.88.scal, bf16[128,16,128]{2,1,0:T(8,128)(2,1)} %bitcast.52, bf16[128,256]{1,0:T(8,128)(2,1)} %bitcast.63, f32[3,21,128]{2,1,0:T(8,128)} %copy-done.17, ...), custom_call_target="tpu_custom_call" | custom-call | flops 10000000000 | bytes 1000000 | tf_op jit(solution)/shard_map/inner/pallas_call | solution.py:968
  40.0 2.3 %collective-permute-start.3 = (f32[64,2048]{1,0:T(8,128)}, f32[64,2048]{1,0:T(8,128)S(1)}, u32[]{:S(2)}, u32[]{:S(2)}) collective-permute-start(f32[64,2048]{1,0:T(8,128)} %get-tuple-element.107), channel_id=1, source_target_pairs={{0,64},{64,0},{128,192},{192,128},{256,320},{320,256},{384,448},{4... | collective-permute-start | bytes 1572872 | tf_op jit(solution)/shard_map/ppermute | solution.py:1053
  42.3 2.0 %collective-permute-start.2 = (f32[64,384]{1,0:T(8,128)S(1)}, f32[64,384]{1,0:T(8,128)S(1)}, u32[]{:S(2)}, u32[]{:S(2)}) collective-permute-start(f32[64,384]{1,0:T(8,128)S(1)} %get-tuple-element.102.mine.keep_mine), channel_id=1, source_target_pairs={{0,64},{64,0},{128,192},{192,128},{256,320},{320,256},{384,448},{4... | collective-permute-start | bytes 294920 | tf_op jit(solution)/shard_map/ppermute | solution.py:1053
  45.2 2.3 %join_states.1.joined = f32[64,2048]{1,0:T(8,128)} custom-call(s32[24]{0:T(128)} %get-tuple-element.88.scal, f32[64,384]{1,0:T(8,128)} %copy-done.4, f32[64,384]{1,0:T(8,128)} %copy-done.5, f32[64,2048]{1,0:T(8,128)} %get-tuple-element.106.smine, f32[64,2048]{1,0:T(8,128)} %copy-done.35), custom_call_target="tpu_custom_call" | custom-call | flops 1000000000 | bytes 1000000 | tf_op jit(solution)/shard_map/join_states/pallas_call | solution.py:968
  47.5 3.0 %all-to-all-done.got = f32[4,16,5888]{2,1,0:T(8,128)S(1)} async-done(((f32[4,16,5888]{2,1,0:T(8,128)}), f32[4,16,5888]{2,1,0:T(8,128)S(1)}, u32[]{:S(2)}, u32[]{:S(2)}) %all-to-all-start) | async-done | bytes 1507360 | tf_op jit(solution)/shard_map/all_to_all | solution.py:1063
  51.6 3.2 %slices.1 = (f32[16,40,128]{2,1,0:T(8,128)}, f32[3,16,2048]{2,1,0:T(8,128)}, f32[4,16,128]{2,1,0:T(8,128)}, f32[32,128]{1,0:T(8,128)}, f32[16,1408]{1,0:T(8,128)...) custom-call(s32[24]{0:T(128)} %get-tuple-element.88.scal, ...), custom_call_target="tpu_custom_call" | custom-call | flops 1000000000 | bytes 1000000 | tf_op jit(solution)/shard_map/slices/pallas_call | solution.py:968
  54.8 12.0 %all-to-all-start.1 = ((f32[16,40,128]{2,1,0:T(8,128)}), f32[16,40,128]{2,1,0:T(8,128)S(1)}, u32[]{:S(2)}, u32[]{:S(2)}) async-start(f32[16,40,128]{2,1,0:T(8,128)} %get-tuple-element.108), calls=%async_computation.1 | async-start | bytes 655360 | tf_op jit(solution)/shard_map/all_to_all | solution.py:1137
  66.8 2.2 %collective-permute-start.4 = (f32[16,4096]{1,0:T(8,128)}, f32[16,4096]{1,0:T(8,128)S(1)}, u32[]{:S(2)}, u32[]{:S(2)}) collective-permute-start(f32[16,4096]{1,0:T(8,128)} %get-tuple-element.110), channel_id=1, source_target_pairs={{0,128},{64,192},{128,256},{192,320},{256,384},{320,448},{384,0},{... | collective-permute-start | bytes 786440 | tf_op jit(solution)/shard_map/ppermute | solution.py:1059
  69.0 3.7 %collective-permute-start.5 = (f32[16,4096]{1,0:T(8,128)}, f32[16,4096]{1,0:T(8,128)S(1)}, u32[]{:S(2)}, u32[]{:S(2)}) collective-permute-start(f32[16,4096]{1,0:T(8,128)} %get-tuple-element.111), channel_id=1, source_target_pairs={{0,256},{64,320},{128,384},{192,448},{256,0},{320,64},{384,128},{4... | collective-permute-start | bytes 786440 | tf_op jit(solution)/shard_map/ppermute | solution.py:1059
  72.8 2.5 %collective-permute-start.6 = (f32[16,4096]{1,0:T(8,128)}, f32[16,4096]{1,0:T(8,128)S(1)}, u32[]{:S(2)}, u32[]{:S(2)}) collective-permute-start(f32[16,4096]{1,0:T(8,128)} %get-tuple-element.112), channel_id=1, source_target_pairs={{0,384},{64,448},{128,0},{192,64},{256,128},{320,192},{384,256},{4... | collective-permute-start | bytes 786440 | tf_op jit(solution)/shard_map/ppermute | solution.py:1059
  77.0 4.5 %collective-permute-done.5.s2.p2 = f32[16,4096]{1,0:T(8,128)S(1)} collective-permute-done((f32[16,4096]{1,0:T(8,128)}, f32[16,4096]{1,0:T(8,128)S(1)}, u32[]{:S(2)}, u32[]{:S(2)}) %collective-permute-start.5) | collective-permute-done | bytes 262176 | tf_op jit(solution)/shard_map/ppermute | solution.py:1059
  81.5 3.9 %collective-permute-done.6.s3.p3 = f32[16,4096]{1,0:T(8,128)S(1)} collective-permute-done((f32[16,4096]{1,0:T(8,128)}, f32[16,4096]{1,0:T(8,128)S(1)}, u32[]{:S(2)}, u32[]{:S(2)}) %collective-permute-start.6) | collective-permute-done | bytes 262176 | tf_op jit(solution)/shard_map/ppermute | solution.py:1059
  86.2 4.1 %chains.1 = f32[4,16,5248]{2,1,0:T(8,128)} custom-call(s32[24]{0:T(128)} %get-tuple-element.88.scal, f32[4,16,5888]{2,1,0:T(8,128)} %copy-done.29, f32[16,40,128]{2,1,0:T(8,128)} %copy-done.31, f32[16,4096]{1,0:T(8,128)} %get-tuple-element.114.s0.p0, f32[16,4096]{1,0:T(8,128)} %copy-done.32, f32[16,4096]{1,0:T(8,128)} %copy-done.33, f32[16,4096]{1,0:T(8,128)} %copy-done.34, ...), custom_call_target="tpu_custom_call" | custom-call | flops 1000000000 | bytes 1000000 | tf_op jit(solution)/shard_map/chains/pallas_call | solution.py:968
  90.3 4.6 %all-to-all-start.2 = ((f32[4,16,5248]{2,1,0:T(8,128)}), f32[4,16,5248]{2,1,0:T(8,128)S(1)}, u32[]{:S(2)}, u32[]{:S(2)}) async-start(f32[4,16,5248]{2,1,0:T(8,128)} %chains.1), calls=%async_computation.2 | async-start | bytes 2686976 | tf_op jit(solution)/shard_map/all_to_all | solution.py:1063
  94.9 3.2 %prompt_inner.1 = (f32[256,128]{1,0:T(8,128)}, f32[256,128]{1,0:T(8,128)}, f32[256,128]{1,0:T(8,128)}, f32[256,128]{1,0:T(8,128)}, f32[256,128]{1,0:T(8,128)}, /*index=5*/f32[256,128]{1,0:T(8,128)}, f32[256,256]{1,0:T(8,128)}) custom-call(s32[24]{0:T(128)} %get-tuple-element.88.scal, bf16[256,128]{1,0:T(8,128)(2,1)} %bitcast.59, bf16[256,256]{1,0:T(8,128)(2,1)} %bitcast.55, ...), custom_call_target="tpu_custom_call" | custom-call | flops 10000000000 | bytes 1000000 | tf_op jit(solution)/shard_map/prompt_inner/pallas_call | solution.py:968
  98.1 12.8 %all-to-all-done.2 = f32[4,16,5248]{2,1,0:T(8,128)S(1)} async-done(((f32[4,16,5248]{2,1,0:T(8,128)}), f32[4,16,5248]{2,1,0:T(8,128)S(1)}, u32[]{:S(2)}, u32[]{:S(2)}) %all-to-all-start.2) | async-done | bytes 1343520 | tf_op jit(solution)/shard_map/all_to_all | solution.py:1063
  110.9 5.1 %collective-permute-start.7 = (f32[64,5248]{1,0:T(8,128)S(1)}, f32[64,5248]{1,0:T(8,128)S(1)}, u32[]{:S(2)}, u32[]{:S(2)}) collective-permute-start(f32[64,5248]{1,0:T(8,128)S(1)} %bitcast.67), channel_id=1, source_target_pairs={{0,64},{64,0},{128,192},{192,128},{256,320},{320,256},{384,448},{4... | collective-permute-start | bytes 4030472 | tf_op jit(solution)/shard_map/ppermute | solution.py:1053
  116.0 4.5 %spread_branch.1 = (f32[64,4096]{1,0:T(8,128)}, f32[64,4096]{1,0:T(8,128)}) custom-call(s32[24]{0:T(128)} %get-tuple-element.88.scal, f32[64,5248]{1,0:T(8,128)} %bitcast.68, f32[16,4096]{1,0:T(8,128)} %get-tuple-element.114.s0.p0, f32[16,4096]{1,0:T(8,128)} %copy-done.32, f32[16,4096]{1,0:T(8,128)} %copy-done.33, f32[16,4096]{1,0:T(8,128)} %copy-done.34, ...), custom_call_target="tpu_custom_call" | custom-call | flops 1000000000 | bytes 1000000 | tf_op jit(solution)/shard_map/spread_branch/pallas_call | solution.py:968
  122.5 5.1 %prompt.1 = (bf16[256,128]{1,0:T(8,128)(2,1)}, f32[256,128]{1,0:T(8,128)}, f32[16,40,128]{2,1,0:T(8,128)}, f32[3,3,128]{2,1,0:T(4,128)}, f32[16,768]{1,0:T(8,128)}) custom-call(s32[24]{0:T(128)} %get-tuple-element.88.scal, bf16[256,128]{1,0:T(8,128)(2,1)} %bitcast.42, f32[4,16,128]{2,1,0:T(8,128)} %bitcast.38, f32[4,256]{1,0:T(4,128)} %bitcast.48, ...), custom_call_target="tpu_custom_call" | custom-call | flops 1000000000 | bytes 1000000 | tf_op jit(solution)/shard_map/prompt/pallas_call | solution.py:968
  127.6 2.8 %collective-permute-start.9 = (f32[3,3,128]{2,1,0:T(4,128)}, f32[3,3,128]{2,1,0:T(4,128)S(1)}, u32[]{:S(2)}, u32[]{:S(2)}) collective-permute-start(f32[3,3,128]{2,1,0:T(4,128)} %get-tuple-element.152), channel_id=1, source_target_pairs={{64,0},{128,64},{192,128},{256,192},{320,256},{384,320},{448,384},... | collective-permute-start | bytes 13832 | tf_op jit(solution)/shard_map/ppermute | solution.py:1194
  130.4 2.3 %collective-permute-done.9.back = f32[3,3,128]{2,1,0:T(4,128)S(1)} collective-permute-done((f32[3,3,128]{2,1,0:T(4,128)}, f32[3,3,128]{2,1,0:T(4,128)S(1)}, u32[]{:S(2)}, u32[]{:S(2)}) %collective-permute-start.9) | collective-permute-done | bytes 4640 | tf_op jit(solution)/shard_map/ppermute | solution.py:1194
  134.6 11.1 %all-to-all-start.3 = ((f32[16,40,128]{2,1,0:T(8,128)}), f32[16,40,128]{2,1,0:T(8,128)S(1)}, u32[]{:S(2)}, u32[]{:S(2)}) async-start(f32[16,40,128]{2,1,0:T(8,128)} %rim.1), calls=%async_computation.3 | async-start | bytes 655360 | tf_op jit(solution)/shard_map/all_to_all | solution.py:1207
  146.8 6.2 %carry.1 = (bf16[128,16,128]{2,1,0:T(8,128)(2,1)}, bf16[128,16,128]{2,1,0:T(8,128)(2,1)}, f32[3,16,128]{2,1,0:T(8,128)}, f32[3,16,128]{2,1,0:T(8,128)}) custom-call(s32[24]{0:T(128)} %get-tuple-element.88.scal, bf16[128,256]{1,0:T(8,128)(2,1)} %bitcast.64, f32[3,21,128]{2,1,0:T(8,128)} %copy-done.17, f32[4,16,128]{2,1,0:T(8,128)} %bitcast.39, ...), custom_call_target="tpu_custom_call" | custom-call | flops 10000000000 | bytes 1000000 | tf_op jit(solution)/shard_map/carry/pallas_call | solution.py:968
  154.9 3.7 %collective-permute-done.10 = f32[3,16,128]{2,1,0:T(8,128)S(1)} collective-permute-done((f32[3,16,128]{2,1,0:T(8,128)}, f32[3,16,128]{2,1,0:T(8,128)S(1)}, u32[]{:S(2)}, u32[]{:S(2)}) %collective-permute-start.10) | collective-permute-done | bytes 24608 | tf_op jit(solution)/shard_map/ppermute | solution.py:1225
  160.0 7.0 %all-to-all-done.3.got = f32[16,40,128]{2,1,0:T(8,128)S(1)} async-done(((f32[16,40,128]{2,1,0:T(8,128)}), f32[16,40,128]{2,1,0:T(8,128)S(1)}, u32[]{:S(2)}, u32[]{:S(2)}) %all-to-all-start.3) | async-done | bytes 327712 | tf_op jit(solution)/shard_map/all_to_all | solution.py:1207
  (92 shorter events, 19.7 us)
Async XLA Ops:
  0.6 6.9 %copy-start.11 = (bf16[1,128,16,1,128]{4,2,3,1,0:T(8,128)(2,1)S(1)}, bf16[1,128,16,1,128]{4,2,3,1,0:T(8,128)(2,1)}, u32[]{:S(2)}) copy-start(bf16[1,128,16,1,128]{4,2,3,1,0:T(8,128)(2,1)} %param.33) | copy-start | bytes 1572868
  0.6 6.9 %copy-start.12 = (bf16[1,128,16,1,128]{4,2,3,1,0:T(8,128)(2,1)S(1)}, bf16[1,128,16,1,128]{4,2,3,1,0:T(8,128)(2,1)}, u32[]{:S(2)}) copy-start(bf16[1,128,16,1,128]{4,2,3,1,0:T(8,128)(2,1)} %param.21) | copy-start | bytes 1572868
  0.7 6.9 %copy-start.13 = (bf16[256,1,256]{2,0,1:T(8,128)(2,1)S(1)}, bf16[256,1,256]{2,0,1:T(8,128)(2,1)}, u32[]{:S(2)}) copy-start(bf16[256,1,256]{2,0,1:T(8,128)(2,1)} %param.19) | copy-start | bytes 393220
  0.7 6.9 %copy-start.15 = (bf16[256,1,1,128]{3,0,2,1:T(8,128)(2,1)S(1)}, bf16[256,1,1,128]{3,0,2,1:T(8,128)(2,1)}, u32[]{:S(2)}) copy-start(bf16[256,1,1,128]{3,0,2,1:T(8,128)(2,1)} %param.18) | copy-start | bytes 196612
  0.7 6.9 %copy-start.16 = (bf16[1,128,1,256]{3,1,2,0:T(8,128)(2,1)S(1)}, bf16[1,128,1,256]{3,1,2,0:T(8,128)(2,1)}, u32[]{:S(2)}) copy-start(bf16[1,128,1,256]{3,1,2,0:T(8,128)(2,1)} %param.22) | copy-start | bytes 196612
  2.9 9.7 %collective-permute-start = (f32[3,21,128]{2,1,0:T(8,128)}, f32[3,21,128]{2,1,0:T(8,128)S(1)}, u32[]{:S(2)}, u32[]{:S(2)}) collective-permute-start(f32[3,21,128]{2,1,0:T(8,128)} %get-tuple-element.95), channel_id=1, source_target_pairs={{0,64},{64,128},{128,192},{192,256},{256,320},{320,384},{384,448},... | collective-permute-start | bytes 96776 | tf_op jit(solution)/shard_map/ppermute | solution.py:1046
  12.6 3.5 %copy-start.21 = (f32[128,128]{1,0:T(8,128)}, f32[128,128]{1,0:T(8,128)S(1)}, u32[]{:S(2)}) copy-start(f32[128,128]{1,0:T(8,128)S(1)} %get-tuple-element.98.table) | copy-start | bytes 196612
  12.6 3.5 %copy-start.22 = (f32[32,128]{1,0:T(8,128)}, f32[32,128]{1,0:T(8,128)S(1)}, u32[]{:S(2)}) copy-start(f32[32,128]{1,0:T(8,128)S(1)} %get-tuple-element.105.wrow) | copy-start | bytes 49156
  12.6 3.5 %copy-start.7 = (f32[4,1,256]{2,0,1:T(4,128)}, f32[4,1,256]{2,0,1:T(4,128)S(1)}, u32[]{:S(2)}) copy-start(f32[4,1,256]{2,0,1:T(4,128)S(1)} %copy.26) | copy-start | bytes 12292
  16.1 10.4 %copy-start = (f32[64,5888]{1,0:T(8,128)}, f32[64,5888]{1,0:T(8,128)S(1)}, u32[]{:S(2)}) copy-start(f32[64,5888]{1,0:T(8,128)S(1)} %get-tuple-element.99.mine) | copy-start | bytes 4521988
  16.1 8.4 %collective-permute-start.1 = (f32[64,5888]{1,0:T(8,128)S(1)}, f32[64,5888]{1,0:T(8,128)S(1)}, u32[]{:S(2)}, u32[]{:S(2)}) collective-permute-start(f32[64,5888]{1,0:T(8,128)S(1)} %get-tuple-element.100), channel_id=1, source_target_pairs={{0,64},{64,0},{128,192},{192,128},{256,320},{320,256},{384,448},{4... | collective-permute-start | bytes 4521992 | tf_op jit(solution)/shard_map/ppermute | solution.py:1053
  27.2 15.1 %copy-start.4 = (f32[64,384]{1,0:T(8,128)}, f32[64,384]{1,0:T(8,128)S(1)}, u32[]{:S(2)}) copy-start(f32[64,384]{1,0:T(8,128)S(1)} %get-tuple-element.102.mine.keep_mine) | copy-start | bytes 294916
  27.2 23.3 %all-to-all-start = ((f32[4,16,5888]{2,1,0:T(8,128)}), f32[4,16,5888]{2,1,0:T(8,128)S(1)}, u32[]{:S(2)}, u32[]{:S(2)}) async-start(f32[4,16,5888]{2,1,0:T(8,128)} %bitcast.15), calls=%async_computation | async-start | bytes 3014656 | tf_op jit(solution)/shard_map/all_to_all | solution.py:1063
  40.0 4.3 %collective-permute-start.3 = (f32[64,2048]{1,0:T(8,128)}, f32[64,2048]{1,0:T(8,128)S(1)}, u32[]{:S(2)}, u32[]{:S(2)}) collective-permute-start(f32[64,2048]{1,0:T(8,128)} %get-tuple-element.107), channel_id=1, source_target_pairs={{0,64},{64,0},{128,192},{192,128},{256,320},{320,256},{384,448},{4... | collective-permute-start | bytes 1572872 | tf_op jit(solution)/shard_map/ppermute | solution.py:1053
  42.3 5.1 %collective-permute-start.2 = (f32[64,384]{1,0:T(8,128)S(1)}, f32[64,384]{1,0:T(8,128)S(1)}, u32[]{:S(2)}, u32[]{:S(2)}) collective-permute-start(f32[64,384]{1,0:T(8,128)S(1)} %get-tuple-element.102.mine.keep_mine), channel_id=1, source_target_pairs={{0,64},{64,0},{128,192},{192,128},{256,320},{320,256},{384,448},{4... | collective-permute-start | bytes 294920 | tf_op jit(solution)/shard_map/ppermute | solution.py:1053
  47.5 42.9 %copy-start.36 = (f32[64,384]{1,0:T(8,128)}, f32[64,384]{1,0:T(8,128)S(1)}, u32[]{:S(2)}) copy-start(f32[64,384]{1,0:T(8,128)S(1)} %collective-permute-done.2.keep_far) | copy-start | bytes 294916
  54.8 30.5 %all-to-all-start.1 = ((f32[16,40,128]{2,1,0:T(8,128)}), f32[16,40,128]{2,1,0:T(8,128)S(1)}, u32[]{:S(2)}, u32[]{:S(2)}) async-start(f32[16,40,128]{2,1,0:T(8,128)} %get-tuple-element.108), calls=%async_computation.1 | async-start | bytes 655360 | tf_op jit(solution)/shard_map/all_to_all | solution.py:1137
  66.8 10.2 %collective-permute-start.4 = (f32[16,4096]{1,0:T(8,128)}, f32[16,4096]{1,0:T(8,128)S(1)}, u32[]{:S(2)}, u32[]{:S(2)}) collective-permute-start(f32[16,4096]{1,0:T(8,128)} %get-tuple-element.110), channel_id=1, source_target_pairs={{0,128},{64,192},{128,256},{192,320},{256,384},{320,448},{384,0},{... | collective-permute-start | bytes 786440 | tf_op jit(solution)/shard_map/ppermute | solution.py:1059
  69.0 12.4 %collective-permute-start.5 = (f32[16,4096]{1,0:T(8,128)}, f32[16,4096]{1,0:T(8,128)S(1)}, u32[]{:S(2)}, u32[]{:S(2)}) collective-permute-start(f32[16,4096]{1,0:T(8,128)} %get-tuple-element.111), channel_id=1, source_target_pairs={{0,256},{64,320},{128,384},{192,448},{256,0},{320,64},{384,128},{4... | collective-permute-start | bytes 786440 | tf_op jit(solution)/shard_map/ppermute | solution.py:1059
  72.8 12.6 %collective-permute-start.6 = (f32[16,4096]{1,0:T(8,128)}, f32[16,4096]{1,0:T(8,128)S(1)}, u32[]{:S(2)}, u32[]{:S(2)}) collective-permute-start(f32[16,4096]{1,0:T(8,128)} %get-tuple-element.112), channel_id=1, source_target_pairs={{0,384},{64,448},{128,0},{192,64},{256,128},{320,192},{384,256},{4... | collective-permute-start | bytes 786440 | tf_op jit(solution)/shard_map/ppermute | solution.py:1059
  77.0 8.3 %copy-start.32 = (f32[16,4096]{1,0:T(8,128)}, f32[16,4096]{1,0:T(8,128)S(1)}, u32[]{:S(2)}) copy-start(f32[16,4096]{1,0:T(8,128)S(1)} %collective-permute-done.4.s1.p1) | copy-start | bytes 786436
  81.5 3.9 %copy-start.33 = (f32[16,4096]{1,0:T(8,128)}, f32[16,4096]{1,0:T(8,128)S(1)}, u32[]{:S(2)}) copy-start(f32[16,4096]{1,0:T(8,128)S(1)} %collective-permute-done.5.s2.p2) | copy-start | bytes 786436
  90.3 20.5 %all-to-all-start.2 = ((f32[4,16,5248]{2,1,0:T(8,128)}), f32[4,16,5248]{2,1,0:T(8,128)S(1)}, u32[]{:S(2)}, u32[]{:S(2)}) async-start(f32[4,16,5248]{2,1,0:T(8,128)} %chains.1), calls=%async_computation.2 | async-start | bytes 2686976 | tf_op jit(solution)/shard_map/all_to_all | solution.py:1063
  110.9 5.1 %copy-start.28 = (f32[4,16,5248]{2,1,0:T(8,128)}, f32[4,16,5248]{2,1,0:T(8,128)S(1)}, u32[]{:S(2)}) copy-start(f32[4,16,5248]{2,1,0:T(8,128)S(1)} %all-to-all-done.2) | copy-start | bytes 4030468
  110.9 9.7 %collective-permute-start.7 = (f32[64,5248]{1,0:T(8,128)S(1)}, f32[64,5248]{1,0:T(8,128)S(1)}, u32[]{:S(2)}, u32[]{:S(2)}) collective-permute-start(f32[64,5248]{1,0:T(8,128)S(1)} %bitcast.67), channel_id=1, source_target_pairs={{0,64},{64,0},{128,192},{192,128},{256,320},{320,256},{384,448},{4... | collective-permute-start | bytes 4030472 | tf_op jit(solution)/shard_map/ppermute | solution.py:1053
  120.5 25.2 %collective-permute-start.8 = (f32[64,4096]{1,0:T(8,128)}, f32[64,4096]{1,0:T(8,128)S(1)}, u32[]{:S(2)}, u32[]{:S(2)}) collective-permute-start(f32[64,4096]{1,0:T(8,128)} %get-tuple-element.149), channel_id=1, source_target_pairs={{0,64},{64,0},{128,192},{192,128},{256,320},{320,256},{384,448},{4... | collective-permute-start | bytes 3145736 | tf_op jit(solution)/shard_map/ppermute | solution.py:1053
  127.6 5.1 %collective-permute-start.9 = (f32[3,3,128]{2,1,0:T(4,128)}, f32[3,3,128]{2,1,0:T(4,128)S(1)}, u32[]{:S(2)}, u32[]{:S(2)}) collective-permute-start(f32[3,3,128]{2,1,0:T(4,128)} %get-tuple-element.152), channel_id=1, source_target_pairs={{64,0},{128,64},{192,128},{256,192},{320,256},{384,320},{448,384},... | collective-permute-start | bytes 13832 | tf_op jit(solution)/shard_map/ppermute | solution.py:1194
  134.6 32.3 %all-to-all-start.3 = ((f32[16,40,128]{2,1,0:T(8,128)}), f32[16,40,128]{2,1,0:T(8,128)S(1)}, u32[]{:S(2)}, u32[]{:S(2)}) async-start(f32[16,40,128]{2,1,0:T(8,128)} %rim.1), calls=%async_computation.3 | async-start | bytes 655360 | tf_op jit(solution)/shard_map/all_to_all | solution.py:1207
  146.8 20.2 %copy-start.10 = (s32[24]{0:T(128)S(1)}, s32[24]{0:T(128)}, u32[]{:S(2)}) copy-start(s32[24]{0:T(128)} %get-tuple-element.88.scal) | copy-start | bytes 292
  146.8 20.2 %copy-start.14 = (f32[256,128]{1,0:T(8,128)S(1)}, f32[256,128]{1,0:T(8,128)}, u32[]{:S(2)}) copy-start(f32[256,128]{1,0:T(8,128)} %get-tuple-element.151.pgx) | copy-start | bytes 393220
  146.8 20.2 %copy-start.19 = (f32[3,3,128]{2,1,0:T(4,128)S(1)}, f32[3,3,128]{2,1,0:T(4,128)}, u32[]{:S(2)}) copy-start(f32[3,3,128]{2,1,0:T(4,128)} %copy-done.18) | copy-start | bytes 13828
  153.0 5.6 %collective-permute-start.10 = (f32[3,16,128]{2,1,0:T(8,128)}, f32[3,16,128]{2,1,0:T(8,128)S(1)}, u32[]{:S(2)}, u32[]{:S(2)}) collective-permute-start(f32[3,16,128]{2,1,0:T(8,128)} %get-tuple-element.157), channel_id=1, source_target_pairs={{64,0},{128,64},{192,128},{256,192},{320,256},{384,320},{448,384},... | collective-permute-start | bytes 73736 | tf_op jit(solution)/shard_map/ppermute | solution.py:1225
  (22 other events, 30.6 us)
